TPU v7x, 128 devices: a whole 4x4x4 slice. The times are simulated.
128 devices in a mesh: lon: 8 (over x, y_lo), lat: 16 (over z, y_hi, core).
Axes of the slice: x: 4, y: 4 (y_hi: 2, y_lo: 2; y = y_hi * 2 + y_lo), z: 4, core: 2. Of those that a mesh axis runs over, the one named last changes fastest.
Arguments:
- adj_final: float32 [36, 30, 64, 1024], P(None, None, 'lat', 'lon'), may hold values from -6 to 6
- saved: bfloat16 [3, 36, 30, 64, 1024], P(None, None, None, 'lat', 'lon'), may hold values from 0.099609375 to 10
- beta: float32 [36, 30], replicated, may hold values from 0 to 0.6
- sea_mask: int32 [64, 1024], P('lat', 'lon'), may hold values 0 or 1
- ice_mask: int32 [64, 1024], P('lat', 'lon'), may hold values 0 or 1
- obs_count: int32 [128, 128], P(('lon', 'lat')), may hold values from 0 to 4, as said below
- obs_cell: int32 [128, 512], P(('lon', 'lat')), may hold values from 0 to 65535, as said below
- obs_value: float32 [128, 512], P(('lon', 'lat')), may hold values from -3000 to 3000
Outputs:
- adj_start: float32 [36, 30, 64, 1024], P(None, None, 'lat', 'lon')
Inputs may be any that keep to these rules, and one draw needn't show every extreme that they name: `obs_count`: each entry is at most 4; in every row some entry equals 4, and one column equals 4 in every row. `obs_cell`: row s lists its observations grouped by tile in device order: the first obs_count[s,0] entries lie in the tile of device 0, the next obs_count[s,1] in that of device 1, and so on, where the device of lon index a and lat index b is number a times the lat axis size plus b and holds rows b * 4 to (b + 1) * 4 - 1 and longitudes a 128 to (a + 1) * 128 - 1. Entries after these are ignored.
All inputs are finite; a program needn't handle non-finite values. No bound on the sum of `sea_mask` or of `ice_mask` on one device may be relied on, other than what follows from the above.
Results may differ from a plain program's by a relative error of at most 0.0003.
Values sent between devices are 32-bit elements; how exact they have to be, the bound alone decides.
No kernel may reach another device: no remote copies, remote signals or barrier semaphores. Data moves between devices by JAX's collectives and lax.ppermute only.
A program may use at most 192 MiB of HBM per device.

v0:
```python
import math

import jax
import jax.numpy as jnp
import numpy as np
from jax import lax
from jax.experimental import pallas as pl
from jax.experimental.pallas import tpu as pltpu
from jax.sharding import PartitionSpec as P

STEPS = 2
CAP = 4
NDIR = 36
NFREQ = 30
PAIRS = NFREQ // 2
LAT = 4
LON = 128
ROWS = NDIR * NFREQ * LAT
HALF = NDIR * NFREQ // 2
HALO = 552
SOUTH0 = 536
N_LAT = 16
N_LON = 8
MIB = 2**20
F32 = jnp.float32

VMEM = pl.BlockSpec(memory_space=pltpu.VMEM)
SMEM = pl.BlockSpec(memory_space=pltpu.SMEM)

SEGMENTS = (
    (0, 4, True, True, True),
    (4, 5, True, True, False),
    (5, 9, True, False, False),
    (9, 13, False, False, False),
    (13, 14, False, False, True),
    (14, 18, False, True, True),
)


def constant_tables():
    angle = (np.arange(NDIR) + 0.5) * (2.0 * math.pi / NDIR)
    per_direction = np.stack([0.7 * np.abs(np.cos(angle)), 0.6 * np.abs(np.sin(angle))])
    j = np.arange(NFREQ)
    speed = 1.1 ** (-j.astype(np.float64))
    growth = 1.1 ** j.astype(np.float64)
    weight = growth / (NDIR * growth.sum())
    rows = np.arange(N_LAT * LAT)
    latitude = (rows + 0.5 - N_LAT * LAT / 2.0) * (100.0 / (N_LAT * LAT))
    stretch = math.cos(50.0 * math.pi / 180.0) / np.cos(latitude * (math.pi / 180.0))
    stretch = np.tile(stretch.reshape(N_LAT, 1, LAT), (1, 2, 1)).reshape(-1)
    column = np.concatenate([np.repeat(speed, LAT), np.repeat(weight, LAT), stretch])
    table = np.tile(column[:, None], (1, LON))
    return per_direction.astype(np.float32), table.astype(np.float32)


SPEED0, WEIGHT0, STRETCH0 = 0, NFREQ * LAT, 2 * NFREQ * LAT


def iotas():
    sub = lax.broadcasted_iota(jnp.int32, (8, LON), 0)
    lane = lax.broadcasted_iota(jnp.int32, (8, LON), 1)
    return sub, lane


def lon_slot(k, east):
    place = jnp.where(k < 9, k, k - 18) if east else k - 9
    return 8 * (place // 8), (place % 8) * PAIRS


def pack_edge(ref, k, east, edge_columns, lane):
    row, base = lon_slot(k, east)
    row = pl.multiple_of(row, 8)
    block = ref[pl.ds(row, 8), :]
    for jp, column in enumerate(edge_columns):
        block = jnp.where(lane == base + jp, column, block)
    ref[pl.ds(row, 8), :] = block


def extract_rows(src, r, first, dst, scale):
    def body(m, carry):
        for u in range(4):
            start = (first + 8 * (4 * m + u)) * LAT + r
            dst[pl.ds(pl.multiple_of(8 * (4 * m + u), 8), 8), :] = (
                src[pl.ds(start, 8, stride=LAT), :] * scale
            )
        return carry

    lax.fori_loop(0, 17, body, 0)


def send_rows(par, src, on_ref, off_ref, field, scale8):
    def put(dst, r, first):
        extract_rows(src, r, first, dst, scale8[r : r + 1, :])
        dst[pl.ds(544, 8), :] = jnp.broadcast_to(field[r : r + 1, :], (8, LON))

    @pl.when(par == 0)
    def _():
        put(on_ref, LAT - 1, SOUTH0)
        put(off_ref, 0, 0)

    @pl.when(par == 1)
    def _():
        put(on_ref, 0, 0)
        put(off_ref, LAT - 1, SOUTH0)


def take_rows(par, on_ref, off_ref, north_ref, south_ref):
    @pl.when(par == 0)
    def _():
        north_ref[...] = on_ref[...]
        south_ref[...] = off_ref[...]

    @pl.when(par == 1)
    def _():
        north_ref[...] = off_ref[...]
        south_ref[...] = on_ref[...]


def pick_observations(count_ref, cell_ref, value_ref, out_ref):
    sub = lax.broadcasted_iota(jnp.int32, (128, 128), 0)
    lane = lax.broadcasted_iota(jnp.int32, (128, 128), 1)
    counts = jnp.broadcast_to(count_ref[...].astype(F32), (128, 128))
    starts = jnp.sum(jnp.where(lane < sub, counts, 0.0), axis=1, keepdims=True)
    mine = jnp.sum(jnp.where(lane == sub, counts, 0.0), axis=1, keepdims=True)
    cell = cell_ref[...]
    local = (((cell >> 10) & (LAT - 1)) * LON + (cell & (LON - 1))).astype(F32)
    value = value_ref[...]
    slots = cell.shape[1]
    slot = lax.broadcasted_iota(jnp.int32, (128, slots), 1).astype(F32)
    listed = jnp.zeros((128, 128), F32)
    for i in range(CAP):
        hit = slot == starts + float(i)
        index_i = jnp.sum(jnp.where(hit, local, 0.0), axis=1, keepdims=True)
        value_i = jnp.sum(jnp.where(hit, value, 0.0), axis=1, keepdims=True)
        value_i = jnp.where(mine > float(i), value_i, 0.0)
        listed = jnp.where(lane == i, index_i, listed)
        listed = jnp.where(lane == CAP + i, value_i, listed)
    out = listed
    for place, shift in enumerate((127, 1, 128 - N_LAT, N_LAT)):
        moved = pltpu.roll(listed, shift, axis=0)
        out = out + pltpu.roll(moved, 8 * (place + 1), axis=1)
    out_ref[...] = out


def start_kernel(
    where_ref, adj_ref, final_ref, table_ref, sea_ref, count_ref, cell_ref, value_ref,
    on_ref, off_ref, west_ref, east_ref, obs_ref, field_ref, sea8_ref,
):
    par = where_ref[0] % 2
    sub, lane = iotas()
    sea = sea_ref[...].astype(F32)
    sea8 = jnp.concatenate([sea, sea], axis=0)
    sea8_ref[...] = sea8

    def moment_body(p, total):
        for q in range(PAIRS):
            both = final_ref[pl.ds(pl.multiple_of(p * 240 + 16 * q, 16), 16), :].astype(F32)
            for h in range(2):
                jp = (2 * q + h) % PAIRS
                total = total + table_ref[WEIGHT0 + 8 * jp : WEIGHT0 + 8 * jp + 8, :] * both[8 * h : 8 * h + 8, :]
        return total

    total = lax.fori_loop(0, NDIR // 2, moment_body, jnp.zeros((8, LON), F32))
    moment = total + pltpu.roll(total, 4, axis=0)
    field = sea8 * 2.0 / jnp.sqrt(moment)
    field_ref[...] = field
    send_rows(par, adj_ref, on_ref, off_ref, field_ref, sea8_ref)

    west_ref[...] = jnp.zeros_like(west_ref)
    east_ref[...] = jnp.zeros_like(east_ref)
    for lo, hi, north, first_east, second_east in SEGMENTS:

        def body(p, carry):
            for h, east in enumerate((first_east, second_east)):
                k = 2 * p + h
                columns = []
                for jp in range(PAIRS):
                    row = pl.multiple_of(p * 240 + 8 * (h * PAIRS + jp), 8)
                    x = adj_ref[pl.ds(row, 8), :] * sea8
                    columns.append(x[:, :1] if east else x[:, LON - 1 :])
                pack_edge(west_ref if east else east_ref, k, east, columns, lane)
            return carry

        lax.fori_loop(lo, hi, body, 0)
    west_ref[24:32, :] = jnp.broadcast_to(field[:, :1], (8, LON))
    east_ref[24:32, :] = jnp.broadcast_to(field[:, LON - 1 :], (8, LON))
    pick_observations(count_ref, cell_ref, value_ref, obs_ref)


def move(
    src_ref, dst_ref, spectrum_ref, table_ref, gx_ref, coef_ref, lon_east_ref, lon_west_ref,
    north_ref, south_ref, sub, lane, scale8=None, add_ref=None, row_add=None, lon_add=None,
):
    upper = sub >= LAT
    row_of = sub % LAT
    carry = (jnp.zeros((8, LON), F32), jnp.zeros((8, LON), F32))
    for lo, hi, north, first_east, second_east in SEGMENTS:

        def body(p, carry):
            coupling, energy = carry
            halo_ref = north_ref if north else south_ref
            both = None
            for h, east in enumerate((first_east, second_east)):
                k = 2 * p + h
                east_speed = coef_ref[0, k]
                north_speed = coef_ref[1, k]
                row, base = lon_slot(k, east)
                block = (lon_east_ref if east else lon_west_ref)[pl.ds(pl.multiple_of(row, 8), 8), :]
                block = pltpu.roll(block, (LON - base) % LON, axis=1)
                for jp in range(PAIRS):
                    n = h * PAIRS + jp
                    tab = slice(8 * jp, 8 * jp + 8)
                    place = pl.ds(pl.multiple_of(p * 240 + 8 * n, 8), 8)
                    if n % 2 == 0:
                        both = spectrum_ref[
                            pl.ds(pl.multiple_of(p * 240 + 8 * n, 16), 16), :
                        ].astype(F32)
                    spectrum = both[8 * (n % 2) : 8 * (n % 2) + 8, :]
                    mu = src_ref[place, :]
                    if scale8 is not None:
                        mu = mu * scale8 + add_ref[tab, :]
                    lon_halo = block[:, jp : jp + 1]
                    first = k * NFREQ + 2 * jp - (0 if north else SOUTH0)
                    row_halo = jnp.where(
                        upper, halo_ref[pl.ds(first + 1, 1), :], halo_ref[pl.ds(first, 1), :]
                    )
                    if lon_add is not None:
                        lon_halo = lon_halo + lon_add[0 if east else 1][tab, :]
                        row_halo = row_halo + row_add[0 if north else 1][tab, :]
                    if east:
                        along = jnp.where(lane == LON - 1, lon_halo, pltpu.roll(mu, LON - 1, axis=1))
                    else:
                        along = jnp.where(lane == 0, lon_halo, pltpu.roll(mu, 1, axis=1))
                    if north:
                        across = jnp.where(row_of == LAT - 1, row_halo, pltpu.roll(mu, 7, axis=0))
                    else:
                        across = jnp.where(row_of == 0, row_halo, pltpu.roll(mu, 1, axis=0))
                    ax = gx_ref[tab, :] * east_speed
                    ay = table_ref[tab, :] * north_speed
                    nu = mu + ax * (along - mu) + ay * (across - mu)
                    dst_ref[place, :] = nu
                    coupling = coupling + spectrum * nu
                    energy = energy + table_ref[WEIGHT0 + 8 * jp : WEIGHT0 + 8 * jp + 8, :] * spectrum
            return coupling, energy

        carry = lax.fori_loop(lo, hi, body, carry)
    coupling, energy = carry
    return coupling + pltpu.roll(coupling, 4, axis=0), energy + pltpu.roll(energy, 4, axis=0)


def set_speeds(where_ref, table_ref, gx_ref):
    place = pl.multiple_of(STRETCH0 + 8 * where_ref[0], 8)
    stretch = table_ref[pl.ds(place, 8), :]
    for jp in range(PAIRS):
        gx_ref[8 * jp : 8 * jp + 8, :] = table_ref[8 * jp : 8 * jp + 8, :] * stretch


def set_weighted(table_ref, field, dst_ref):
    for jp in range(PAIRS):
        tab = slice(8 * jp, 8 * jp + 8)
        dst_ref[tab, :] = table_ref[WEIGHT0 + 8 * jp : WEIGHT0 + 8 * jp + 8, :] * field


def rates(beta_ref, k, jp, upper):
    return jnp.where(upper, beta_ref[k, 2 * jp + 1], beta_ref[k, 2 * jp])


def middle_kernel(
    where_ref, coef_ref, beta_ref, adj_ref, spectrum_ref, table_ref, sea8_ref, ice_ref, field_ref,
    obs_ref, on_in, off_in, lon_east_ref, lon_west_ref,
    mu_ref, on_ref, off_ref, west_ref, east_ref,
    gx_ref, north_ref, south_ref, add_ref, add_n, add_s, add_e, add_w, one_ref,
):
    par = where_ref[0] % 2
    sub, lane = iotas()
    upper = sub >= LAT
    sea8 = sea8_ref[...]
    set_speeds(where_ref, table_ref, gx_ref)
    take_rows(par, on_in, off_in, north_ref, south_ref)

    wide = lax.broadcasted_iota(jnp.int32, (128, 128), 1).astype(F32)
    own = [jnp.zeros((128, 128), F32) for _ in range(LAT)]
    beside = [jnp.zeros((128, 128), F32) for _ in range(4)]
    for i in range(CAP):
        index = obs_ref[:, i : i + 1]
        value = obs_ref[:, CAP + i : CAP + i + 1]
        for r in range(LAT):
            own[r] = own[r] + jnp.where(index == wide + float(r * LON), value, 0.0)
        for place, target in enumerate(
            (wide, wide + float((LAT - 1) * LON), wide * LON, wide * LON + (LON - 1.0))
        ):
            index = obs_ref[:, 8 * place + 8 + i : 8 * place + 9 + i]
            value = obs_ref[:, 8 * place + 8 + CAP + i : 8 * place + 9 + CAP + i]
            beside[place] = beside[place] + jnp.where(index == target, value, 0.0)
    force = jnp.zeros((8, LON), F32)
    for r in range(LAT):
        force = jnp.where(sub % LAT == r, jnp.sum(own[r], axis=0, keepdims=True), force)
    lines = [jnp.sum(b, axis=0, keepdims=True) for b in beside]
    force_n, force_s = lines[0], lines[1]
    force_e, force_w = (
        jnp.sum(jnp.where(lane == sub % LAT, line, 0.0), axis=1, keepdims=True) for line in lines[2:]
    )
    set_weighted(table_ref, force * field_ref[...], add_ref)
    set_weighted(table_ref, force_n * north_ref[544:552, :], add_n)
    set_weighted(table_ref, force_s * south_ref[544:552, :], add_s)
    set_weighted(table_ref, force_e * lon_east_ref[24:32, :], add_e)
    set_weighted(table_ref, force_w * lon_west_ref[24:32, :], add_w)

    coupling, energy = move(
        adj_ref, mu_ref, spectrum_ref, table_ref, gx_ref, coef_ref, lon_east_ref, lon_west_ref,
        north_ref, south_ref, sub, lane, sea8, add_ref, (add_n, add_s), (add_e, add_w),
    )
    ice = ice_ref[...].astype(F32)
    rate = sea8 * (1.0 - jnp.concatenate([ice, ice], axis=0))
    base = sea8 - 0.2 * rate * energy
    set_weighted(table_ref, 0.2 * rate * coupling, add_ref)
    for lo, hi, north, first_east, second_east in SEGMENTS:

        def body(p, carry):
            for h, east in enumerate((first_east, second_east)):
                k = 2 * p + h
                columns = []
                for jp in range(PAIRS):
                    place = pl.ds(pl.multiple_of(p * 240 + 8 * (h * PAIRS + jp), 8), 8)
                    x = mu_ref[place, :] * (base + rate * rates(beta_ref, k, jp, upper))
                    x = x - add_ref[8 * jp : 8 * jp + 8, :]
                    mu_ref[place, :] = x
                    columns.append(x[:, :1] if east else x[:, LON - 1 :])
                pack_edge(west_ref if east else east_ref, k, east, columns, lane)
            return carry

        lax.fori_loop(lo, hi, body, 0)
    one_ref[...] = jnp.ones((8, LON), F32)
    send_rows(par, mu_ref, on_ref, off_ref, one_ref, one_ref)


def last_kernel(
    where_ref, coef_ref, beta_ref, mu_ref, spectrum_ref, table_ref, ice_ref,
    on_in, off_in, lon_east_ref, lon_west_ref,
    out_ref,
    gx_ref, north_ref, south_ref, add_ref,
):
    par = where_ref[0] % 2
    sub, lane = iotas()
    upper = sub >= LAT
    set_speeds(where_ref, table_ref, gx_ref)
    take_rows(par, on_in, off_in, north_ref, south_ref)
    coupling, energy = move(
        mu_ref, out_ref, spectrum_ref, table_ref, gx_ref, coef_ref, lon_east_ref, lon_west_ref,
        north_ref, south_ref, sub, lane,
    )
    ice = ice_ref[...].astype(F32)
    rate = 1.0 - jnp.concatenate([ice, ice], axis=0)
    base = 1.0 - 0.2 * rate * energy
    set_weighted(table_ref, 0.2 * rate * coupling, add_ref)

    def body(p, carry):
        for h in range(2):
            k = 2 * p + h
            for jp in range(PAIRS):
                place = pl.ds(pl.multiple_of(p * 240 + 8 * (h * PAIRS + jp), 8), 8)
                x = out_ref[place, :] * (base + rate * rates(beta_ref, k, jp, upper))
                out_ref[place, :] = x - add_ref[8 * jp : 8 * jp + 8, :]
        return carry

    lax.fori_loop(0, NDIR // 2, body, 0)


def params():
    return pltpu.CompilerParams(vmem_limit_bytes=40 * MIB)


def f32(*shape):
    return jax.ShapeDtypeStruct(shape, F32)


def level(step):
    return pl.BlockSpec((ROWS, LON), lambda i: (step, 0))


def whole(*shape):
    return pl.BlockSpec(shape, lambda i: tuple(0 for _ in shape))


def exchange(on, off, west, east):
    n_lon, n_lat = lax.axis_size("lon"), lax.axis_size("lat")
    near = [(i, i ^ 1) for i in range(n_lat)]
    far = [(i, ((i + 1) ^ 1) - 1) for i in range(1, n_lat - 1)]
    off = lax.ppermute(off, "lat", far)
    on = lax.ppermute(on, "lat", near)
    from_east = lax.ppermute(west, "lon", [(i, (i - 1) % n_lon) for i in range(n_lon)])
    from_west = lax.ppermute(east, "lon", [(i, (i + 1) % n_lon) for i in range(n_lon)])
    return on, off, from_east, from_west


def on_device(adj_final, saved, beta, sea_mask, ice_mask, obs_count, obs_cell, obs_value):
    per_direction, table = constant_tables()
    coef = jnp.asarray(per_direction)
    table = jnp.asarray(table)
    where = lax.axis_index("lat").astype(jnp.int32).reshape(1)
    adj = adj_final.reshape(ROWS, LON)
    saved = saved.reshape((STEPS + 1) * ROWS, LON)
    tiles = lambda rows: pltpu.VMEM((rows, LON), F32)
    tab_shape = table.shape

    on, off, west, east, obs, field, sea8 = pl.pallas_call(
        start_kernel,
        grid=(1,),
        out_shape=(f32(HALO, LON), f32(HALO, LON), f32(32, LON), f32(32, LON), f32(128, 128), f32(8, LON), f32(8, LON)),
        in_specs=[
            SMEM, whole(ROWS, LON), level(2), whole(*tab_shape), whole(LAT, LON),
            whole(1, 128), whole(*obs_cell.shape), whole(*obs_value.shape),
        ],
        out_specs=(
            whole(HALO, LON), whole(HALO, LON), whole(32, LON), whole(32, LON), whole(128, 128),
            whole(8, LON), whole(8, LON),
        ),
        compiler_params=params(),
        name="edges_and_observations",
    )(where, adj, saved, table, sea_mask, obs_count, obs_cell, obs_value)

    on, off, from_east, from_west = exchange(on, off, west, east)
    obs = lax.all_to_all(obs.reshape(128, 1, 128), ("lon", "lat"), split_axis=0, concat_axis=0, tiled=True)
    obs = obs.reshape(128, 128)

    mu, on, off, west, east = pl.pallas_call(
        middle_kernel,
        grid=(1,),
        out_shape=(f32(ROWS, LON), f32(HALO, LON), f32(HALO, LON), f32(32, LON), f32(32, LON)),
        in_specs=[
            SMEM, SMEM, SMEM, whole(ROWS, LON), level(1), whole(*tab_shape), whole(8, LON), whole(LAT, LON),
            whole(8, LON), whole(128, 128), whole(HALO, LON), whole(HALO, LON), whole(32, LON), whole(32, LON),
        ],
        out_specs=(
            whole(ROWS, LON), whole(HALO, LON), whole(HALO, LON), whole(32, LON), whole(32, LON),
        ),
        scratch_shapes=[tiles(120), tiles(HALO), tiles(HALO)] + [tiles(120)] * 5 + [tiles(8)],
        compiler_params=params(),
        name="first_step",
    )(where, coef, beta, adj, saved, table, sea8, ice_mask, field, obs, on, off, from_east, from_west)

    on, off, from_east, from_west = exchange(on, off, west, east)

    out = pl.pallas_call(
        last_kernel,
        grid=(1,),
        out_shape=f32(ROWS, LON),
        in_specs=[
            SMEM, SMEM, SMEM, whole(ROWS, LON), level(0), whole(*tab_shape), whole(LAT, LON),
            whole(HALO, LON), whole(HALO, LON), whole(32, LON), whole(32, LON),
        ],
        out_specs=whole(ROWS, LON),
        scratch_shapes=[tiles(120), tiles(HALO), tiles(HALO), tiles(120)],
        compiler_params=params(),
        name="last_step",
    )(where, coef, beta, mu, saved, table, ice_mask, on, off, from_east, from_west)
    return out.reshape(adj_final.shape)


def solution(mesh):
    return jax.shard_map(
        on_device,
        mesh=mesh,
        in_specs=(
            P(None, None, "lat", "lon"),
            P(None, None, None, "lat", "lon"),
            P(),
            P("lat", "lon"),
            P("lat", "lon"),
            P(("lon", "lat"), None),
            P(("lon", "lat"), None),
            P(("lon", "lat"), None),
        ),
        out_specs=P(None, None, "lat", "lon"),
        check_vma=False,
    )
```

profile of v0, /device:TPU:1, one launch (start us, length us, event | category | flops | bytes accessed | tf_op | source)
XLA Modules:
  0.0 68.3 jit_solution(4033844255219660549)
XLA Ops:
  0.0 1.9 %copy-done = bf16[3,36,30,4,128]{4,3,2,1,0:T(4,128)(2,1)S(1)} copy-done((bf16[3,36,30,4,128]{4,3,2,1,0:T(4,128)(2,1)S(1)}, bf16[3,36,30,4,128]{4,3,2,1,0:T(4,128)(2,1)}, u32[]{:S(2)}) %copy-start) | copy-done | bytes 3317784
  1.9 1.6 %copy-done.2 = f32[36,30,4,128]{3,2,1,0:T(4,128)S(1)} copy-done((f32[36,30,4,128]{3,2,1,0:T(4,128)S(1)}, f32[36,30,4,128]{3,2,1,0:T(4,128)}, u32[]{:S(2)}) %copy-start.2) | copy-done | bytes 2211864
  3.6 0.9 %copy-done.4 = f32[368,128]{1,0:T(8,128)S(1)} copy-done((f32[368,128]{1,0:T(8,128)S(1)}, f32[368,128]{1,0:T(8,128)}, u32[]{:S(2)}) %copy-start.4) | copy-done | bytes 188440
  4.5 0.7 copy-done.9
  5.2 0.7 copy-done.10
  5.9 0.7 copy-done.11
  6.5 0.7 copy-done.12
  7.2 3.8 %edges_and_observations.1 = (f32[552,128]{1,0:T(8,128)}, f32[552,128]{1,0:T(8,128)}, f32[32,128]{1,0:T(8,128)}, f32[32,128]{1,0:T(8,128)}, f32[128,128]{1,0:T(8,...) custom-call(s32[1]{0:T(128)} %bitcast.where_ref, f32[4320,128]{1,0:T(8,128)S(1)} %bitcast.11, ...), custom_call_target="tpu_custom_call" | custom-call | tf_op jit(solution)/shard_map/edges_and_observations/pallas_call | solution.py:406
  11.0 0.6 copy-done.6
  11.6 1.4 %collective-permute-start = (f32[552,128]{1,0:T(8,128)}, f32[552,128]{1,0:T(8,128)}, u32[]{:S(2)}, u32[]{:S(2)}) collective-permute-start(f32[552,128]{1,0:T(8,128)} %get-tuple-element.20), channel_id=1, source_target_pairs={{0,1},{1,0},{2,3},{3,2},{4,5},{5,4},{6,7},{7,6},{8,9},{9,8},{10,11... | collective-permute-start | bytes 847880 | tf_op jit(solution)/shard_map/ppermute | solution.py:390
  13.0 4.8 %collective-permute-start.1 = (f32[552,128]{1,0:T(8,128)}, f32[552,128]{1,0:T(8,128)}, u32[]{:S(2)}, u32[]{:S(2)}) collective-permute-start(f32[552,128]{1,0:T(8,128)} %get-tuple-element.21), channel_id=1, source_target_pairs={{1,2},{2,1},{3,4},{4,3},{5,6},{6,5},{7,8},{8,7},{9,10},{10,9},{11,... | collective-permute-start | bytes 847880 | tf_op jit(solution)/shard_map/ppermute | solution.py:389
  17.8 9.3 %all-to-all-start = ((f32[128,1,128]{2,1,0:T(1,128)}), f32[128,1,128]{2,1,0:T(1,128)}, u32[]{:S(2)}, u32[]{:S(2)}) async-start(f32[128,1,128]{2,1,0:T(1,128)} %bitcast.13), calls=%async_computation | async-start | bytes 131072 | tf_op jit(solution)/shard_map/all_to_all | solution.py:423
  27.1 3.6 %collective-permute-start.2 = (f32[32,128]{1,0:T(8,128)}, f32[32,128]{1,0:T(8,128)S(1)}, u32[]{:S(2)}, u32[]{:S(2)}) collective-permute-start(f32[32,128]{1,0:T(8,128)} %get-tuple-element.22), channel_id=1, source_target_pairs={{0,112},{16,0},{32,16},{48,32},{64,48},{80,64},{96,80},{112,96},{1... | collective-permute-start | bytes 49160 | tf_op jit(solution)/shard_map/ppermute | solution.py:391
  30.7 0.0 collective-permute-start.3
  30.7 0.8 %copy.15.beta_ref = f32[36,30]{1,0:T(8,128)S(1)} copy(f32[36,30]{0,1:T(8,128)} %param.12) | data formatting | bytes 8640 | tf_op args[2]
  31.5 0.3 collective-permute-done.2.lon_east_ref
  31.8 4.2 %collective-permute-done.3.lon_west_ref = f32[32,128]{1,0:T(8,128)} collective-permute-done((f32[32,128]{1,0:T(8,128)}, f32[32,128]{1,0:T(8,128)}, u32[]{:S(2)}, u32[]{:S(2)}) %collective-permute-start.3) | collective-permute-done | bytes 16416 | tf_op jit(solution)/shard_map/ppermute | solution.py:392
  36.0 0.6 all-to-all-done
  36.7 0.0 collective-permute-done.on_in
  36.7 0.0 collective-permute-done.1.off_in
  36.7 0.0 copy-start.3
  36.7 1.6 %copy-done.3 = f32[36,30,4,128]{3,2,1,0:T(4,128)S(1)} copy-done((f32[36,30,4,128]{3,2,1,0:T(4,128)S(1)}, f32[36,30,4,128]{3,2,1,0:T(4,128)}, u32[]{:S(2)}) %copy-start.3) | copy-done | bytes 2211864
  38.3 0.7 copy-done.8
  39.0 8.5 %first_step.1 = (f32[4320,128]{1,0:T(8,128)S(1)}, f32[552,128]{1,0:T(8,128)S(1)}, f32[552,128]{1,0:T(8,128)S(1)}, f32[32,128]{1,0:T(8,128)S(1)}, f32[32,128]{1,0:T(8,128)S(1)}) custom-call(s32[1]{0:T(128)} %bitcast.where_ref, f32[2,36]{1,0:T(2,128)S(1)} %copy-done.8, f32[36,30]{1,0:T(8,128)S(1)} %copy.15.beta_ref, f32[4320,128]{1,0:T(8,128)S(1)} %bitcast.12, ...), custom_call_target="tpu_custom_call" | custom-call | tf_op jit(solution)/shard_map/first_step/pallas_call | solution.py:426
  47.5 1.2 %collective-permute-start.4 = (f32[552,128]{1,0:T(8,128)S(1)}, f32[552,128]{1,0:T(8,128)S(1)}, u32[]{:S(2)}, u32[]{:S(2)}) collective-permute-start(f32[552,128]{1,0:T(8,128)S(1)} %get-tuple-element.25), channel_id=1, source_target_pairs={{0,1},{1,0},{2,3},{3,2},{4,5},{5,4},{6,7},{7,6},{8,9},{9,8},{10,11... | collective-permute-start | bytes 847880 | tf_op jit(solution)/shard_map/ppermute | solution.py:390
  48.7 4.1 %collective-permute-start.5 = (f32[552,128]{1,0:T(8,128)S(1)}, f32[552,128]{1,0:T(8,128)S(1)}, u32[]{:S(2)}, u32[]{:S(2)}) collective-permute-start(f32[552,128]{1,0:T(8,128)S(1)} %get-tuple-element.26), channel_id=1, source_target_pairs={{1,2},{2,1},{3,4},{4,3},{5,6},{6,5},{7,8},{8,7},{9,10},{10,9},{11,... | collective-permute-start | bytes 847880 | tf_op jit(solution)/shard_map/ppermute | solution.py:389
  52.8 0.1 collective-permute-start.6
  52.8 1.5 %collective-permute-start.7 = (f32[32,128]{1,0:T(8,128)S(1)}, f32[32,128]{1,0:T(8,128)S(1)}, u32[]{:S(2)}, u32[]{:S(2)}) collective-permute-start(f32[32,128]{1,0:T(8,128)S(1)} %get-tuple-element.28), channel_id=1, source_target_pairs={{0,16},{16,32},{32,48},{48,64},{64,80},{80,96},{96,112},{112,0},{1... | collective-permute-start | bytes 49160 | tf_op jit(solution)/shard_map/ppermute | solution.py:392
  54.3 1.8 %collective-permute-done.6.lon_east_ref = f32[32,128]{1,0:T(8,128)S(1)} collective-permute-done((f32[32,128]{1,0:T(8,128)S(1)}, f32[32,128]{1,0:T(8,128)S(1)}, u32[]{:S(2)}, u32[]{:S(2)}) %collective-permute-start.6) | collective-permute-done | bytes 16416 | tf_op jit(solution)/shard_map/ppermute | solution.py:391
  56.1 1.5 %collective-permute-done.7.lon_west_ref = f32[32,128]{1,0:T(8,128)S(1)} collective-permute-done((f32[32,128]{1,0:T(8,128)S(1)}, f32[32,128]{1,0:T(8,128)S(1)}, u32[]{:S(2)}, u32[]{:S(2)}) %collective-permute-start.7) | collective-permute-done | bytes 16416 | tf_op jit(solution)/shard_map/ppermute | solution.py:392
  57.6 3.6 %collective-permute-done.5.off_in = f32[552,128]{1,0:T(8,128)S(1)} collective-permute-done((f32[552,128]{1,0:T(8,128)S(1)}, f32[552,128]{1,0:T(8,128)S(1)}, u32[]{:S(2)}, u32[]{:S(2)}) %collective-permute-start.5) | collective-permute-done | bytes 282656 | tf_op jit(solution)/shard_map/ppermute | solution.py:389
  61.3 7.1 %last_step.1 = f32[4320,128]{1,0:T(8,128)} custom-call(s32[1]{0:T(128)} %bitcast.where_ref, f32[2,36]{1,0:T(2,128)S(1)} %copy-done.8, f32[36,30]{1,0:T(8,128)S(1)} %copy.15.beta_ref, f32[4320,128]{1,0:T(8,128)S(1)} %get-tuple-element.24.mu_ref, bf16[12960,128]{1,0:T(8,128)(2,1)S(1)} %bitcast.10, f32[368,128]{1,0:T(8,128)S(1)} %copy-done.5, ...), custom_call_target="tpu_custom_call" | custom-call | tf_op jit(solution)/shard_map/last_step/pallas_call | solution.py:444
  (16 shorter events, 0.0 us)
Async XLA Ops:
  0.0 1.9 %copy-start = (bf16[3,36,30,4,128]{4,3,2,1,0:T(4,128)(2,1)S(1)}, bf16[3,36,30,4,128]{4,3,2,1,0:T(4,128)(2,1)}, u32[]{:S(2)}) copy-start(bf16[3,36,30,4,128]{4,3,2,1,0:T(4,128)(2,1)} %param.11) | copy-start | bytes 9953284
  1.9 1.6 %copy-start.2 = (f32[36,30,4,128]{3,2,1,0:T(4,128)S(1)}, f32[36,30,4,128]{3,2,1,0:T(4,128)}, u32[]{:S(2)}) copy-start(f32[36,30,4,128]{3,2,1,0:T(4,128)} %param.10) | copy-start | bytes 6635524
  3.6 0.9 %copy-start.4 = (f32[368,128]{1,0:T(8,128)S(1)}, f32[368,128]{1,0:T(8,128)}, u32[]{:S(2)}) copy-start(f32[368,128]{1,0:T(8,128)} %constant.9.clone.table_ref) | copy-start | bytes 565252
  4.5 0.7 copy-start.9
  5.2 0.7 copy-start.10
  5.9 0.7 copy-start.11
  6.5 0.7 copy-start.12
  7.2 29.5 %copy-start.1 = (bf16[3,36,30,4,128]{4,3,2,1,0:T(4,128)(2,1)S(1)}, bf16[3,36,30,4,128]{4,3,2,1,0:T(4,128)(2,1)}, u32[]{:S(2)}) copy-start(bf16[3,36,30,4,128]{4,3,2,1,0:T(4,128)(2,1)} %param.11) | copy-start | bytes 9953284
  7.2 29.5 %copy-start.5 = (f32[368,128]{1,0:T(8,128)S(1)}, f32[368,128]{1,0:T(8,128)}, u32[]{:S(2)}) copy-start(f32[368,128]{1,0:T(8,128)} %constant.9.clone.table_ref) | copy-start | bytes 565252
  7.2 29.5 %copy-start.7 = (s32[4,128]{1,0:T(4,128)S(1)}, s32[4,128]{1,0:T(4,128)}, u32[]{:S(2)}) copy-start(s32[4,128]{1,0:T(4,128)} %ice_ref.3) | copy-start | bytes 6148
  10.9 0.6 copy-start.6
  11.6 25.1 %collective-permute-start = (f32[552,128]{1,0:T(8,128)}, f32[552,128]{1,0:T(8,128)}, u32[]{:S(2)}, u32[]{:S(2)}) collective-permute-start(f32[552,128]{1,0:T(8,128)} %get-tuple-element.20), channel_id=1, source_target_pairs={{0,1},{1,0},{2,3},{3,2},{4,5},{5,4},{6,7},{7,6},{8,9},{9,8},{10,11... | collective-permute-start | bytes 847880 | tf_op jit(solution)/shard_map/ppermute | solution.py:390
  13.0 23.7 %collective-permute-start.1 = (f32[552,128]{1,0:T(8,128)}, f32[552,128]{1,0:T(8,128)}, u32[]{:S(2)}, u32[]{:S(2)}) collective-permute-start(f32[552,128]{1,0:T(8,128)} %get-tuple-element.21), channel_id=1, source_target_pairs={{1,2},{2,1},{3,4},{4,3},{5,6},{6,5},{7,8},{8,7},{9,10},{10,9},{11,... | collective-permute-start | bytes 847880 | tf_op jit(solution)/shard_map/ppermute | solution.py:389
  17.8 18.9 %all-to-all-start = ((f32[128,1,128]{2,1,0:T(1,128)}), f32[128,1,128]{2,1,0:T(1,128)}, u32[]{:S(2)}, u32[]{:S(2)}) async-start(f32[128,1,128]{2,1,0:T(1,128)} %bitcast.13), calls=%async_computation | async-start | bytes 131072 | tf_op jit(solution)/shard_map/all_to_all | solution.py:423
  27.1 4.7 %collective-permute-start.2 = (f32[32,128]{1,0:T(8,128)}, f32[32,128]{1,0:T(8,128)S(1)}, u32[]{:S(2)}, u32[]{:S(2)}) collective-permute-start(f32[32,128]{1,0:T(8,128)} %get-tuple-element.22), channel_id=1, source_target_pairs={{0,112},{16,0},{32,16},{48,32},{64,48},{80,64},{96,80},{112,96},{1... | collective-permute-start | bytes 49160 | tf_op jit(solution)/shard_map/ppermute | solution.py:391
  30.7 5.3 %collective-permute-start.3 = (f32[32,128]{1,0:T(8,128)}, f32[32,128]{1,0:T(8,128)}, u32[]{:S(2)}, u32[]{:S(2)}) collective-permute-start(f32[32,128]{1,0:T(8,128)} %get-tuple-element.23), channel_id=1, source_target_pairs={{0,16},{16,32},{32,48},{48,64},{64,80},{80,96},{96,112},{112,0},{1... | collective-permute-start | bytes 49160 | tf_op jit(solution)/shard_map/ppermute | solution.py:392
  36.7 1.6 %copy-start.3 = (f32[36,30,4,128]{3,2,1,0:T(4,128)S(1)}, f32[36,30,4,128]{3,2,1,0:T(4,128)}, u32[]{:S(2)}) copy-start(f32[36,30,4,128]{3,2,1,0:T(4,128)} %param.10) | copy-start | bytes 6635524
  38.3 0.7 copy-start.8
  47.5 10.1 %collective-permute-start.4 = (f32[552,128]{1,0:T(8,128)S(1)}, f32[552,128]{1,0:T(8,128)S(1)}, u32[]{:S(2)}, u32[]{:S(2)}) collective-permute-start(f32[552,128]{1,0:T(8,128)S(1)} %get-tuple-element.25), channel_id=1, source_target_pairs={{0,1},{1,0},{2,3},{3,2},{4,5},{5,4},{6,7},{7,6},{8,9},{9,8},{10,11... | collective-permute-start | bytes 847880 | tf_op jit(solution)/shard_map/ppermute | solution.py:390
  48.7 12.6 %collective-permute-start.5 = (f32[552,128]{1,0:T(8,128)S(1)}, f32[552,128]{1,0:T(8,128)S(1)}, u32[]{:S(2)}, u32[]{:S(2)}) collective-permute-start(f32[552,128]{1,0:T(8,128)S(1)} %get-tuple-element.26), channel_id=1, source_target_pairs={{1,2},{2,1},{3,4},{4,3},{5,6},{6,5},{7,8},{8,7},{9,10},{10,9},{11,... | collective-permute-start | bytes 847880 | tf_op jit(solution)/shard_map/ppermute | solution.py:389
  52.8 3.3 %collective-permute-start.6 = (f32[32,128]{1,0:T(8,128)S(1)}, f32[32,128]{1,0:T(8,128)S(1)}, u32[]{:S(2)}, u32[]{:S(2)}) collective-permute-start(f32[32,128]{1,0:T(8,128)S(1)} %get-tuple-element.27), channel_id=1, source_target_pairs={{0,112},{16,0},{32,16},{48,32},{64,48},{80,64},{96,80},{112,96},{1... | collective-permute-start | bytes 49160 | tf_op jit(solution)/shard_map/ppermute | solution.py:391
  52.8 4.8 %collective-permute-start.7 = (f32[32,128]{1,0:T(8,128)S(1)}, f32[32,128]{1,0:T(8,128)S(1)}, u32[]{:S(2)}, u32[]{:S(2)}) collective-permute-start(f32[32,128]{1,0:T(8,128)S(1)} %get-tuple-element.28), channel_id=1, source_target_pairs={{0,16},{16,32},{32,48},{48,64},{64,80},{80,96},{96,112},{112,0},{1... | collective-permute-start | bytes 49160 | tf_op jit(solution)/shard_map/ppermute | solution.py:392
where the time goes:
time: 68.8 us; the launch traced here: 68.3 us
  starting transfers between devices  25.9 us (38%)
  Pallas kernels  19.3 us (28%)
  waiting for transfers between devices  12.1 us (18%)
  local copies, waits for them, and re-layouts  10.9 us (16%)
    unnamed x27, local copies, waits for them, and re-layouts  10.9 us
    all_to_all x1, starting transfers between devices, on_device(): lax.all_to_all(obs.reshape(128, 1, 128), ('lon', 'lat'), split_axis=0, co...  9.33 us
    ppermute x2, starting transfers between devices, exchange(): off = lax.ppermute(off, 'lat', far)  8.84 us
    pallas_call x1, Pallas kernels, on_device(): pl.pallas_call(middle_kernel, grid=(1,), out_shape=(f32(ROWS, LON), f32(H...  8.5 us
    pallas_call x1, Pallas kernels, on_device(): pl.pallas_call(last_kernel, grid=(1,), out_shape=f32(ROWS, LON), in_specs...  7.07 us
    ppermute x2, waiting for transfers between devices, exchange(): lax.ppermute(east, 'lon', [(i, (i + 1) % n_lon) for i in range(n_lon)])  5.73 us
    pallas_call x1, Pallas kernels, on_device(): pl.pallas_call(start_kernel, grid=(1,), out_shape=(f32(HALO, LON), f32(HA...  3.75 us
    ppermute x2, waiting for transfers between devices, exchange(): off = lax.ppermute(off, 'lat', far)  3.65 us
  transfers between devices with their start and end apart: 9, of which 6 were waited for; matrix products, arithmetic and copies ran while one was open for 1% of the time, Pallas kernels for 0%

commit v1 on v0

v1 whole, which is shorter than its diff:
```python
import math

import jax
import jax.numpy as jnp
import numpy as np
from jax import lax
from jax.experimental import pallas as pl
from jax.experimental.pallas import tpu as pltpu
from jax.sharding import PartitionSpec as P

STEPS = 2
CAP = 4
NDIR = 36
NFREQ = 30
QUAD = NDIR // 4
PAIRS = NFREQ // 2
LAT = 4
LON = 128
BLOCK = NFREQ * LAT
ROWS = NDIR * BLOCK
HALO = 552
SOUTH0 = 536
EDGE = 40
SPREAD = 2208
N_LAT = 16
N_LON = 8
MIB = 2**20
F32 = jnp.float32

HBM = pl.BlockSpec(memory_space=pltpu.HBM)
VMEM = pl.BlockSpec(memory_space=pltpu.VMEM)
SMEM = pl.BlockSpec(memory_space=pltpu.SMEM)

QUADRANTS = ((True, True), (True, False), (False, False), (False, True))

WEIGHT0 = 0
SPEED0 = BLOCK
COS0 = 2 * BLOCK
SIN0 = COS0 + 8 * QUAD
STRETCH0 = SIN0 + 8 * QUAD


def constant_table():
    angle = (np.arange(QUAD) + 0.5) * (2.0 * math.pi / NDIR)
    j = np.arange(NFREQ)
    speed = 1.1 ** (-j.astype(np.float64))
    growth = 1.1 ** j.astype(np.float64)
    weight = growth / (NDIR * growth.sum())
    rows = np.arange(N_LAT * LAT)
    latitude = (rows + 0.5 - N_LAT * LAT / 2.0) * (100.0 / (N_LAT * LAT))
    stretch = math.cos(50.0 * math.pi / 180.0) / np.cos(latitude * (math.pi / 180.0))
    stretch = np.tile(stretch.reshape(N_LAT, 1, LAT), (1, 2, 1)).reshape(-1)
    column = np.concatenate(
        [
            np.repeat(weight, LAT),
            np.repeat(speed, LAT),
            np.repeat(np.cos(angle), 8),
            np.repeat(np.sin(angle), 8),
            stretch,
        ]
    )
    return np.tile(column[:, None], (1, LON)).astype(np.float32)


def iotas():
    sub = lax.broadcasted_iota(jnp.int32, (8, LON), 0)
    lane = lax.broadcasted_iota(jnp.int32, (8, LON), 1)
    return sub, lane


def tab(jp):
    return slice(8 * jp, 8 * jp + 8)


def weights(table_ref, jp):
    return table_ref[WEIGHT0 + 8 * jp : WEIGHT0 + 8 * jp + 8, :]


def edge_block(quadrant, jp):
    first = 8 * (2 * (quadrant // 2) + jp // 8)
    return slice(first, first + 8)


def over_directions(body, carry):
    def two(v, carry):
        return body(2 * v + 1, 1, body(2 * v, 0, carry))

    carry = lax.fori_loop(0, QUAD // 2, two, carry)
    return body(QUAD - 1, (QUAD - 1) % 2, carry)


def spectrum_reader(ref, k, odd, level=0):
    first = level * ROWS + k * BLOCK - (8 if odd else 0)
    held = {}

    def read(jp):
        place, part = divmod(jp + odd, 2)
        if place not in held:
            held.clear()
            rows = pl.ds(pl.multiple_of(first + 16 * place, 16), 16)
            held[place] = ref[rows, :].astype(F32)
        return held[place][8 * part : 8 * part + 8, :]

    return read


def direction_rows(i, quadrant, jp=0, count=8):
    return pl.ds(pl.multiple_of((i + QUAD * quadrant) * BLOCK + 8 * jp, 8), count)


def extract_rows(src, r, first, dst, scale):
    def body(m, carry):
        for u in range(4):
            start = (first + 8 * (4 * m + u)) * LAT + r
            value = src[pl.ds(start, 8, stride=LAT), :]
            if scale is not None:
                value = value * scale
            dst[pl.ds(pl.multiple_of(8 * (4 * m + u), 8), 8), :] = value
        return carry

    lax.fori_loop(0, 17, body, 0)


def send_rows(par, src, on_ref, off_ref, field=None, scale8=None):
    def put(dst, r, first):
        extract_rows(src, r, first, dst, None if scale8 is None else scale8[r : r + 1, :])
        if field is not None:
            dst[pl.ds(544, 8), :] = jnp.broadcast_to(field[r : r + 1, :], (8, LON))

    @pl.when(par == 0)
    def _():
        put(on_ref, LAT - 1, SOUTH0)
        put(off_ref, 0, 0)

    @pl.when(par == 1)
    def _():
        put(on_ref, 0, 0)
        put(off_ref, LAT - 1, SOUTH0)


def spread_rows(par, on_ref, off_ref, north_ref, south_ref, field_ref=None):
    def spread(src, dst, r):
        def body(m, carry):
            for u in range(4):
                first = 8 * (4 * m + u)
                dst[pl.ds(first * LAT + r, 8, stride=LAT), :] = src[pl.ds(pl.multiple_of(first, 8), 8), :]
            return carry

        lax.fori_loop(0, 17, body, 0)

    for parity, (north, south) in enumerate(((on_ref, off_ref), (off_ref, on_ref))):

        @pl.when(par == parity)
        def _():
            spread(north, north_ref, LAT - 1)
            spread(south, south_ref, 0)
            if field_ref is not None:
                field_ref[0:8, :] = north[544:552, :]
                field_ref[8:16, :] = south[544:552, :]


def pack_edges(west_ref, east_ref, i, value_of, lane):
    relative = lane - 8 * i
    here = (relative >= 0) & (relative < 8)
    refs = [west_ref if east else east_ref for _, east in QUADRANTS]
    for lo, hi in ((0, 8), (8, PAIRS)):
        blocks = [None] * 4
        for jp in range(lo, hi):
            for q, (_, east) in enumerate(QUADRANTS):
                x = value_of(q, jp)
                shift = jp - lo + (0 if east else 1)
                x = pltpu.roll(x, shift, axis=1) if shift else x
                blocks[q] = x if jp == lo else jnp.where(lane == jp - lo, x, blocks[q])
        for q in range(4):
            place = edge_block(q, lo)
            moved = pltpu.roll(blocks[q], 8 * i, axis=1)
            refs[q][place, :] = jnp.where(here, moved, refs[q][place, :])


def pick_observations(count, cell, value, out_ref):
    sub = lax.broadcasted_iota(jnp.int32, (128, 128), 0)
    lane = lax.broadcasted_iota(jnp.int32, (128, 128), 1)
    counts = jnp.broadcast_to(count.astype(F32), (128, 128))
    starts = jnp.sum(jnp.where(lane < sub, counts, 0.0), axis=1, keepdims=True)
    mine = jnp.sum(jnp.where(lane == sub, counts, 0.0), axis=1, keepdims=True)
    local = (((cell >> 10) & (LAT - 1)) * LON + (cell & (LON - 1))).astype(F32)
    slots = cell.shape[1]
    slot = lax.broadcasted_iota(jnp.int32, (128, slots), 1).astype(F32)
    listed = jnp.zeros((128, 128), F32)
    for i in range(CAP):
        hit = slot == starts + float(i)
        index_i = jnp.sum(jnp.where(hit, local, 0.0), axis=1, keepdims=True)
        value_i = jnp.sum(jnp.where(hit, value, 0.0), axis=1, keepdims=True)
        value_i = jnp.where(mine > float(i), value_i, 0.0)
        listed = jnp.where(lane == i, index_i, listed)
        listed = jnp.where(lane == CAP + i, value_i, listed)
    out = listed
    for place, shift in enumerate((127, 1, 128 - N_LAT, N_LAT)):
        moved = pltpu.roll(listed, shift, axis=0)
        out = out + pltpu.roll(moved, 8 * (place + 1), axis=1)
    out_ref[...] = out


def fetch(sems, *pairs):
    copies = [pltpu.make_async_copy(src, dst, sems.at[n]) for n, (src, dst) in enumerate(pairs)]
    for copy in copies:
        copy.start()
    return copies


def start_kernel(
    where_ref, adj_hbm, saved_hbm, table_hbm, sea_hbm, count_hbm, cell_hbm, value_hbm,
    on_ref, off_ref, west_ref, east_ref, obs_ref, field_ref, sea8_ref, early_ref,
    adj_ref, final_ref, table_ref, sea_ref, count_ref, cell_ref, value_ref, sems,
):
    half = ROWS // 2
    final0 = STEPS * ROWS
    copies = fetch(
        sems,
        (count_hbm, count_ref),
        (cell_hbm, cell_ref),
        (value_hbm, value_ref),
        (sea_hbm, sea_ref),
        (table_hbm.at[pl.ds(0, BLOCK)], table_ref),
        (saved_hbm.at[pl.ds(final0, half)], final_ref.at[pl.ds(0, half)]),
        (saved_hbm.at[pl.ds(final0 + half, half)], final_ref.at[pl.ds(half, half)]),
        (adj_hbm.at[pl.ds(0, half)], adj_ref.at[pl.ds(0, half)]),
        (adj_hbm.at[pl.ds(half, half)], adj_ref.at[pl.ds(half, half)]),
        (saved_hbm.at[pl.ds(ROWS, ROWS)], early_ref.at[pl.ds(ROWS, ROWS)]),
        (saved_hbm.at[pl.ds(0, ROWS)], early_ref.at[pl.ds(0, ROWS)]),
    )
    par = where_ref[0] % 2
    sub, lane = iotas()
    for copy in copies[:3]:
        copy.wait()
    pick_observations(count_ref[...], cell_ref[...], value_ref[...], obs_ref)
    for copy in copies[3:7]:
        copy.wait()
    sea = sea_ref[...].astype(F32)
    sea8 = jnp.concatenate([sea, sea], axis=0)
    sea8_ref[...] = sea8

    def moment(i, odd, total):
        read = [spectrum_reader(final_ref, i + QUAD * q, (odd + q) % 2) for q in range(4)]
        for jp in range(PAIRS):
            both = (read[0](jp) + read[1](jp)) + (read[2](jp) + read[3](jp))
            total = total + weights(table_ref, jp) * both
        return total

    total = over_directions(moment, jnp.zeros((8, LON), F32))
    field = sea8 * 2.0 / jnp.sqrt(total + pltpu.roll(total, 4, axis=0))
    field_ref[...] = field
    for copy in copies[7:9]:
        copy.wait()
    send_rows(par, adj_ref, on_ref, off_ref, field_ref, sea8_ref)

    west_ref[...] = jnp.zeros_like(west_ref)
    east_ref[...] = jnp.zeros_like(east_ref)

    def pack(i, carry):
        pack_edges(west_ref, east_ref, i, lambda q, jp: adj_ref[direction_rows(i, q, jp), :], lane)
        return carry

    lax.fori_loop(0, QUAD, pack, 0)
    west_sea = jnp.broadcast_to(sea8[:, :1], (8, LON))
    east_sea = jnp.broadcast_to(sea8[:, LON - 1 :], (8, LON))
    for block in range(4):
        west_ref[tab(block), :] = west_ref[tab(block), :] * west_sea
        east_ref[tab(block), :] = east_ref[tab(block), :] * east_sea
    west_ref[32:40, :] = jnp.broadcast_to(field[:, :1], (8, LON))
    east_ref[32:40, :] = jnp.broadcast_to(field[:, LON - 1 :], (8, LON))
    for copy in copies[9:]:
        copy.wait()


def speeds_of(table_ref, stretch, i):
    cos_i = table_ref[pl.ds(pl.multiple_of(COS0 + 8 * i, 8), 8), :]
    sin_i = table_ref[pl.ds(pl.multiple_of(SIN0 + 8 * i, 8), 8), :]
    stretched = 0.7 * stretch
    return (cos_i * stretched, sin_i * stretched), (0.6 * sin_i, 0.6 * cos_i)


def turned_edges(lon_east_ref, lon_west_ref, i):
    turn = (LON - 8 * i) % LON
    out = {}
    for q, (_, east) in enumerate(QUADRANTS):
        for lo in (0, 8):
            ref = lon_east_ref if east else lon_west_ref
            out[q, lo] = pltpu.roll(ref[edge_block(q, lo), :], turn, axis=1)

    def edge(q, jp):
        shift = ((LON - 1 if QUADRANTS[q][1] else 0) - jp % 8) % LON
        block = out[q, 8 * (jp // 8)]
        return pltpu.roll(block, shift, axis=1) if shift else block

    return edge


def row_halo_of(north_ref, south_ref, i, q, jp):
    if QUADRANTS[q][0]:
        return north_ref[direction_rows(i, q, jp), :]
    row = (i + QUAD * q - NDIR // 2) * BLOCK + 8 * jp + 16
    return south_ref[pl.ds(pl.multiple_of(row, 8), 8), :]


def both_halves(total):
    return total + pltpu.roll(total, 4, axis=0)


def speed_of(table_ref, jp):
    return table_ref[SPEED0 + 8 * jp : SPEED0 + 8 * jp + 8, :]


def move(dst_ref, spectrum_ref, level, table_ref, stretch, sub, lane, value_of, lon_of, row_of):
    row = sub % LAT

    def body(i, odd, carry):
        coupling, energy = carry
        x_speed, y_speed = speeds_of(table_ref, stretch, i)
        read = [spectrum_reader(spectrum_ref, i + QUAD * q, (odd + q) % 2, level) for q in range(4)]
        lon_halo = lon_of(i)
        for jp in range(PAIRS):
            all_of = None
            for q, (north, east) in enumerate(QUADRANTS):
                spectrum = read[q](jp)
                mu = value_of(i, q, jp)
                turned = pltpu.roll(mu, LON - 1 if east else 1, axis=1)
                along = jnp.where(lane == (LON - 1 if east else 0), lon_halo(q, jp), turned)
                shifted = pltpu.roll(mu, 7 if north else 1, axis=0)
                across = jnp.where(row == (LAT - 1 if north else 0), row_of(i, q, jp), shifted)
                change = x_speed[q % 2] * (along - mu) + y_speed[q % 2] * (across - mu)
                nu = mu + speed_of(table_ref, jp) * change
                dst_ref[direction_rows(i, q, jp), :] = nu
                coupling = coupling + spectrum * nu
                all_of = spectrum if all_of is None else all_of + spectrum
            energy = energy + weights(table_ref, jp) * all_of
        return coupling, energy

    coupling, energy = over_directions(body, (jnp.zeros((8, LON), F32), jnp.zeros((8, LON), F32)))
    return both_halves(coupling), both_halves(energy)


def stretch_of(where_ref, table_ref):
    return table_ref[pl.ds(pl.multiple_of(STRETCH0 + 8 * where_ref[0], 8), 8), :]


def set_weighted(table_ref, field, dst_ref):
    for jp in range(PAIRS):
        dst_ref[tab(jp), :] = weights(table_ref, jp) * field


def rate_of(beta_ref, k, jp, upper):
    return jnp.where(upper, beta_ref[2 * jp + 1, k], beta_ref[2 * jp, k])


def sum_observations(obs_ref, sub, lane):
    wide = lax.broadcasted_iota(jnp.int32, (128, 128), 1).astype(F32)
    own = [jnp.zeros((128, 128), F32) for _ in range(LAT)]
    beside = [jnp.zeros((128, 128), F32) for _ in range(4)]
    for i in range(CAP):
        index = obs_ref[:, i : i + 1]
        value = obs_ref[:, CAP + i : CAP + i + 1]
        for r in range(LAT):
            own[r] = own[r] + jnp.where(index == wide + float(r * LON), value, 0.0)
        for place, target in enumerate(
            (wide, wide + float((LAT - 1) * LON), wide * LON, wide * LON + (LON - 1.0))
        ):
            index = obs_ref[:, 8 * place + 8 + i : 8 * place + 9 + i]
            value = obs_ref[:, 8 * place + 8 + CAP + i : 8 * place + 9 + CAP + i]
            beside[place] = beside[place] + jnp.where(index == target, value, 0.0)
    force = jnp.zeros((8, LON), F32)
    for r in range(LAT):
        force = jnp.where(sub % LAT == r, jnp.sum(own[r], axis=0, keepdims=True), force)
    lines = [jnp.sum(b, axis=0, keepdims=True) for b in beside]
    force_n, force_s = lines[0], lines[1]
    force_e, force_w = (
        jnp.sum(jnp.where(lane == sub % LAT, line, 0.0), axis=1, keepdims=True) for line in lines[2:]
    )
    return force, force_n, force_s, force_e, force_w


def middle_kernel(
    where_ref, beta_hbm, adj_ref, spectrum_ref, table_ref, sea8_ref, ice_ref, field_ref,
    obs_ref, on_in, off_in, lon_east_ref, lon_west_ref,
    mu_ref, on_ref, off_ref, west_ref, east_ref,
    beta_ref, north_ref, south_ref, fields_ref, add_ref, add_n, add_s, add_e, add_w, sems,
):
    copies = fetch(sems, (beta_hbm, beta_ref))
    par = where_ref[0] % 2
    sub, lane = iotas()
    sea8 = sea8_ref[...]
    stretch = stretch_of(where_ref, table_ref)
    force, force_n, force_s, force_e, force_w = sum_observations(obs_ref, sub, lane)
    spread_rows(par, on_in, off_in, north_ref, south_ref, fields_ref)
    set_weighted(table_ref, force * field_ref[...], add_ref)
    set_weighted(table_ref, force_n * fields_ref[0:8, :], add_n)
    set_weighted(table_ref, force_s * fields_ref[8:16, :], add_s)
    set_weighted(table_ref, force_e * lon_east_ref[32:40, :], add_e)
    set_weighted(table_ref, force_w * lon_west_ref[32:40, :], add_w)

    def lon_of(i):
        edge = turned_edges(lon_east_ref, lon_west_ref, i)
        return lambda q, jp: edge(q, jp) + (add_e if QUADRANTS[q][1] else add_w)[tab(jp), :]

    coupling, energy = move(
        mu_ref, spectrum_ref, 1, table_ref, stretch, sub, lane,
        lambda i, q, jp: adj_ref[direction_rows(i, q, jp), :] * sea8 + add_ref[tab(jp), :],
        lon_of,
        lambda i, q, jp: row_halo_of(north_ref, south_ref, i, q, jp)
        + (add_n if QUADRANTS[q][0] else add_s)[tab(jp), :],
    )
    upper = sub >= LAT
    ice = ice_ref[...].astype(F32)
    rate = sea8 * (1.0 - jnp.concatenate([ice, ice], axis=0))
    base = sea8 - 0.2 * rate * energy
    set_weighted(table_ref, 0.2 * rate * coupling, add_ref)
    west_ref[...] = jnp.zeros_like(west_ref)
    east_ref[...] = jnp.zeros_like(east_ref)
    copies[0].wait()

    def source(i, carry):
        def value_of(q, jp):
            beta = rate_of(beta_ref, i + QUAD * q, jp, upper)
            place = direction_rows(i, q, jp)
            x = mu_ref[place, :] * (base + rate * beta) - add_ref[tab(jp), :]
            mu_ref[place, :] = x
            return x

        pack_edges(west_ref, east_ref, i, value_of, lane)
        return carry

    lax.fori_loop(0, QUAD, source, 0)
    send_rows(par, mu_ref, on_ref, off_ref)


def inner_kernel(where_ref, mu_ref, spectrum_ref, table_ref, nu_ref, coupling_ref, energy_ref):
    sub, lane = iotas()
    coupling, energy = move(
        nu_ref, spectrum_ref, 0, table_ref, stretch_of(where_ref, table_ref), sub, lane,
        lambda i, q, jp: mu_ref[direction_rows(i, q, jp), :],
        lambda i: lambda q, jp: 0.0,
        lambda i, q, jp: 0.0,
    )
    coupling_ref[...] = coupling
    energy_ref[...] = energy


def last_kernel(
    where_ref, beta_hbm, nu_ref, spectrum_ref, table_ref, ice_ref, coupling_ref, energy_ref,
    on_in, off_in, lon_east_ref, lon_west_ref,
    out_hbm,
    beta_ref, north_ref, south_ref, add_ref, gain_ref, sems, out_sems,
):
    copies = fetch(sems, (beta_hbm, beta_ref))
    par = where_ref[0] % 2
    sub, lane = iotas()
    row = sub % LAT
    spread_rows(par, on_in, off_in, north_ref, south_ref)
    stretch = stretch_of(where_ref, table_ref)

    def gains(i, odd, coupling):
        x_speed, y_speed = speeds_of(table_ref, stretch, i)
        read = [spectrum_reader(spectrum_ref, i + QUAD * q, (odd + q) % 2) for q in range(4)]
        edge = turned_edges(lon_east_ref, lon_west_ref, i)
        for jp in range(PAIRS):
            for q, (north, east) in enumerate(QUADRANTS):
                along = jnp.where(lane == (LON - 1 if east else 0), edge(q, jp), 0.0)
                halo = row_halo_of(north_ref, south_ref, i, q, jp)
                across = jnp.where(row == (LAT - 1 if north else 0), halo, 0.0)
                gain = speed_of(table_ref, jp) * (x_speed[q % 2] * along + y_speed[q % 2] * across)
                gain_ref[direction_rows(i, q, jp), :] = gain
                coupling = coupling + read[q](jp) * gain
        return coupling

    gained = over_directions(gains, jnp.zeros((8, LON), F32))
    coupling = coupling_ref[...] + both_halves(gained)
    upper = sub >= LAT
    ice = ice_ref[...].astype(F32)
    rate = 1.0 - jnp.concatenate([ice, ice], axis=0)
    base = 1.0 - 0.2 * rate * energy_ref[...]
    set_weighted(table_ref, 0.2 * rate * coupling, add_ref)
    copies[0].wait()

    def chunk(g):
        rows = pl.ds(pl.multiple_of(g * 4 * BLOCK, 8), 4 * BLOCK)
        return pltpu.make_async_copy(gain_ref.at[rows], out_hbm.at[rows], out_sems.at[g])

    def body(g, carry):
        for jp in range(PAIRS):
            for h in range(4):
                beta = rate_of(beta_ref, 4 * g + h, jp, upper)
                place = pl.ds(pl.multiple_of((4 * g + h) * BLOCK + 8 * jp, 8), 8)
                x = (nu_ref[place, :] + gain_ref[place, :]) * (base + rate * beta)
                gain_ref[place, :] = x - add_ref[tab(jp), :]
        chunk(g).start()
        return carry

    lax.fori_loop(0, NDIR // 4, body, 0)
    for g in range(NDIR // 4):
        chunk(g).wait()


FIRST = 54


def params(limit=24):
    return pltpu.CompilerParams(vmem_limit_bytes=limit * MIB)


def f32(*shape):
    return jax.ShapeDtypeStruct(shape, F32)


def exchange(on, off, west, east):
    n_lon, n_lat = lax.axis_size("lon"), lax.axis_size("lat")
    near = [(i, i ^ 1) for i in range(n_lat)]
    far = [(i, ((i + 1) ^ 1) - 1) for i in range(1, n_lat - 1)]
    off = lax.ppermute(off, "lat", far)
    on = lax.ppermute(on, "lat", near)
    from_east = lax.ppermute(west, "lon", [(i, (i - 1) % n_lon) for i in range(n_lon)])
    from_west = lax.ppermute(east, "lon", [(i, (i + 1) % n_lon) for i in range(n_lon)])
    return on, off, from_east, from_west


def on_device(adj_final, saved, beta, sea_mask, ice_mask, obs_count, obs_cell, obs_value):
    table = jnp.asarray(constant_table())
    where = lax.axis_index("lat").astype(jnp.int32).reshape(1)
    adj = adj_final.reshape(ROWS, LON)
    saved = saved.reshape((STEPS + 1) * ROWS, LON)
    beta = beta.T
    tiles = lambda rows: pltpu.VMEM((rows, LON), F32)
    whole = lambda x: pltpu.VMEM(x.shape, x.dtype)
    level = pltpu.VMEM((ROWS, LON), jnp.bfloat16)
    payload = (f32(HALO, LON), f32(HALO, LON), f32(EDGE, LON), f32(EDGE, LON))
    dma = lambda *n: pltpu.SemaphoreType.DMA(n)

    on, off, west, east, obs, field, sea8, early = pl.pallas_call(
        start_kernel,
        out_shape=payload
        + (f32(128, 128), tiles(8), tiles(8))
        + (pltpu.VMEM((2 * ROWS, LON), jnp.bfloat16),),
        in_specs=[SMEM] + [HBM] * 7,
        out_specs=(VMEM,) * 8,
        scratch_shapes=[
            tiles(ROWS), level, tiles(BLOCK), whole(sea_mask), whole(obs_count), whole(obs_cell), whole(obs_value), dma(11),
        ],
        compiler_params=params(FIRST),
        name="edges_and_observations",
    )(where, adj, saved, table, sea_mask, obs_count, obs_cell, obs_value)

    on, off, from_east, from_west = exchange(on, off, west, east)
    obs = lax.all_to_all(obs.reshape(128, 1, 128), ("lon", "lat"), split_axis=0, concat_axis=0, tiled=True)
    obs = obs.reshape(128, 128)

    rates = pltpu.SMEM(beta.shape, F32)
    mu, on, off, west, east = pl.pallas_call(
        middle_kernel,
        out_shape=(f32(ROWS, LON),) + payload,
        in_specs=[SMEM, HBM] + [VMEM] * 11,
        out_specs=(VMEM,) * 5,
        scratch_shapes=[rates, tiles(SPREAD), tiles(SPREAD), tiles(16)] + [tiles(BLOCK)] * 5 + [dma(1)],
        compiler_params=params(),
        name="first_step",
    )(where, beta, adj, early, table, sea8, ice_mask, field, obs, on, off, from_east, from_west)

    on, off, from_east, from_west = exchange(on, off, west, east)

    nu, coupling, energy = pl.pallas_call(
        inner_kernel,
        out_shape=(f32(ROWS, LON), f32(8, LON), f32(8, LON)),
        in_specs=[SMEM] + [VMEM] * 3,
        out_specs=(VMEM,) * 3,
        compiler_params=params(),
        cost_estimate=pl.CostEstimate(flops=20_000_000, bytes_accessed=6_000_000, transcendentals=0),
        name="last_step_inside",
    )(where, mu, early, table)

    out = pl.pallas_call(
        last_kernel,
        out_shape=f32(ROWS, LON),
        in_specs=[SMEM, HBM] + [VMEM] * 10,
        out_specs=HBM,
        scratch_shapes=[rates, tiles(SPREAD), tiles(SPREAD), tiles(BLOCK), tiles(ROWS), dma(1), dma(NDIR // 4)],
        compiler_params=params(),
        name="last_step_edges",
    )(where, beta, nu, early, table, ice_mask, coupling, energy, on, off, from_east, from_west)
    return out.reshape(adj_final.shape)


def solution(mesh):
    return jax.shard_map(
        on_device,
        mesh=mesh,
        in_specs=(
            P(None, None, "lat", "lon"),
            P(None, None, None, "lat", "lon"),
            P(),
            P("lat", "lon"),
            P("lat", "lon"),
            P(("lon", "lat"), None),
            P(("lon", "lat"), None),
            P(("lon", "lat"), None),
        ),
        out_specs=P(None, None, "lat", "lon"),
        check_vma=False,
    )
```

time: 68.8 us -> 54.6 us (0.79)
  local copies, waits for them, and re-layouts: 10.9 us -> 1.63 us
  Pallas kernels: 19.3 us -> 15.6 us
    unnamed x27 -> x8, local copies, waits for them, and re-layouts: 10.9 us -> 1.63 us
    pallas_call x3 -> x4, Pallas kernels: 19.3 us -> 15.6 us  [the longest x1 5.8 us: on_device(): pl.pallas_call(middle_kernel, out_shape=(f32(ROWS, LON),) + payload, in_s...]
  transfers between devices with their start and end apart: 9 -> 9, of which waited for: 6 -> 6; matrix products, arithmetic and copies ran while one was open for 1% -> 0% of each run, Pallas kernels for 0% -> 2%
where the time goes in v1:
time: 54.6 us; the launch traced here: 54.4 us
  starting transfers between devices  25.4 us (47%)
  Pallas kernels  15.6 us (29%)
  waiting for transfers between devices  11.7 us (21%)
  local copies, waits for them, and re-layouts  1.63 us (3%)
    ppermute x2, starting transfers between devices, exchange(): off = lax.ppermute(off, 'lat', far)  8.89 us
    all_to_all x1, starting transfers between devices, on_device(): lax.all_to_all(obs.reshape(128, 1, 128), ('lon', 'lat'), split_axis=0, co...  8.87 us
    pallas_call x1, Pallas kernels, on_device(): pl.pallas_call(middle_kernel, out_shape=(f32(ROWS, LON),) + payload, in_s...  5.8 us
    ppermute x2, waiting for transfers between devices, exchange(): lax.ppermute(east, 'lon', [(i, (i + 1) % n_lon) for i in range(n_lon)])  5.57 us
    pallas_call x1, Pallas kernels, on_device(): pl.pallas_call(start_kernel, out_shape=payload + (f32(128, 128), tiles(8)...  4.99 us
    ppermute x2, starting transfers between devices, exchange(): lax.ppermute(west, 'lon', [(i, (i - 1) % n_lon) for i in range(n_lon)])  3.64 us
    ppermute x2, waiting for transfers between devices, exchange(): off = lax.ppermute(off, 'lat', far)  3.63 us
    pallas_call x1, Pallas kernels, on_device(): pl.pallas_call(last_kernel, out_shape=f32(ROWS, LON), in_specs=[SMEM, HBM...  3.47 us
  transfers between devices with their start and end apart: 9, of which 6 were waited for; matrix products, arithmetic and copies ran while one was open for 0% of the time, Pallas kernels for 2%

profile of v1, /device:TPU:1, one launch (start us, length us, event | category | flops | bytes accessed | tf_op | source)
XLA Modules:
  0.0 54.4 jit_solution(6936636530841267320)
XLA Ops:
  0.0 0.0 copy-start.1
  0.0 0.0 copy-start.2
  0.0 0.0 copy-start.3
  0.0 5.0 %edges_and_observations.1 = (f32[552,128]{1,0:T(8,128)}, f32[552,128]{1,0:T(8,128)}, f32[40,128]{1,0:T(8,128)}, f32[40,128]{1,0:T(8,128)}, f32[128,128]{1,0:T(8,...) custom-call(s32[1]{0:T(128)} %bitcast.where_ref, f32[4320,128]{1,0:T(8,128)} %bitcast.9, ...), custom_call_target="tpu_custom_call" | custom-call | tf_op jit(solution)/shard_map/edges_and_observations/pallas_call | solution.py:537
  5.0 1.5 %collective-permute-start = (f32[552,128]{1,0:T(8,128)}, f32[552,128]{1,0:T(8,128)S(1)}, u32[]{:S(2)}, u32[]{:S(2)}) collective-permute-start(f32[552,128]{1,0:T(8,128)} %get-tuple-element.25), channel_id=1, source_target_pairs={{0,1},{1,0},{2,3},{3,2},{4,5},{5,4},{6,7},{7,6},{8,9},{9,8},{10,11... | collective-permute-start | bytes 847880 | tf_op jit(solution)/shard_map/ppermute | solution.py:519
  6.5 4.8 %collective-permute-start.1 = (f32[552,128]{1,0:T(8,128)}, f32[552,128]{1,0:T(8,128)S(1)}, u32[]{:S(2)}, u32[]{:S(2)}) collective-permute-start(f32[552,128]{1,0:T(8,128)} %get-tuple-element.26), channel_id=1, source_target_pairs={{1,2},{2,1},{3,4},{4,3},{5,6},{6,5},{7,8},{8,7},{9,10},{10,9},{11,... | collective-permute-start | bytes 847880 | tf_op jit(solution)/shard_map/ppermute | solution.py:518
  11.3 8.9 %all-to-all-start = ((f32[128,1,128]{2,1,0:T(1,128)}), f32[128,1,128]{2,1,0:T(1,128)S(1)}, u32[]{:S(2)}, u32[]{:S(2)}) async-start(f32[128,1,128]{2,1,0:T(1,128)} %bitcast.15), calls=%async_computation | async-start | bytes 131072 | tf_op jit(solution)/shard_map/all_to_all | solution.py:552
  20.2 3.6 %collective-permute-start.2 = (f32[40,128]{1,0:T(8,128)}, f32[40,128]{1,0:T(8,128)S(1)}, u32[]{:S(2)}, u32[]{:S(2)}) collective-permute-start(f32[40,128]{1,0:T(8,128)} %get-tuple-element.27), channel_id=1, source_target_pairs={{0,112},{16,0},{32,16},{48,32},{64,48},{80,64},{96,80},{112,96},{1... | collective-permute-start | bytes 61448 | tf_op jit(solution)/shard_map/ppermute | solution.py:520
  23.8 0.0 collective-permute-start.3
  23.8 1.1 %collective-permute-done.2.lon_east_ref = f32[40,128]{1,0:T(8,128)S(1)} collective-permute-done((f32[40,128]{1,0:T(8,128)}, f32[40,128]{1,0:T(8,128)S(1)}, u32[]{:S(2)}, u32[]{:S(2)}) %collective-permute-start.2) | collective-permute-done | bytes 20512 | tf_op jit(solution)/shard_map/ppermute | solution.py:520
  24.9 4.1 %collective-permute-done.3.lon_west_ref = f32[40,128]{1,0:T(8,128)S(1)} collective-permute-done((f32[40,128]{1,0:T(8,128)}, f32[40,128]{1,0:T(8,128)S(1)}, u32[]{:S(2)}, u32[]{:S(2)}) %collective-permute-start.3) | collective-permute-done | bytes 20512 | tf_op jit(solution)/shard_map/ppermute | solution.py:521
  29.0 0.8 %all-to-all-done = f32[128,1,128]{2,1,0:T(1,128)S(1)} async-done(((f32[128,1,128]{2,1,0:T(1,128)}), f32[128,1,128]{2,1,0:T(1,128)S(1)}, u32[]{:S(2)}, u32[]{:S(2)}) %all-to-all-start) | async-done | bytes 65568 | tf_op jit(solution)/shard_map/all_to_all | solution.py:552
  29.8 0.0 collective-permute-done.on_in
  29.8 0.0 collective-permute-done.1.off_in
  29.8 0.0 copy-done.1
  29.8 0.0 copy-done.2
  29.8 0.0 copy-done.3
  29.8 0.0 copy-start
  29.8 1.6 %copy-done = f32[36,30,4,128]{3,2,1,0:T(4,128)S(1)} copy-done((f32[36,30,4,128]{3,2,1,0:T(4,128)S(1)}, f32[36,30,4,128]{3,2,1,0:T(4,128)}, u32[]{:S(2)}) %copy-start) | copy-done | bytes 2211864
  31.5 5.8 %first_step.1 = (f32[4320,128]{1,0:T(8,128)S(1)}, f32[552,128]{1,0:T(8,128)S(1)}, f32[552,128]{1,0:T(8,128)S(1)}, f32[40,128]{1,0:T(8,128)S(1)}, f32[40,128]{1,0:T(8,128)S(1)}) custom-call(s32[1]{0:T(128)} %bitcast.where_ref, f32[30,36]{1,0:T(8,128)S(1)} %bitcast.12, f32[4320,128]{1,0:T(8,128)S(1)} %bitcast.10, ...), custom_call_target="tpu_custom_call" | custom-call | tf_op jit(solution)/shard_map/first_step/pallas_call | solution.py:556
  37.3 1.0 %collective-permute-start.4 = (f32[552,128]{1,0:T(8,128)S(1)}, f32[552,128]{1,0:T(8,128)S(1)}, u32[]{:S(2)}, u32[]{:S(2)}) collective-permute-start(f32[552,128]{1,0:T(8,128)S(1)} %get-tuple-element.33), channel_id=1, source_target_pairs={{0,1},{1,0},{2,3},{3,2},{4,5},{5,4},{6,7},{7,6},{8,9},{9,8},{10,11... | collective-permute-start | bytes 847880 | tf_op jit(solution)/shard_map/ppermute | solution.py:519
  38.3 4.1 %collective-permute-start.5 = (f32[552,128]{1,0:T(8,128)S(1)}, f32[552,128]{1,0:T(8,128)S(1)}, u32[]{:S(2)}, u32[]{:S(2)}) collective-permute-start(f32[552,128]{1,0:T(8,128)S(1)} %get-tuple-element.34), channel_id=1, source_target_pairs={{1,2},{2,1},{3,4},{4,3},{5,6},{6,5},{7,8},{8,7},{9,10},{10,9},{11,... | collective-permute-start | bytes 847880 | tf_op jit(solution)/shard_map/ppermute | solution.py:518
  42.4 0.1 collective-permute-start.6
  42.5 1.5 %collective-permute-start.7 = (f32[40,128]{1,0:T(8,128)S(1)}, f32[40,128]{1,0:T(8,128)S(1)}, u32[]{:S(2)}, u32[]{:S(2)}) collective-permute-start(f32[40,128]{1,0:T(8,128)S(1)} %get-tuple-element.36), channel_id=1, source_target_pairs={{0,16},{16,32},{32,48},{48,64},{64,80},{80,96},{96,112},{112,0},{1... | collective-permute-start | bytes 61448 | tf_op jit(solution)/shard_map/ppermute | solution.py:521
  43.9 1.3 %last_step_inside.1 = (f32[4320,128]{1,0:T(8,128)S(1)}, f32[8,128]{1,0:T(8,128)S(1)}, f32[8,128]{1,0:T(8,128)S(1)}) custom-call(s32[1]{0:T(128)} %bitcast.where_ref, f32[4320,128]{1,0:T(8,128)S(1)} %get-tuple-element.29.mu_ref, bf16[8640,128]{1,0:T(8,128)(2,1)S(1)} %get-tuple-element.21.spectrum_ref, f32[512,128]{1,0:T(8,128)S(1)} %copy-done.1), custom_call_target="tpu_custom_call" | custom-call | flops 20000000 | bytes 6000000 | tf_op jit(solution)/shard_map/last_step_inside/pallas_call | solution.py:568
  45.2 0.6 %collective-permute-done.6.lon_east_ref = f32[40,128]{1,0:T(8,128)S(1)} collective-permute-done((f32[40,128]{1,0:T(8,128)S(1)}, f32[40,128]{1,0:T(8,128)S(1)}, u32[]{:S(2)}, u32[]{:S(2)}) %collective-permute-start.6) | collective-permute-done | bytes 20512 | tf_op jit(solution)/shard_map/ppermute | solution.py:520
  45.8 1.4 %collective-permute-done.7.lon_west_ref = f32[40,128]{1,0:T(8,128)S(1)} collective-permute-done((f32[40,128]{1,0:T(8,128)S(1)}, f32[40,128]{1,0:T(8,128)S(1)}, u32[]{:S(2)}, u32[]{:S(2)}) %collective-permute-start.7) | collective-permute-done | bytes 20512 | tf_op jit(solution)/shard_map/ppermute | solution.py:521
  47.3 0.0 collective-permute-done.4.on_in
  47.3 3.6 %collective-permute-done.5.off_in = f32[552,128]{1,0:T(8,128)S(1)} collective-permute-done((f32[552,128]{1,0:T(8,128)S(1)}, f32[552,128]{1,0:T(8,128)S(1)}, u32[]{:S(2)}, u32[]{:S(2)}) %collective-permute-start.5) | collective-permute-done | bytes 282656 | tf_op jit(solution)/shard_map/ppermute | solution.py:518
  50.9 3.5 %last_step_edges.1 = f32[4320,128]{1,0:T(8,128)} custom-call(s32[1]{0:T(128)} %bitcast.where_ref, f32[30,36]{1,0:T(8,128)S(1)} %bitcast.13, f32[4320,128]{1,0:T(8,128)S(1)} %get-tuple-element.30.nu_ref, bf16[8640,128]{1,0:T(8,128)(2,1)S(1)} %get-tuple-element.21.spectrum_ref, f32[512,128]{1,0:T(8,128)S(1)} %copy-done.1, s32[4,128]{1,0:T(4,128)S(1)} %copy-done.3, ...), custom_call_target="tpu_custom_call" | custom-call | tf_op jit(solution)/shard_map/last_step_edges/pallas_call | solution.py:578
Async XLA Ops:
  0.0 29.8 %copy-start.1 = (f32[512,128]{1,0:T(8,128)S(1)}, f32[512,128]{1,0:T(8,128)}, u32[]{:S(2)}) copy-start(f32[512,128]{1,0:T(8,128)} %constant.6.clone.table_hbm.table_ref) | copy-start | bytes 786436
  0.0 29.8 %copy-start.2 = (f32[36,30]{0,1:T(8,128)S(1)}, f32[36,30]{0,1:T(8,128)}, u32[]{:S(2)}) copy-start(f32[36,30]{0,1:T(8,128)} %param.11) | copy-start | bytes 12964
  0.0 29.8 %copy-start.3 = (s32[4,128]{1,0:T(4,128)S(1)}, s32[4,128]{1,0:T(4,128)}, u32[]{:S(2)}) copy-start(s32[4,128]{1,0:T(4,128)} %ice_ref.3) | copy-start | bytes 6148
  5.0 24.8 %collective-permute-start = (f32[552,128]{1,0:T(8,128)}, f32[552,128]{1,0:T(8,128)S(1)}, u32[]{:S(2)}, u32[]{:S(2)}) collective-permute-start(f32[552,128]{1,0:T(8,128)} %get-tuple-element.25), channel_id=1, source_target_pairs={{0,1},{1,0},{2,3},{3,2},{4,5},{5,4},{6,7},{7,6},{8,9},{9,8},{10,11... | collective-permute-start | bytes 847880 | tf_op jit(solution)/shard_map/ppermute | solution.py:519
  6.5 23.3 %collective-permute-start.1 = (f32[552,128]{1,0:T(8,128)}, f32[552,128]{1,0:T(8,128)S(1)}, u32[]{:S(2)}, u32[]{:S(2)}) collective-permute-start(f32[552,128]{1,0:T(8,128)} %get-tuple-element.26), channel_id=1, source_target_pairs={{1,2},{2,1},{3,4},{4,3},{5,6},{6,5},{7,8},{8,7},{9,10},{10,9},{11,... | collective-permute-start | bytes 847880 | tf_op jit(solution)/shard_map/ppermute | solution.py:518
  11.3 18.5 %all-to-all-start = ((f32[128,1,128]{2,1,0:T(1,128)}), f32[128,1,128]{2,1,0:T(1,128)S(1)}, u32[]{:S(2)}, u32[]{:S(2)}) async-start(f32[128,1,128]{2,1,0:T(1,128)} %bitcast.15), calls=%async_computation | async-start | bytes 131072 | tf_op jit(solution)/shard_map/all_to_all | solution.py:552
  20.2 4.7 %collective-permute-start.2 = (f32[40,128]{1,0:T(8,128)}, f32[40,128]{1,0:T(8,128)S(1)}, u32[]{:S(2)}, u32[]{:S(2)}) collective-permute-start(f32[40,128]{1,0:T(8,128)} %get-tuple-element.27), channel_id=1, source_target_pairs={{0,112},{16,0},{32,16},{48,32},{64,48},{80,64},{96,80},{112,96},{1... | collective-permute-start | bytes 61448 | tf_op jit(solution)/shard_map/ppermute | solution.py:520
  23.8 5.2 %collective-permute-start.3 = (f32[40,128]{1,0:T(8,128)}, f32[40,128]{1,0:T(8,128)S(1)}, u32[]{:S(2)}, u32[]{:S(2)}) collective-permute-start(f32[40,128]{1,0:T(8,128)} %get-tuple-element.28), channel_id=1, source_target_pairs={{0,16},{16,32},{32,48},{48,64},{64,80},{80,96},{96,112},{112,0},{1... | collective-permute-start | bytes 61448 | tf_op jit(solution)/shard_map/ppermute | solution.py:521
  29.8 1.6 %copy-start = (f32[36,30,4,128]{3,2,1,0:T(4,128)S(1)}, f32[36,30,4,128]{3,2,1,0:T(4,128)}, u32[]{:S(2)}) copy-start(f32[36,30,4,128]{3,2,1,0:T(4,128)} %param.9) | copy-start | bytes 6635524
  37.3 10.0 %collective-permute-start.4 = (f32[552,128]{1,0:T(8,128)S(1)}, f32[552,128]{1,0:T(8,128)S(1)}, u32[]{:S(2)}, u32[]{:S(2)}) collective-permute-start(f32[552,128]{1,0:T(8,128)S(1)} %get-tuple-element.33), channel_id=1, source_target_pairs={{0,1},{1,0},{2,3},{3,2},{4,5},{5,4},{6,7},{7,6},{8,9},{9,8},{10,11... | collective-permute-start | bytes 847880 | tf_op jit(solution)/shard_map/ppermute | solution.py:519
  38.3 12.6 %collective-permute-start.5 = (f32[552,128]{1,0:T(8,128)S(1)}, f32[552,128]{1,0:T(8,128)S(1)}, u32[]{:S(2)}, u32[]{:S(2)}) collective-permute-start(f32[552,128]{1,0:T(8,128)S(1)} %get-tuple-element.34), channel_id=1, source_target_pairs={{1,2},{2,1},{3,4},{4,3},{5,6},{6,5},{7,8},{8,7},{9,10},{10,9},{11,... | collective-permute-start | bytes 847880 | tf_op jit(solution)/shard_map/ppermute | solution.py:518
  42.4 3.5 %collective-permute-start.6 = (f32[40,128]{1,0:T(8,128)S(1)}, f32[40,128]{1,0:T(8,128)S(1)}, u32[]{:S(2)}, u32[]{:S(2)}) collective-permute-start(f32[40,128]{1,0:T(8,128)S(1)} %get-tuple-element.35), channel_id=1, source_target_pairs={{0,112},{16,0},{32,16},{48,32},{64,48},{80,64},{96,80},{112,96},{1... | collective-permute-start | bytes 61448 | tf_op jit(solution)/shard_map/ppermute | solution.py:520
  42.5 4.8 %collective-permute-start.7 = (f32[40,128]{1,0:T(8,128)S(1)}, f32[40,128]{1,0:T(8,128)S(1)}, u32[]{:S(2)}, u32[]{:S(2)}) collective-permute-start(f32[40,128]{1,0:T(8,128)S(1)} %get-tuple-element.36), channel_id=1, source_target_pairs={{0,16},{16,32},{32,48},{48,64},{64,80},{80,96},{96,112},{112,0},{1... | collective-permute-start | bytes 61448 | tf_op jit(solution)/shard_map/ppermute | solution.py:521

commit v2 on v1

--- a/solution.py
+++ b/solution.py
@@ -1,3 +1,4 @@
+import functools
 import math
 
 import jax
@@ -353,62 +354,119 @@
     return jnp.where(upper, beta_ref[2 * jp + 1, k], beta_ref[2 * jp, k])
 
 
+def edge_gains(
+    spectrum_ref, level, table_ref, stretch, lon_east_ref, lon_west_ref, north_ref, south_ref,
+    sub, lane, extra_of, keep,
+):
+    row = sub % LAT
+
+    def body(i, odd, coupling):
+        x_speed, y_speed = speeds_of(table_ref, stretch, i)
+        read = [spectrum_reader(spectrum_ref, i + QUAD * q, (odd + q) % 2, level) for q in range(4)]
+        edge = turned_edges(lon_east_ref, lon_west_ref, i)
+        extra = [extra_of(q, x_speed[q % 2], y_speed[q % 2]) for q in range(4)]
+        for jp in range(PAIRS):
+            for q, (north, east) in enumerate(QUADRANTS):
+                along = jnp.where(lane == (LON - 1 if east else 0), edge(q, jp), 0.0)
+                halo = row_halo_of(north_ref, south_ref, i, q, jp)
+                across = jnp.where(row == (LAT - 1 if north else 0), halo, 0.0)
+                gain = speed_of(table_ref, jp) * (x_speed[q % 2] * along + y_speed[q % 2] * across)
+                gain = keep(direction_rows(i, q, jp), jp, gain, extra[q])
+                coupling = coupling + read[q](jp) * gain
+        return coupling
+
+    return both_halves(over_directions(body, jnp.zeros((8, LON), F32)))
+
+
+def three_parts(x):
+    parts = []
+    for _ in range(3):
+        part = x.astype(jnp.bfloat16)
+        parts.append(part)
+        x = x - part.astype(F32)
+    return jnp.concatenate(parts, axis=0)
+
+
 def sum_observations(obs_ref, sub, lane):
-    wide = lax.broadcasted_iota(jnp.int32, (128, 128), 1).astype(F32)
-    own = [jnp.zeros((128, 128), F32) for _ in range(LAT)]
-    beside = [jnp.zeros((128, 128), F32) for _ in range(4)]
-    for i in range(CAP):
-        index = obs_ref[:, i : i + 1]
-        value = obs_ref[:, CAP + i : CAP + i + 1]
-        for r in range(LAT):
-            own[r] = own[r] + jnp.where(index == wide + float(r * LON), value, 0.0)
-        for place, target in enumerate(
-            (wide, wide + float((LAT - 1) * LON), wide * LON, wide * LON + (LON - 1.0))
-        ):
-            index = obs_ref[:, 8 * place + 8 + i : 8 * place + 9 + i]
-            value = obs_ref[:, 8 * place + 8 + CAP + i : 8 * place + 9 + CAP + i]
-            beside[place] = beside[place] + jnp.where(index == target, value, 0.0)
-    force = jnp.zeros((8, LON), F32)
-    for r in range(LAT):
-        force = jnp.where(sub % LAT == r, jnp.sum(own[r], axis=0, keepdims=True), force)
-    lines = [jnp.sum(b, axis=0, keepdims=True) for b in beside]
-    force_n, force_s = lines[0], lines[1]
-    force_e, force_w = (
-        jnp.sum(jnp.where(lane == sub % LAT, line, 0.0), axis=1, keepdims=True) for line in lines[2:]
-    )
-    return force, force_n, force_s, force_e, force_w
+    listed = jnp.transpose(obs_ref[...])
+    column = lax.broadcasted_iota(jnp.int32, (128, 128), 0).astype(F32)
+    row8 = (sub % LAT).astype(F32)
+
+    def slots(tile):
+        for i in range(CAP):
+            index = listed[8 * tile + i : 8 * tile + i + 1, :]
+            value = listed[8 * tile + CAP + i : 8 * tile + CAP + i + 1, :]
+            row = jnp.floor(index * (1.0 / LON))
+            yield row, index - row * LON, value
+
+    def spread(tile, takes):
+        left, right = [], []
+        for row, col, value in slots(tile):
+            left.append(jnp.where(takes(row), value, jnp.zeros((8, LON), F32)))
+            right.append(jnp.where(column == col, 1.0, 0.0).astype(jnp.bfloat16))
+        parts = three_parts(jnp.concatenate(left, axis=1))
+        out = lax.dot_general(
+            parts, jnp.concatenate(right, axis=1), (((1,), (1,)), ((), ())), preferred_element_type=F32
+        )
+        return out[0:8, :] + out[8:16, :] + out[16:24, :]
+
+    def line(tile, at):
+        total = jnp.zeros((8, LON), F32)
+        for row, col, value in slots(tile):
+            total = total + jnp.where((row8 == row) & (col == at), value, 0.0)
+        return jnp.sum(total, axis=1, keepdims=True)
+
+    own = spread(0, lambda row: row8 == row)
+    north = spread(1, lambda row: row8 * 0.0 == row)
+    south = spread(2, lambda row: row8 * 0.0 + (LAT - 1.0) == row)
+    return own, north, south, line(3, 0.0), line(4, LON - 1.0)
 
 
 def middle_kernel(
-    where_ref, beta_hbm, adj_ref, spectrum_ref, table_ref, sea8_ref, ice_ref, field_ref,
-    obs_ref, on_in, off_in, lon_east_ref, lon_west_ref,
+    where_ref, beta_hbm, nu_ref, spectrum_ref, table_ref, sea8_ref, ice_ref, field_ref,
+    coupling_ref, energy_ref, obs_ref, on_in, off_in, lon_east_ref, lon_west_ref,
     mu_ref, on_ref, off_ref, west_ref, east_ref,
-    beta_ref, north_ref, south_ref, fields_ref, add_ref, add_n, add_s, add_e, add_w, sems,
+    beta_ref, north_ref, south_ref, fields_ref, add_ref, sems,
 ):
     copies = fetch(sems, (beta_hbm, beta_ref))
     par = where_ref[0] % 2
     sub, lane = iotas()
+    row = sub % LAT
     sea8 = sea8_ref[...]
     stretch = stretch_of(where_ref, table_ref)
     force, force_n, force_s, force_e, force_w = sum_observations(obs_ref, sub, lane)
     spread_rows(par, on_in, off_in, north_ref, south_ref, fields_ref)
-    set_weighted(table_ref, force * field_ref[...], add_ref)
-    set_weighted(table_ref, force_n * fields_ref[0:8, :], add_n)
-    set_weighted(table_ref, force_s * fields_ref[8:16, :], add_s)
-    set_weighted(table_ref, force_e * lon_east_ref[32:40, :], add_e)
-    set_weighted(table_ref, force_w * lon_west_ref[32:40, :], add_w)
-
-    def lon_of(i):
-        edge = turned_edges(lon_east_ref, lon_west_ref, i)
-        return lambda q, jp: edge(q, jp) + (add_e if QUADRANTS[q][1] else add_w)[tab(jp), :]
-
-    coupling, energy = move(
-        mu_ref, spectrum_ref, 1, table_ref, stretch, sub, lane,
-        lambda i, q, jp: adj_ref[direction_rows(i, q, jp), :] * sea8 + add_ref[tab(jp), :],
-        lon_of,
-        lambda i, q, jp: row_halo_of(north_ref, south_ref, i, q, jp)
-        + (add_n if QUADRANTS[q][0] else add_s)[tab(jp), :],
+
+    own = force * field_ref[...]
+    set_weighted(table_ref, own, add_ref)
+    first_weight = table_ref[WEIGHT0 : WEIGHT0 + 1, :]
+    along_of, across_of = {}, {}
+    for east, halo, ref in ((True, force_e, lon_east_ref), (False, force_w, lon_west_ref)):
+        beside = halo * ref[32:40, :]
+        turned = pltpu.roll(own, LON - 1 if east else 1, axis=1)
+        here = jnp.where(lane == (LON - 1 if east else 0), beside, turned)
+        along_of[east] = first_weight * (here - own)
+    for north, halo, place in ((True, force_n, 0), (False, force_s, 8)):
+        beside = halo * fields_ref[place : place + 8, :]
+        shifted = pltpu.roll(own, 7 if north else 1, axis=0)
+        here = jnp.where(row == (LAT - 1 if north else 0), beside, shifted)
+        across_of[north] = first_weight * (here - own)
+
+    def extra_of(q, x_speed, y_speed):
+        north, east = QUADRANTS[q]
+        return x_speed * along_of[east] + y_speed * across_of[north]
+
+    def keep(place, jp, gain, extra):
+        gain = gain + (add_ref[tab(jp), :] + extra)
+        mu_ref[place, :] = nu_ref[place, :] + gain
+        return gain
+
+    gained = edge_gains(
+        spectrum_ref, 1, table_ref, stretch, lon_east_ref, lon_west_ref, north_ref, south_ref,
+        sub, lane, extra_of, keep,
     )
+    coupling = coupling_ref[...] + gained
+    energy = energy_ref[...]
     upper = sub >= LAT
     ice = ice_ref[...].astype(F32)
     rate = sea8 * (1.0 - jnp.concatenate([ice, ice], axis=0))
@@ -433,13 +491,18 @@
     send_rows(par, mu_ref, on_ref, off_ref)
 
 
-def inner_kernel(where_ref, mu_ref, spectrum_ref, table_ref, nu_ref, coupling_ref, energy_ref):
+def inner_kernel(level, where_ref, mu_ref, spectrum_ref, table_ref, *rest):
     sub, lane = iotas()
+    nu_ref, coupling_ref, energy_ref = rest[-3:]
+    sea8 = rest[0][...] if len(rest) == 4 else None
+
+    def value_of(i, q, jp):
+        mu = mu_ref[direction_rows(i, q, jp), :]
+        return mu if sea8 is None else mu * sea8
+
     coupling, energy = move(
-        nu_ref, spectrum_ref, 0, table_ref, stretch_of(where_ref, table_ref), sub, lane,
-        lambda i, q, jp: mu_ref[direction_rows(i, q, jp), :],
-        lambda i: lambda q, jp: 0.0,
-        lambda i, q, jp: 0.0,
+        nu_ref, spectrum_ref, level, table_ref, stretch_of(where_ref, table_ref), sub, lane,
+        value_of, lambda i: lambda q, jp: 0.0, lambda i, q, jp: 0.0,
     )
     coupling_ref[...] = coupling
     energy_ref[...] = energy
@@ -458,22 +521,15 @@
     spread_rows(par, on_in, off_in, north_ref, south_ref)
     stretch = stretch_of(where_ref, table_ref)
 
-    def gains(i, odd, coupling):
-        x_speed, y_speed = speeds_of(table_ref, stretch, i)
-        read = [spectrum_reader(spectrum_ref, i + QUAD * q, (odd + q) % 2) for q in range(4)]
-        edge = turned_edges(lon_east_ref, lon_west_ref, i)
-        for jp in range(PAIRS):
-            for q, (north, east) in enumerate(QUADRANTS):
-                along = jnp.where(lane == (LON - 1 if east else 0), edge(q, jp), 0.0)
-                halo = row_halo_of(north_ref, south_ref, i, q, jp)
-                across = jnp.where(row == (LAT - 1 if north else 0), halo, 0.0)
-                gain = speed_of(table_ref, jp) * (x_speed[q % 2] * along + y_speed[q % 2] * across)
-                gain_ref[direction_rows(i, q, jp), :] = gain
-                coupling = coupling + read[q](jp) * gain
-        return coupling
-
-    gained = over_directions(gains, jnp.zeros((8, LON), F32))
-    coupling = coupling_ref[...] + both_halves(gained)
+    def keep(place, jp, gain, extra):
+        gain_ref[place, :] = gain
+        return gain
+
+    gained = edge_gains(
+        spectrum_ref, 0, table_ref, stretch, lon_east_ref, lon_west_ref, north_ref, south_ref,
+        sub, lane, lambda q, x_speed, y_speed: None, keep,
+    )
+    coupling = coupling_ref[...] + gained
     upper = sub >= LAT
     ice = ice_ref[...].astype(F32)
     rate = 1.0 - jnp.concatenate([ice, ice], axis=0)
@@ -553,28 +609,35 @@
     obs = obs.reshape(128, 128)
 
     rates = pltpu.SMEM(beta.shape, F32)
+
+    def inside(level, name, *operands):
+        return pl.pallas_call(
+            functools.partial(inner_kernel, level),
+            out_shape=(f32(ROWS, LON), f32(8, LON), f32(8, LON)),
+            in_specs=[SMEM] + [VMEM] * len(operands),
+            out_specs=(VMEM,) * 3,
+            compiler_params=params(),
+            cost_estimate=pl.CostEstimate(flops=20_000_000, bytes_accessed=6_000_000, transcendentals=0),
+            name=name,
+        )(where, *operands)
+
+    nu, coupling, energy = inside(1, "first_step_inside", adj, early, table, sea8)
     mu, on, off, west, east = pl.pallas_call(
         middle_kernel,
         out_shape=(f32(ROWS, LON),) + payload,
-        in_specs=[SMEM, HBM] + [VMEM] * 11,
+        in_specs=[SMEM, HBM] + [VMEM] * 13,
         out_specs=(VMEM,) * 5,
-        scratch_shapes=[rates, tiles(SPREAD), tiles(SPREAD), tiles(16)] + [tiles(BLOCK)] * 5 + [dma(1)],
+        scratch_shapes=[rates, tiles(SPREAD), tiles(SPREAD), tiles(16), tiles(BLOCK), dma(1)],
         compiler_params=params(),
-        name="first_step",
-    )(where, beta, adj, early, table, sea8, ice_mask, field, obs, on, off, from_east, from_west)
+        name="first_step_edges",
+    )(
+        where, beta, nu, early, table, sea8, ice_mask, field, coupling, energy, obs, on, off,
+        from_east, from_west,
+    )
 
     on, off, from_east, from_west = exchange(on, off, west, east)
 
-    nu, coupling, energy = pl.pallas_call(
-        inner_kernel,
-        out_shape=(f32(ROWS, LON), f32(8, LON), f32(8, LON)),
-        in_specs=[SMEM] + [VMEM] * 3,
-        out_specs=(VMEM,) * 3,
-        compiler_params=params(),
-        cost_estimate=pl.CostEstimate(flops=20_000_000, bytes_accessed=6_000_000, transcendentals=0),
-        name="last_step_inside",
-    )(where, mu, early, table)
-
+    nu, coupling, energy = inside(0, "last_step_inside", mu, early, table)
     out = pl.pallas_call(
         last_kernel,
         out_shape=f32(ROWS, LON),

time: 54.6 us -> 53.4 us (0.978)
  waiting for transfers between devices: 11.7 us -> 7.34 us
  local copies, waits for them, and re-layouts: 1.63 us -> 4.6 us
    unnamed x8 -> x12, local copies, waits for them, and re-layouts: 1.63 us -> 4.6 us
    ppermute x2, waiting for transfers between devices: 5.57 us -> 3.69 us  [exchange(): lax.ppermute(east, 'lon', [(i, (i + 1) % n_lon) for i in range(n_lon)])]
    ppermute x2, starting transfers between devices: 3.64 us -> 5.12 us  [exchange(): lax.ppermute(west, 'lon', [(i, (i - 1) % n_lon) for i in range(n_lon)])]
    ppermute x2, starting transfers between devices: 1.46 us -> 0.01 us  [exchange(): lax.ppermute(east, 'lon', [(i, (i + 1) % n_lon) for i in range(n_lon)])]
    ppermute x2, waiting for transfers between devices: 3.63 us -> 2.23 us  [exchange(): off = lax.ppermute(off, 'lat', far)]
    pallas_call x1 -> x2, Pallas kernels: 1.31 us -> 2.67 us  [inside(): pl.pallas_call(functools.partial(inner_kernel, level), out_shape=(f32(ROW...]
    pallas_call x1, Pallas kernels: 5.8 us -> 4.63 us  [on_device(): pl.pallas_call(middle_kernel, out_shape=(f32(ROWS, LON),) + payload, in_s...]
    ppermute x2, waiting for transfers between devices: 1.72 us -> 0.63 us  [exchange(): lax.ppermute(west, 'lon', [(i, (i - 1) % n_lon) for i in range(n_lon)])]
  transfers between devices with their start and end apart: 9 -> 9, of which waited for: 6 -> 5; matrix products, arithmetic and copies ran while one was open for 0% -> 0% of each run, Pallas kernels for 2% -> 5%
where the time goes in v2:
time: 53.4 us; the launch traced here: 53.2 us
  starting transfers between devices  25.4 us (48%)
  Pallas kernels  15.8 us (30%)
  waiting for transfers between devices  7.34 us (14%)
  local copies, waits for them, and re-layouts  4.6 us (9%)
    ppermute x2, starting transfers between devices, exchange(): off = lax.ppermute(off, 'lat', far)  8.89 us
    all_to_all x1, starting transfers between devices, on_device(): lax.all_to_all(obs.reshape(128, 1, 128), ('lon', 'lat'), split_axis=0, co...  8.87 us
    ppermute x2, starting transfers between devices, exchange(): lax.ppermute(west, 'lon', [(i, (i - 1) % n_lon) for i in range(n_lon)])  5.12 us
    pallas_call x1, Pallas kernels, on_device(): pl.pallas_call(start_kernel, out_shape=payload + (f32(128, 128), tiles(8)...  5.02 us
    pallas_call x1, Pallas kernels, on_device(): pl.pallas_call(middle_kernel, out_shape=(f32(ROWS, LON),) + payload, in_s...  4.63 us
    unnamed x12, local copies, waits for them, and re-layouts  4.6 us
    ppermute x2, waiting for transfers between devices, exchange(): lax.ppermute(east, 'lon', [(i, (i + 1) % n_lon) for i in range(n_lon)])  3.69 us
    pallas_call x1, Pallas kernels, on_device(): pl.pallas_call(last_kernel, out_shape=f32(ROWS, LON), in_specs=[SMEM, HBM...  3.46 us
  transfers between devices with their start and end apart: 9, of which 5 were waited for; matrix products, arithmetic and copies ran while one was open for 0% of the time, Pallas kernels for 5%

profile of v2, /device:TPU:1, one launch (start us, length us, event | category | flops | bytes accessed | tf_op | source)
XLA Modules:
  0.0 53.2 jit_solution(1988960647283733601)
XLA Ops:
  0.0 0.0 copy-start.1
  0.0 5.0 %edges_and_observations.1 = (f32[552,128]{1,0:T(8,128)}, f32[552,128]{1,0:T(8,128)}, f32[40,128]{1,0:T(8,128)}, f32[40,128]{1,0:T(8,128)}, f32[128,128]{1,0:T(8,...) custom-call(s32[1]{0:T(128)} %bitcast.where_ref, f32[4320,128]{1,0:T(8,128)} %bitcast.9, ...), custom_call_target="tpu_custom_call" | custom-call | tf_op jit(solution)/shard_map/edges_and_observations/pallas_call | solution.py:593
  5.0 1.5 %collective-permute-start = (f32[552,128]{1,0:T(8,128)}, f32[552,128]{1,0:T(8,128)S(1)}, u32[]{:S(2)}, u32[]{:S(2)}) collective-permute-start(f32[552,128]{1,0:T(8,128)} %get-tuple-element.31), channel_id=1, source_target_pairs={{0,1},{1,0},{2,3},{3,2},{4,5},{5,4},{6,7},{7,6},{8,9},{9,8},{10,11... | collective-permute-start | bytes 847880 | tf_op jit(solution)/shard_map/ppermute | solution.py:575
  6.5 4.8 %collective-permute-start.1 = (f32[552,128]{1,0:T(8,128)}, f32[552,128]{1,0:T(8,128)S(1)}, u32[]{:S(2)}, u32[]{:S(2)}) collective-permute-start(f32[552,128]{1,0:T(8,128)} %get-tuple-element.32), channel_id=1, source_target_pairs={{1,2},{2,1},{3,4},{4,3},{5,6},{6,5},{7,8},{8,7},{9,10},{10,9},{11,... | collective-permute-start | bytes 847880 | tf_op jit(solution)/shard_map/ppermute | solution.py:574
  11.3 8.9 %all-to-all-start = ((f32[128,1,128]{2,1,0:T(1,128)}), f32[128,1,128]{2,1,0:T(1,128)S(1)}, u32[]{:S(2)}, u32[]{:S(2)}) async-start(f32[128,1,128]{2,1,0:T(1,128)} %bitcast.15), calls=%async_computation | async-start | bytes 131072 | tf_op jit(solution)/shard_map/all_to_all | solution.py:608
  20.2 3.6 %collective-permute-start.2 = (f32[40,128]{1,0:T(8,128)}, f32[40,128]{1,0:T(8,128)S(1)}, u32[]{:S(2)}, u32[]{:S(2)}) collective-permute-start(f32[40,128]{1,0:T(8,128)} %get-tuple-element.33), channel_id=1, source_target_pairs={{0,112},{16,0},{32,16},{48,32},{64,48},{80,64},{96,80},{112,96},{1... | collective-permute-start | bytes 61448 | tf_op jit(solution)/shard_map/ppermute | solution.py:576
  23.8 0.0 collective-permute-start.3
  23.8 0.0 copy-done.1
  23.8 1.6 %copy-done = f32[36,30,4,128]{3,2,1,0:T(4,128)S(1)} copy-done((f32[36,30,4,128]{3,2,1,0:T(4,128)S(1)}, f32[36,30,4,128]{3,2,1,0:T(4,128)}, u32[]{:S(2)}) %copy-start) | copy-done | bytes 2211864
  25.4 1.3 %first_step_inside.1 = (f32[4320,128]{1,0:T(8,128)S(1)}, f32[8,128]{1,0:T(8,128)S(1)}, f32[8,128]{1,0:T(8,128)S(1)}) custom-call(s32[1]{0:T(128)} %bitcast.where_ref, f32[4320,128]{1,0:T(8,128)S(1)} %bitcast.10, bf16[8640,128]{1,0:T(8,128)(2,1)S(1)} %get-tuple-element.24.spectrum_ref, f32[512,128]{1,0:T(8,128)S(1)} %copy-done.1, ...), custom_call_target="tpu_custom_call" | custom-call | flops 20000000 | bytes 6000000 | tf_op jit(solution)/shard_map/first_step_inside/pallas_call | solution.py:614
  26.8 0.0 copy-start.2
  26.8 1.3 %copy-done.2 = f32[4320,128]{1,0:T(8,128)} copy-done((f32[4320,128]{1,0:T(8,128)}, f32[4320,128]{1,0:T(8,128)S(1)}, u32[]{:S(2)}) %copy-start.2) | copy-done | bytes 2211864
  28.1 0.0 collective-permute-done.2.lon_east_ref
  28.1 0.9 %collective-permute-done.3.lon_west_ref = f32[40,128]{1,0:T(8,128)S(1)} collective-permute-done((f32[40,128]{1,0:T(8,128)}, f32[40,128]{1,0:T(8,128)S(1)}, u32[]{:S(2)}, u32[]{:S(2)}) %collective-permute-start.3) | collective-permute-done | bytes 20512 | tf_op jit(solution)/shard_map/ppermute | solution.py:577
  29.0 0.8 %all-to-all-done = f32[128,1,128]{2,1,0:T(1,128)S(1)} async-done(((f32[128,1,128]{2,1,0:T(1,128)}), f32[128,1,128]{2,1,0:T(1,128)S(1)}, u32[]{:S(2)}, u32[]{:S(2)}) %all-to-all-start) | async-done | bytes 65568 | tf_op jit(solution)/shard_map/all_to_all | solution.py:608
  29.8 0.0 collective-permute-done.on_in
  29.8 0.0 collective-permute-done.1.off_in
  29.8 0.0 copy-done.4
  29.8 0.0 copy-done.5
  29.9 0.0 copy-start.3
  29.9 1.6 %copy-done.3 = f32[4320,128]{1,0:T(8,128)S(1)} copy-done((f32[4320,128]{1,0:T(8,128)S(1)}, f32[4320,128]{1,0:T(8,128)}, u32[]{:S(2)}) %copy-start.3) | copy-done | bytes 2211864
  31.5 4.6 %first_step_edges.1 = (f32[4320,128]{1,0:T(8,128)S(1)}, f32[552,128]{1,0:T(8,128)S(1)}, f32[552,128]{1,0:T(8,128)S(1)}, f32[40,128]{1,0:T(8,128)S(1)}, f32[40,128]{1,0:T(8,128)S(1)}) custom-call(s32[1]{0:T(128)} %bitcast.where_ref, f32[30,36]{1,0:T(8,128)S(1)} %bitcast.12, f32[4320,128]{1,0:T(8,128)S(1)} %copy-done.3, ...), custom_call_target="tpu_custom_call" | custom-call | tf_op jit(solution)/shard_map/first_step_edges/pallas_call | solution.py:625
  36.1 1.0 %collective-permute-start.4 = (f32[552,128]{1,0:T(8,128)S(1)}, f32[552,128]{1,0:T(8,128)S(1)}, u32[]{:S(2)}, u32[]{:S(2)}) collective-permute-start(f32[552,128]{1,0:T(8,128)S(1)} %get-tuple-element.39), channel_id=1, source_target_pairs={{0,1},{1,0},{2,3},{3,2},{4,5},{5,4},{6,7},{7,6},{8,9},{9,8},{10,11... | collective-permute-start | bytes 847880 | tf_op jit(solution)/shard_map/ppermute | solution.py:575
  37.1 4.1 %collective-permute-start.5 = (f32[552,128]{1,0:T(8,128)S(1)}, f32[552,128]{1,0:T(8,128)S(1)}, u32[]{:S(2)}, u32[]{:S(2)}) collective-permute-start(f32[552,128]{1,0:T(8,128)S(1)} %get-tuple-element.40), channel_id=1, source_target_pairs={{1,2},{2,1},{3,4},{4,3},{5,6},{6,5},{7,8},{8,7},{9,10},{10,9},{11,... | collective-permute-start | bytes 847880 | tf_op jit(solution)/shard_map/ppermute | solution.py:574
  41.2 1.5 %collective-permute-start.6 = (f32[40,128]{1,0:T(8,128)S(1)}, f32[40,128]{1,0:T(8,128)S(1)}, u32[]{:S(2)}, u32[]{:S(2)}) collective-permute-start(f32[40,128]{1,0:T(8,128)S(1)} %get-tuple-element.41), channel_id=1, source_target_pairs={{0,112},{16,0},{32,16},{48,32},{64,48},{80,64},{96,80},{112,96},{1... | collective-permute-start | bytes 61448 | tf_op jit(solution)/shard_map/ppermute | solution.py:576
  42.8 0.0 collective-permute-start.7
  42.8 1.3 %last_step_inside.1 = (f32[4320,128]{1,0:T(8,128)S(1)}, f32[8,128]{1,0:T(8,128)S(1)}, f32[8,128]{1,0:T(8,128)S(1)}) custom-call(s32[1]{0:T(128)} %bitcast.where_ref, f32[4320,128]{1,0:T(8,128)S(1)} %get-tuple-element.35.mu_ref, bf16[8640,128]{1,0:T(8,128)(2,1)S(1)} %get-tuple-element.24.spectrum_ref, f32[512,128]{1,0:T(8,128)S(1)} %copy-done.1), custom_call_target="tpu_custom_call" | custom-call | flops 20000000 | bytes 6000000 | tf_op jit(solution)/shard_map/last_step_inside/pallas_call | solution.py:614
  44.1 0.6 %collective-permute-done.6.lon_east_ref = f32[40,128]{1,0:T(8,128)S(1)} collective-permute-done((f32[40,128]{1,0:T(8,128)S(1)}, f32[40,128]{1,0:T(8,128)S(1)}, u32[]{:S(2)}, u32[]{:S(2)}) %collective-permute-start.6) | collective-permute-done | bytes 20512 | tf_op jit(solution)/shard_map/ppermute | solution.py:576
  44.8 2.8 %collective-permute-done.7.lon_west_ref = f32[40,128]{1,0:T(8,128)S(1)} collective-permute-done((f32[40,128]{1,0:T(8,128)S(1)}, f32[40,128]{1,0:T(8,128)S(1)}, u32[]{:S(2)}, u32[]{:S(2)}) %collective-permute-start.7) | collective-permute-done | bytes 20512 | tf_op jit(solution)/shard_map/ppermute | solution.py:577
  47.5 0.0 collective-permute-done.4.on_in
  47.5 2.2 %collective-permute-done.5.off_in = f32[552,128]{1,0:T(8,128)S(1)} collective-permute-done((f32[552,128]{1,0:T(8,128)S(1)}, f32[552,128]{1,0:T(8,128)S(1)}, u32[]{:S(2)}, u32[]{:S(2)}) %collective-permute-start.5) | collective-permute-done | bytes 282656 | tf_op jit(solution)/shard_map/ppermute | solution.py:574
  49.7 3.5 %last_step_edges.1 = f32[4320,128]{1,0:T(8,128)} custom-call(s32[1]{0:T(128)} %bitcast.where_ref, f32[30,36]{1,0:T(8,128)S(1)} %bitcast.13, f32[4320,128]{1,0:T(8,128)S(1)} %get-tuple-element.36.nu_ref, bf16[8640,128]{1,0:T(8,128)(2,1)S(1)} %get-tuple-element.24.spectrum_ref, f32[512,128]{1,0:T(8,128)S(1)} %copy-done.1, s32[4,128]{1,0:T(4,128)S(1)} %copy-done.5, ...), custom_call_target="tpu_custom_call" | custom-call | tf_op jit(solution)/shard_map/last_step_edges/pallas_call | solution.py:641
  (3 shorter events, 0.0 us)
Async XLA Ops:
  0.0 23.8 %copy-start.1 = (f32[512,128]{1,0:T(8,128)S(1)}, f32[512,128]{1,0:T(8,128)}, u32[]{:S(2)}) copy-start(f32[512,128]{1,0:T(8,128)} %constant.6.clone.table_hbm.table_ref) | copy-start | bytes 786436
  5.0 24.8 %collective-permute-start = (f32[552,128]{1,0:T(8,128)}, f32[552,128]{1,0:T(8,128)S(1)}, u32[]{:S(2)}, u32[]{:S(2)}) collective-permute-start(f32[552,128]{1,0:T(8,128)} %get-tuple-element.31), channel_id=1, source_target_pairs={{0,1},{1,0},{2,3},{3,2},{4,5},{5,4},{6,7},{7,6},{8,9},{9,8},{10,11... | collective-permute-start | bytes 847880 | tf_op jit(solution)/shard_map/ppermute | solution.py:575
  6.5 23.3 %collective-permute-start.1 = (f32[552,128]{1,0:T(8,128)}, f32[552,128]{1,0:T(8,128)S(1)}, u32[]{:S(2)}, u32[]{:S(2)}) collective-permute-start(f32[552,128]{1,0:T(8,128)} %get-tuple-element.32), channel_id=1, source_target_pairs={{1,2},{2,1},{3,4},{4,3},{5,6},{6,5},{7,8},{8,7},{9,10},{10,9},{11,... | collective-permute-start | bytes 847880 | tf_op jit(solution)/shard_map/ppermute | solution.py:574
  11.3 18.5 %all-to-all-start = ((f32[128,1,128]{2,1,0:T(1,128)}), f32[128,1,128]{2,1,0:T(1,128)S(1)}, u32[]{:S(2)}, u32[]{:S(2)}) async-start(f32[128,1,128]{2,1,0:T(1,128)} %bitcast.15), calls=%async_computation | async-start | bytes 131072 | tf_op jit(solution)/shard_map/all_to_all | solution.py:608
  20.2 7.9 %collective-permute-start.2 = (f32[40,128]{1,0:T(8,128)}, f32[40,128]{1,0:T(8,128)S(1)}, u32[]{:S(2)}, u32[]{:S(2)}) collective-permute-start(f32[40,128]{1,0:T(8,128)} %get-tuple-element.33), channel_id=1, source_target_pairs={{0,112},{16,0},{32,16},{48,32},{64,48},{80,64},{96,80},{112,96},{1... | collective-permute-start | bytes 61448 | tf_op jit(solution)/shard_map/ppermute | solution.py:576
  23.8 5.2 %collective-permute-start.3 = (f32[40,128]{1,0:T(8,128)}, f32[40,128]{1,0:T(8,128)S(1)}, u32[]{:S(2)}, u32[]{:S(2)}) collective-permute-start(f32[40,128]{1,0:T(8,128)} %get-tuple-element.34), channel_id=1, source_target_pairs={{0,16},{16,32},{32,48},{48,64},{64,80},{80,96},{96,112},{112,0},{1... | collective-permute-start | bytes 61448 | tf_op jit(solution)/shard_map/ppermute | solution.py:577
  23.8 1.6 %copy-start = (f32[36,30,4,128]{3,2,1,0:T(4,128)S(1)}, f32[36,30,4,128]{3,2,1,0:T(4,128)}, u32[]{:S(2)}) copy-start(f32[36,30,4,128]{3,2,1,0:T(4,128)} %param.9) | copy-start | bytes 6635524
  25.4 4.4 %copy-start.4 = (f32[36,30]{0,1:T(8,128)S(1)}, f32[36,30]{0,1:T(8,128)}, u32[]{:S(2)}) copy-start(f32[36,30]{0,1:T(8,128)} %param.11) | copy-start | bytes 12964
  25.4 4.4 %copy-start.5 = (s32[4,128]{1,0:T(4,128)S(1)}, s32[4,128]{1,0:T(4,128)}, u32[]{:S(2)}) copy-start(s32[4,128]{1,0:T(4,128)} %ice_ref.3) | copy-start | bytes 6148
  26.8 1.4 %copy-start.2 = (f32[4320,128]{1,0:T(8,128)}, f32[4320,128]{1,0:T(8,128)S(1)}, u32[]{:S(2)}) copy-start(f32[4320,128]{1,0:T(8,128)S(1)} %get-tuple-element.26.nu_ref) | copy-start | bytes 6635524
  29.9 1.6 %copy-start.3 = (f32[4320,128]{1,0:T(8,128)S(1)}, f32[4320,128]{1,0:T(8,128)}, u32[]{:S(2)}) copy-start(f32[4320,128]{1,0:T(8,128)} %copy-done.2) | copy-start | bytes 6635524
  36.1 11.4 %collective-permute-start.4 = (f32[552,128]{1,0:T(8,128)S(1)}, f32[552,128]{1,0:T(8,128)S(1)}, u32[]{:S(2)}, u32[]{:S(2)}) collective-permute-start(f32[552,128]{1,0:T(8,128)S(1)} %get-tuple-element.39), channel_id=1, source_target_pairs={{0,1},{1,0},{2,3},{3,2},{4,5},{5,4},{6,7},{7,6},{8,9},{9,8},{10,11... | collective-permute-start | bytes 847880 | tf_op jit(solution)/shard_map/ppermute | solution.py:575
  37.1 12.6 %collective-permute-start.5 = (f32[552,128]{1,0:T(8,128)S(1)}, f32[552,128]{1,0:T(8,128)S(1)}, u32[]{:S(2)}, u32[]{:S(2)}) collective-permute-start(f32[552,128]{1,0:T(8,128)S(1)} %get-tuple-element.40), channel_id=1, source_target_pairs={{1,2},{2,1},{3,4},{4,3},{5,6},{6,5},{7,8},{8,7},{9,10},{10,9},{11,... | collective-permute-start | bytes 847880 | tf_op jit(solution)/shard_map/ppermute | solution.py:574
  41.2 3.5 %collective-permute-start.6 = (f32[40,128]{1,0:T(8,128)S(1)}, f32[40,128]{1,0:T(8,128)S(1)}, u32[]{:S(2)}, u32[]{:S(2)}) collective-permute-start(f32[40,128]{1,0:T(8,128)S(1)} %get-tuple-element.41), channel_id=1, source_target_pairs={{0,112},{16,0},{32,16},{48,32},{64,48},{80,64},{96,80},{112,96},{1... | collective-permute-start | bytes 61448 | tf_op jit(solution)/shard_map/ppermute | solution.py:576
  42.8 4.7 %collective-permute-start.7 = (f32[40,128]{1,0:T(8,128)S(1)}, f32[40,128]{1,0:T(8,128)S(1)}, u32[]{:S(2)}, u32[]{:S(2)}) collective-permute-start(f32[40,128]{1,0:T(8,128)S(1)} %get-tuple-element.42), channel_id=1, source_target_pairs={{0,16},{16,32},{32,48},{48,64},{64,80},{80,96},{96,112},{112,0},{1... | collective-permute-start | bytes 61448 | tf_op jit(solution)/shard_map/ppermute | solution.py:577

commit v3 on v2

--- a/solution.py
+++ b/solution.py
@@ -1,4 +1,3 @@
-import functools
 import math
 
 import jax
@@ -33,6 +32,8 @@
 SMEM = pl.BlockSpec(memory_space=pltpu.SMEM)
 
 QUADRANTS = ((True, True), (True, False), (False, False), (False, True))
+
+BOTH_WAYS = ((0, 1), (3, 2))
 
 WEIGHT0 = 0
 SPEED0 = BLOCK
@@ -109,6 +110,24 @@
     return pl.ds(pl.multiple_of((i + QUAD * quadrant) * BLOCK + 8 * jp, 8), count)
 
 
+def piecewise(src, dst, sems, i):
+    return [
+        pltpu.make_async_copy(
+            src.at[direction_rows(i, q, 0, BLOCK)], dst.at[direction_rows(i, q, 0, BLOCK)], sems.at[i, q]
+        )
+        for q in range(4)
+    ]
+
+
+def over_pieces(src, dst, sems, act):
+    def body(i, carry):
+        for copy in piecewise(src, dst, sems, i):
+            act(copy)
+        return carry
+
+    lax.fori_loop(0, QUAD, body, 0)
+
+
 def extract_rows(src, r, first, dst, scale):
     def body(m, carry):
         for u in range(4):
@@ -163,19 +182,20 @@
 def pack_edges(west_ref, east_ref, i, value_of, lane):
     relative = lane - 8 * i
     here = (relative >= 0) & (relative < 8)
-    refs = [west_ref if east else east_ref for _, east in QUADRANTS]
     for lo, hi in ((0, 8), (8, PAIRS)):
         blocks = [None] * 4
         for jp in range(lo, hi):
-            for q, (_, east) in enumerate(QUADRANTS):
-                x = value_of(q, jp)
-                shift = jp - lo + (0 if east else 1)
-                x = pltpu.roll(x, shift, axis=1) if shift else x
-                blocks[q] = x if jp == lo else jnp.where(lane == jp - lo, x, blocks[q])
-        for q in range(4):
+            c = jp - lo
+            for eastward, westward in BOTH_WAYS:
+                ends = jnp.where(lane == LON - 1, value_of(westward, jp), value_of(eastward, jp))
+                ends = pltpu.roll(ends, c, axis=1) if c else ends
+                for q, at in ((eastward, c), (westward, (c - 1) % LON)):
+                    blocks[q] = jnp.where(lane == at, ends, blocks[q]) if c else ends
+        for q, (_, east) in enumerate(QUADRANTS):
+            ref = west_ref if east else east_ref
             place = edge_block(q, lo)
-            moved = pltpu.roll(blocks[q], 8 * i, axis=1)
-            refs[q][place, :] = jnp.where(here, moved, refs[q][place, :])
+            moved = pltpu.roll(blocks[q], 8 * i + (0 if east else 1), axis=1)
+            ref[place, :] = jnp.where(here, moved, ref[place, :])
 
 
 def pick_observations(count, cell, value, out_ref):
@@ -202,9 +222,11 @@
     out_ref[...] = out
 
 
-def fetch(sems, *pairs):
+def fetch(sems, *pairs, ahead=None):
     copies = [pltpu.make_async_copy(src, dst, sems.at[n]) for n, (src, dst) in enumerate(pairs)]
-    for copy in copies:
+    for n, copy in enumerate(copies):
+        if n == 5 and ahead is not None:
+            ahead()
         copy.start()
     return copies
 
@@ -212,7 +234,7 @@
 def start_kernel(
     where_ref, adj_hbm, saved_hbm, table_hbm, sea_hbm, count_hbm, cell_hbm, value_hbm,
     on_ref, off_ref, west_ref, east_ref, obs_ref, field_ref, sea8_ref, early_ref,
-    adj_ref, final_ref, table_ref, sea_ref, count_ref, cell_ref, value_ref, sems,
+    adj_ref, final_ref, table_ref, sea_ref, count_ref, cell_ref, value_ref, sems, adj_sems,
 ):
     half = ROWS // 2
     final0 = STEPS * ROWS
@@ -225,21 +247,32 @@
         (table_hbm.at[pl.ds(0, BLOCK)], table_ref),
         (saved_hbm.at[pl.ds(final0, half)], final_ref.at[pl.ds(0, half)]),
         (saved_hbm.at[pl.ds(final0 + half, half)], final_ref.at[pl.ds(half, half)]),
-        (adj_hbm.at[pl.ds(0, half)], adj_ref.at[pl.ds(0, half)]),
-        (adj_hbm.at[pl.ds(half, half)], adj_ref.at[pl.ds(half, half)]),
         (saved_hbm.at[pl.ds(ROWS, ROWS)], early_ref.at[pl.ds(ROWS, ROWS)]),
         (saved_hbm.at[pl.ds(0, ROWS)], early_ref.at[pl.ds(0, ROWS)]),
+        ahead=lambda: over_pieces(adj_hbm, adj_ref, adj_sems, lambda copy: copy.start()),
     )
     par = where_ref[0] % 2
     sub, lane = iotas()
     for copy in copies[:3]:
         copy.wait()
     pick_observations(count_ref[...], cell_ref[...], value_ref[...], obs_ref)
-    for copy in copies[3:7]:
+    for copy in copies[3:5]:
         copy.wait()
     sea = sea_ref[...].astype(F32)
     sea8 = jnp.concatenate([sea, sea], axis=0)
     sea8_ref[...] = sea8
+    west_ref[...] = jnp.zeros_like(west_ref)
+    east_ref[...] = jnp.zeros_like(east_ref)
+
+    def pack(i, carry):
+        for copy in piecewise(adj_hbm, adj_ref, adj_sems, i):
+            copy.wait()
+        pack_edges(west_ref, east_ref, i, lambda q, jp: adj_ref[direction_rows(i, q, jp), :], lane)
+        return carry
+
+    lax.fori_loop(0, QUAD, pack, 0)
+    for copy in copies[5:7]:
+        copy.wait()
 
     def moment(i, odd, total):
         read = [spectrum_reader(final_ref, i + QUAD * q, (odd + q) % 2) for q in range(4)]
@@ -249,20 +282,9 @@
         return total
 
     total = over_directions(moment, jnp.zeros((8, LON), F32))
-    field = sea8 * 2.0 / jnp.sqrt(total + pltpu.roll(total, 4, axis=0))
+    field = sea8 * 2.0 / jnp.sqrt(both_halves(total))
     field_ref[...] = field
-    for copy in copies[7:9]:
-        copy.wait()
     send_rows(par, adj_ref, on_ref, off_ref, field_ref, sea8_ref)
-
-    west_ref[...] = jnp.zeros_like(west_ref)
-    east_ref[...] = jnp.zeros_like(east_ref)
-
-    def pack(i, carry):
-        pack_edges(west_ref, east_ref, i, lambda q, jp: adj_ref[direction_rows(i, q, jp), :], lane)
-        return carry
-
-    lax.fori_loop(0, QUAD, pack, 0)
     west_sea = jnp.broadcast_to(sea8[:, :1], (8, LON))
     east_sea = jnp.broadcast_to(sea8[:, LON - 1 :], (8, LON))
     for block in range(4):
@@ -270,7 +292,7 @@
         east_ref[tab(block), :] = east_ref[tab(block), :] * east_sea
     west_ref[32:40, :] = jnp.broadcast_to(field[:, :1], (8, LON))
     east_ref[32:40, :] = jnp.broadcast_to(field[:, LON - 1 :], (8, LON))
-    for copy in copies[9:]:
+    for copy in copies[7:]:
         copy.wait()
 
 
@@ -281,18 +303,23 @@
     return (cos_i * stretched, sin_i * stretched), (0.6 * sin_i, 0.6 * cos_i)
 
 
-def turned_edges(lon_east_ref, lon_west_ref, i):
-    turn = (LON - 8 * i) % LON
-    out = {}
+def turned_edges(lon_east_ref, lon_west_ref, i, lane):
+    turned = {}
     for q, (_, east) in enumerate(QUADRANTS):
         for lo in (0, 8):
             ref = lon_east_ref if east else lon_west_ref
-            out[q, lo] = pltpu.roll(ref[edge_block(q, lo), :], turn, axis=1)
+            turn = (LON - 8 * i + (0 if east else 1)) % LON
+            turned[q, lo] = pltpu.roll(ref[edge_block(q, lo), :], turn, axis=1)
+    held = {}
 
     def edge(q, jp):
-        shift = ((LON - 1 if QUADRANTS[q][1] else 0) - jp % 8) % LON
-        block = out[q, 8 * (jp // 8)]
-        return pltpu.roll(block, shift, axis=1) if shift else block
+        pair = q // 2
+        if held.get(pair, (None, None))[0] != jp:
+            eastward, westward = BOTH_WAYS[pair]
+            lo, c = 8 * (jp // 8), jp % 8
+            ends = jnp.where(lane == c + 1, turned[westward, lo], turned[eastward, lo])
+            held[pair] = (jp, pltpu.roll(ends, LON - 1 - c, axis=1))
+        return held[pair][1]
 
     return edge
 
@@ -312,10 +339,14 @@
     return table_ref[SPEED0 + 8 * jp : SPEED0 + 8 * jp + 8, :]
 
 
-def move(dst_ref, spectrum_ref, level, table_ref, stretch, sub, lane, value_of, lon_of, row_of):
+def move(
+    dst_ref, spectrum_ref, level, table_ref, stretch, sub, lane, value_of, lon_of, row_of,
+    before=lambda i: None, after=lambda i: None,
+):
     row = sub % LAT
 
     def body(i, odd, carry):
+        before(i)
         coupling, energy = carry
         x_speed, y_speed = speeds_of(table_ref, stretch, i)
         read = [spectrum_reader(spectrum_ref, i + QUAD * q, (odd + q) % 2, level) for q in range(4)]
@@ -335,6 +366,7 @@
                 coupling = coupling + spectrum * nu
                 all_of = spectrum if all_of is None else all_of + spectrum
             energy = energy + weights(table_ref, jp) * all_of
+        after(i)
         return coupling, energy
 
     coupling, energy = over_directions(body, (jnp.zeros((8, LON), F32), jnp.zeros((8, LON), F32)))
@@ -363,7 +395,7 @@
     def body(i, odd, coupling):
         x_speed, y_speed = speeds_of(table_ref, stretch, i)
         read = [spectrum_reader(spectrum_ref, i + QUAD * q, (odd + q) % 2, level) for q in range(4)]
-        edge = turned_edges(lon_east_ref, lon_west_ref, i)
+        edge = turned_edges(lon_east_ref, lon_west_ref, i, lane)
         extra = [extra_of(q, x_speed[q % 2], y_speed[q % 2]) for q in range(4)]
         for jp in range(PAIRS):
             for q, (north, east) in enumerate(QUADRANTS):
@@ -423,12 +455,12 @@
 
 
 def middle_kernel(
-    where_ref, beta_hbm, nu_ref, spectrum_ref, table_ref, sea8_ref, ice_ref, field_ref,
+    where_ref, beta_hbm, nu_hbm, spectrum_ref, table_ref, sea8_ref, ice_ref, field_ref,
     coupling_ref, energy_ref, obs_ref, on_in, off_in, lon_east_ref, lon_west_ref,
     mu_ref, on_ref, off_ref, west_ref, east_ref,
-    beta_ref, north_ref, south_ref, fields_ref, add_ref, sems,
+    beta_ref, nu_ref, north_ref, south_ref, fields_ref, add_ref, sems,
 ):
-    copies = fetch(sems, (beta_hbm, beta_ref))
+    copies = fetch(sems, (beta_hbm, beta_ref), (nu_hbm, nu_ref))
     par = where_ref[0] % 2
     sub, lane = iotas()
     row = sub % LAT
@@ -458,7 +490,7 @@
 
     def keep(place, jp, gain, extra):
         gain = gain + (add_ref[tab(jp), :] + extra)
-        mu_ref[place, :] = nu_ref[place, :] + gain
+        mu_ref[place, :] = gain
         return gain
 
     gained = edge_gains(
@@ -474,13 +506,14 @@
     set_weighted(table_ref, 0.2 * rate * coupling, add_ref)
     west_ref[...] = jnp.zeros_like(west_ref)
     east_ref[...] = jnp.zeros_like(east_ref)
-    copies[0].wait()
+    for copy in copies:
+        copy.wait()
 
     def source(i, carry):
         def value_of(q, jp):
             beta = rate_of(beta_ref, i + QUAD * q, jp, upper)
             place = direction_rows(i, q, jp)
-            x = mu_ref[place, :] * (base + rate * beta) - add_ref[tab(jp), :]
+            x = (nu_ref[place, :] + mu_ref[place, :]) * (base + rate * beta) - add_ref[tab(jp), :]
             mu_ref[place, :] = x
             return x
 
@@ -491,21 +524,37 @@
     send_rows(par, mu_ref, on_ref, off_ref)
 
 
-def inner_kernel(level, where_ref, mu_ref, spectrum_ref, table_ref, *rest):
+def first_inner_kernel(
+    where_ref, adj_hbm, spectrum_ref, table_ref, sea8_ref, nu_hbm, coupling_ref, energy_ref,
+    adj_ref, nu_ref, adj_sems, nu_sems,
+):
+    over_pieces(adj_hbm, adj_ref, adj_sems, lambda copy: copy.start())
     sub, lane = iotas()
-    nu_ref, coupling_ref, energy_ref = rest[-3:]
-    sea8 = rest[0][...] if len(rest) == 4 else None
-
-    def value_of(i, q, jp):
-        mu = mu_ref[direction_rows(i, q, jp), :]
-        return mu if sea8 is None else mu * sea8
-
-    coupling, energy = move(
-        nu_ref, spectrum_ref, level, table_ref, stretch_of(where_ref, table_ref), sub, lane,
-        value_of, lambda i: lambda q, jp: 0.0, lambda i, q, jp: 0.0,
+    sea8 = sea8_ref[...]
+
+    def before(i):
+        for copy in piecewise(adj_hbm, adj_ref, adj_sems, i):
+            copy.wait()
+
+    def after(i):
+        for copy in piecewise(nu_ref, nu_hbm, nu_sems, i):
+            copy.start()
+
+    coupling_ref[...], energy_ref[...] = move(
+        nu_ref, spectrum_ref, 1, table_ref, stretch_of(where_ref, table_ref), sub, lane,
+        lambda i, q, jp: adj_ref[direction_rows(i, q, jp), :] * sea8,
+        lambda i: lambda q, jp: 0.0, lambda i, q, jp: 0.0, before, after,
     )
-    coupling_ref[...] = coupling
-    energy_ref[...] = energy
+    over_pieces(nu_ref, nu_hbm, nu_sems, lambda copy: copy.wait())
+
+
+def inner_kernel(where_ref, mu_ref, spectrum_ref, table_ref, nu_ref, coupling_ref, energy_ref):
+    sub, lane = iotas()
+    coupling_ref[...], energy_ref[...] = move(
+        nu_ref, spectrum_ref, 0, table_ref, stretch_of(where_ref, table_ref), sub, lane,
+        lambda i, q, jp: mu_ref[direction_rows(i, q, jp), :],
+        lambda i: lambda q, jp: 0.0, lambda i, q, jp: 0.0,
+    )
 
 
 def last_kernel(
@@ -598,7 +647,8 @@
         in_specs=[SMEM] + [HBM] * 7,
         out_specs=(VMEM,) * 8,
         scratch_shapes=[
-            tiles(ROWS), level, tiles(BLOCK), whole(sea_mask), whole(obs_count), whole(obs_cell), whole(obs_value), dma(11),
+            tiles(ROWS), level, tiles(BLOCK), whole(sea_mask), whole(obs_count), whole(obs_cell), whole(obs_value), dma(9),
+            dma(QUAD, 4),
         ],
         compiler_params=params(FIRST),
         name="edges_and_observations",
@@ -610,34 +660,41 @@
 
     rates = pltpu.SMEM(beta.shape, F32)
 
-    def inside(level, name, *operands):
-        return pl.pallas_call(
-            functools.partial(inner_kernel, level),
-            out_shape=(f32(ROWS, LON), f32(8, LON), f32(8, LON)),
-            in_specs=[SMEM] + [VMEM] * len(operands),
-            out_specs=(VMEM,) * 3,
-            compiler_params=params(),
-            cost_estimate=pl.CostEstimate(flops=20_000_000, bytes_accessed=6_000_000, transcendentals=0),
-            name=name,
-        )(where, *operands)
-
-    nu, coupling, energy = inside(1, "first_step_inside", adj, early, table, sea8)
+    hint = pl.CostEstimate(flops=20_000_000, bytes_accessed=6_000_000, transcendentals=0)
+    nu, coupling, energy = pl.pallas_call(
+        first_inner_kernel,
+        out_shape=(pltpu.HBM((ROWS, LON), F32), tiles(8), tiles(8)),
+        in_specs=[SMEM, HBM] + [VMEM] * 3,
+        out_specs=(HBM, VMEM, VMEM),
+        scratch_shapes=[tiles(ROWS), tiles(ROWS), dma(QUAD, 4), dma(QUAD, 4)],
+        compiler_params=params(),
+        cost_estimate=hint,
+        name="first_step_inside",
+    )(where, pltpu.with_memory_space_constraint(adj, pltpu.HBM), early, table, sea8)
     mu, on, off, west, east = pl.pallas_call(
         middle_kernel,
         out_shape=(f32(ROWS, LON),) + payload,
-        in_specs=[SMEM, HBM] + [VMEM] * 13,
+        in_specs=[SMEM, HBM, HBM] + [VMEM] * 12,
         out_specs=(VMEM,) * 5,
-        scratch_shapes=[rates, tiles(SPREAD), tiles(SPREAD), tiles(16), tiles(BLOCK), dma(1)],
+        scratch_shapes=[rates, tiles(ROWS), tiles(SPREAD), tiles(SPREAD), tiles(16), tiles(BLOCK), dma(2)],
         compiler_params=params(),
         name="first_step_edges",
     )(
-        where, beta, nu, early, table, sea8, ice_mask, field, coupling, energy, obs, on, off,
+        where, beta, pltpu.with_memory_space_constraint(nu, pltpu.HBM), early, table, sea8, ice_mask, field, coupling, energy, obs, on, off,
         from_east, from_west,
     )
 
     on, off, from_east, from_west = exchange(on, off, west, east)
 
-    nu, coupling, energy = inside(0, "last_step_inside", mu, early, table)
+    nu, coupling, energy = pl.pallas_call(
+        inner_kernel,
+        out_shape=(f32(ROWS, LON), f32(8, LON), f32(8, LON)),
+        in_specs=[SMEM] + [VMEM] * 3,
+        out_specs=(VMEM,) * 3,
+        compiler_params=params(),
+        cost_estimate=hint,
+        name="last_step_inside",
+    )(where, mu, early, table)
     out = pl.pallas_call(
         last_kernel,
         out_shape=f32(ROWS, LON),

time: 53.4 us -> 51.7 us (0.968)
  local copies, waits for them, and re-layouts: 4.6 us -> 0.01 us
  Pallas kernels: 15.8 us -> 18.1 us
  waiting for transfers between devices: 7.34 us -> 7.89 us
    unnamed x12 -> x6, local copies, waits for them, and re-layouts: 4.6 us -> 0.01 us
    pallas_call x2, Pallas kernels: 2.67 us -> 5.1 us  [the longest x1 3.75 us: on_device(): pl.pallas_call(first_inner_kernel, out_shape=(pltpu.HBM((ROWS, LON), F32)...]
  transfers between devices with their start and end apart: 9 -> 9, of which waited for: 5 -> 5; matrix products, arithmetic and copies ran while one was open for 0% -> 0% of each run, Pallas kernels for 5% -> 10%
where the time goes in v3:
time: 51.7 us; the launch traced here: 51.5 us
  starting transfers between devices  25.4 us (49%)
  Pallas kernels  18.1 us (35%)
  waiting for transfers between devices  7.89 us (15%)
    ppermute x2, starting transfers between devices, exchange(): off = lax.ppermute(off, 'lat', far)  8.88 us
    all_to_all x1, starting transfers between devices, on_device(): lax.all_to_all(obs.reshape(128, 1, 128), ('lon', 'lat'), split_axis=0, co...  8.87 us
    pallas_call x1, Pallas kernels, on_device(): pl.pallas_call(start_kernel, out_shape=payload + (f32(128, 128), tiles(8)...  4.73 us
    pallas_call x1, Pallas kernels, on_device(): pl.pallas_call(middle_kernel, out_shape=(f32(ROWS, LON),) + payload, in_s...  4.67 us
    ppermute x2, starting transfers between devices, exchange(): lax.ppermute(west, 'lon', [(i, (i - 1) % n_lon) for i in range(n_lon)])  4.6 us
    pallas_call x1, Pallas kernels, on_device(): pl.pallas_call(first_inner_kernel, out_shape=(pltpu.HBM((ROWS, LON), F32)...  3.75 us
    ppermute x2, waiting for transfers between devices, exchange(): lax.ppermute(east, 'lon', [(i, (i + 1) % n_lon) for i in range(n_lon)])  3.7 us
    pallas_call x1, Pallas kernels, on_device(): pl.pallas_call(last_kernel, out_shape=f32(ROWS, LON), in_specs=[SMEM, HBM...  3.57 us
  transfers between devices with their start and end apart: 9, of which 5 were waited for; matrix products, arithmetic and copies ran while one was open for 0% of the time, Pallas kernels for 10%

profile of v3, /device:TPU:1, one launch (start us, length us, event | category | flops | bytes accessed | tf_op | source)
XLA Modules:
  0.0 51.5 jit_solution(15674664621419879447)
XLA Ops:
  0.0 0.0 copy-start
  0.0 4.7 %edges_and_observations.1 = (f32[552,128]{1,0:T(8,128)}, f32[552,128]{1,0:T(8,128)}, f32[40,128]{1,0:T(8,128)}, f32[40,128]{1,0:T(8,128)}, f32[128,128]{1,0:T(8,...) custom-call(s32[1]{0:T(128)} %bitcast.where_ref, f32[4320,128]{1,0:T(8,128)} %bitcast.12, ...), custom_call_target="tpu_custom_call" | custom-call | tf_op jit(solution)/shard_map/edges_and_observations/pallas_call | solution.py:642
  4.7 1.5 %collective-permute-start = (f32[552,128]{1,0:T(8,128)}, f32[552,128]{1,0:T(8,128)S(1)}, u32[]{:S(2)}, u32[]{:S(2)}) collective-permute-start(f32[552,128]{1,0:T(8,128)} %get-tuple-element.31), channel_id=1, source_target_pairs={{0,1},{1,0},{2,3},{3,2},{4,5},{5,4},{6,7},{7,6},{8,9},{9,8},{10,11... | collective-permute-start | bytes 847880 | tf_op jit(solution)/shard_map/ppermute | solution.py:624
  6.2 4.8 %collective-permute-start.1 = (f32[552,128]{1,0:T(8,128)}, f32[552,128]{1,0:T(8,128)S(1)}, u32[]{:S(2)}, u32[]{:S(2)}) collective-permute-start(f32[552,128]{1,0:T(8,128)} %get-tuple-element.32), channel_id=1, source_target_pairs={{1,2},{2,1},{3,4},{4,3},{5,6},{6,5},{7,8},{8,7},{9,10},{10,9},{11,... | collective-permute-start | bytes 847880 | tf_op jit(solution)/shard_map/ppermute | solution.py:623
  11.1 8.9 %all-to-all-start = ((f32[128,1,128]{2,1,0:T(1,128)}), f32[128,1,128]{2,1,0:T(1,128)S(1)}, u32[]{:S(2)}, u32[]{:S(2)}) async-start(f32[128,1,128]{2,1,0:T(1,128)} %bitcast.15), calls=%async_computation | async-start | bytes 131072 | tf_op jit(solution)/shard_map/all_to_all | solution.py:658
  19.9 3.6 %collective-permute-start.2 = (f32[40,128]{1,0:T(8,128)}, f32[40,128]{1,0:T(8,128)S(1)}, u32[]{:S(2)}, u32[]{:S(2)}) collective-permute-start(f32[40,128]{1,0:T(8,128)} %get-tuple-element.33), channel_id=1, source_target_pairs={{0,112},{16,0},{32,16},{48,32},{64,48},{80,64},{96,80},{112,96},{1... | collective-permute-start | bytes 61448 | tf_op jit(solution)/shard_map/ppermute | solution.py:625
  23.5 0.0 collective-permute-start.3
  23.5 0.0 copy-done
  23.5 0.0 copy-start.1
  23.5 0.0 copy-start.2
  23.5 3.8 %first_step_inside.1 = (f32[4320,128]{1,0:T(8,128)}, f32[8,128]{1,0:T(8,128)S(1)}, f32[8,128]{1,0:T(8,128)S(1)}) custom-call(s32[1]{0:T(128)} %bitcast.where_ref, f32[4320,128]{1,0:T(8,128)} %bitcast.13, bf16[8640,128]{1,0:T(8,128)(2,1)S(1)} %get-tuple-element.24.spectrum_ref, f32[512,128]{1,0:T(8,128)S(1)} %copy-done, f32[8,128]{1,0:T(8,128)S(1)} %get-tuple-element.25.sea8_ref), custom_call_target="tpu_custom_call" | custom-call | flops 20000000 | bytes 6000000 | tf_op jit(solution)/shard_map/first_step_inside/pallas_call | solution.py:664
  27.3 0.0 collective-permute-done.2.lon_east_ref
  27.3 1.5 %collective-permute-done.3.lon_west_ref = f32[40,128]{1,0:T(8,128)S(1)} collective-permute-done((f32[40,128]{1,0:T(8,128)}, f32[40,128]{1,0:T(8,128)S(1)}, u32[]{:S(2)}, u32[]{:S(2)}) %collective-permute-start.3) | collective-permute-done | bytes 20512 | tf_op jit(solution)/shard_map/ppermute | solution.py:626
  28.8 0.8 %all-to-all-done = f32[128,1,128]{2,1,0:T(1,128)S(1)} async-done(((f32[128,1,128]{2,1,0:T(1,128)}), f32[128,1,128]{2,1,0:T(1,128)S(1)}, u32[]{:S(2)}, u32[]{:S(2)}) %all-to-all-start) | async-done | bytes 65568 | tf_op jit(solution)/shard_map/all_to_all | solution.py:658
  29.5 0.0 collective-permute-done.on_in
  29.5 0.0 collective-permute-done.1.off_in
  29.5 0.0 copy-done.1
  29.6 0.0 copy-done.2
  29.6 4.7 %first_step_edges.1 = (f32[4320,128]{1,0:T(8,128)S(1)}, f32[552,128]{1,0:T(8,128)S(1)}, f32[552,128]{1,0:T(8,128)S(1)}, f32[40,128]{1,0:T(8,128)S(1)}, f32[40,128]{1,0:T(8,128)S(1)}) custom-call(s32[1]{0:T(128)} %bitcast.where_ref, f32[30,36]{1,0:T(8,128)S(1)} %bitcast.10, f32[4320,128]{1,0:T(8,128)} %get-tuple-element.26.nu_hbm, ...), custom_call_target="tpu_custom_call" | custom-call | tf_op jit(solution)/shard_map/first_step_edges/pallas_call | solution.py:674
  34.2 1.0 %collective-permute-start.4 = (f32[552,128]{1,0:T(8,128)S(1)}, f32[552,128]{1,0:T(8,128)S(1)}, u32[]{:S(2)}, u32[]{:S(2)}) collective-permute-start(f32[552,128]{1,0:T(8,128)S(1)} %get-tuple-element.39), channel_id=1, source_target_pairs={{0,1},{1,0},{2,3},{3,2},{4,5},{5,4},{6,7},{7,6},{8,9},{9,8},{10,11... | collective-permute-start | bytes 847880 | tf_op jit(solution)/shard_map/ppermute | solution.py:624
  35.3 4.1 %collective-permute-start.5 = (f32[552,128]{1,0:T(8,128)S(1)}, f32[552,128]{1,0:T(8,128)S(1)}, u32[]{:S(2)}, u32[]{:S(2)}) collective-permute-start(f32[552,128]{1,0:T(8,128)S(1)} %get-tuple-element.40), channel_id=1, source_target_pairs={{1,2},{2,1},{3,4},{4,3},{5,6},{6,5},{7,8},{8,7},{9,10},{10,9},{11,... | collective-permute-start | bytes 847880 | tf_op jit(solution)/shard_map/ppermute | solution.py:623
  39.4 1.0 %collective-permute-start.6 = (f32[40,128]{1,0:T(8,128)S(1)}, f32[40,128]{1,0:T(8,128)S(1)}, u32[]{:S(2)}, u32[]{:S(2)}) collective-permute-start(f32[40,128]{1,0:T(8,128)S(1)} %get-tuple-element.41), channel_id=1, source_target_pairs={{0,112},{16,0},{32,16},{48,32},{64,48},{80,64},{96,80},{112,96},{1... | collective-permute-start | bytes 61448 | tf_op jit(solution)/shard_map/ppermute | solution.py:625
  40.4 0.5 collective-permute-start.7
  40.9 1.3 %last_step_inside.1 = (f32[4320,128]{1,0:T(8,128)S(1)}, f32[8,128]{1,0:T(8,128)S(1)}, f32[8,128]{1,0:T(8,128)S(1)}) custom-call(s32[1]{0:T(128)} %bitcast.where_ref, f32[4320,128]{1,0:T(8,128)S(1)} %get-tuple-element.35.mu_ref, bf16[8640,128]{1,0:T(8,128)(2,1)S(1)} %get-tuple-element.24.spectrum_ref, f32[512,128]{1,0:T(8,128)S(1)} %copy-done), custom_call_target="tpu_custom_call" | custom-call | flops 20000000 | bytes 6000000 | tf_op jit(solution)/shard_map/last_step_inside/pallas_call | solution.py:689
  42.2 0.6 %collective-permute-done.6.lon_east_ref = f32[40,128]{1,0:T(8,128)S(1)} collective-permute-done((f32[40,128]{1,0:T(8,128)S(1)}, f32[40,128]{1,0:T(8,128)S(1)}, u32[]{:S(2)}, u32[]{:S(2)}) %collective-permute-start.6) | collective-permute-done | bytes 20512 | tf_op jit(solution)/shard_map/ppermute | solution.py:625
  42.9 2.2 %collective-permute-done.7.lon_west_ref = f32[40,128]{1,0:T(8,128)S(1)} collective-permute-done((f32[40,128]{1,0:T(8,128)S(1)}, f32[40,128]{1,0:T(8,128)S(1)}, u32[]{:S(2)}, u32[]{:S(2)}) %collective-permute-start.7) | collective-permute-done | bytes 20512 | tf_op jit(solution)/shard_map/ppermute | solution.py:626
  45.1 0.0 collective-permute-done.4.on_in
  45.1 2.8 %collective-permute-done.5.off_in = f32[552,128]{1,0:T(8,128)S(1)} collective-permute-done((f32[552,128]{1,0:T(8,128)S(1)}, f32[552,128]{1,0:T(8,128)S(1)}, u32[]{:S(2)}, u32[]{:S(2)}) %collective-permute-start.5) | collective-permute-done | bytes 282656 | tf_op jit(solution)/shard_map/ppermute | solution.py:623
  47.9 3.6 %last_step_edges.1 = f32[4320,128]{1,0:T(8,128)} custom-call(s32[1]{0:T(128)} %bitcast.where_ref, f32[30,36]{1,0:T(8,128)S(1)} %bitcast.11, f32[4320,128]{1,0:T(8,128)S(1)} %get-tuple-element.36.nu_ref, bf16[8640,128]{1,0:T(8,128)(2,1)S(1)} %get-tuple-element.24.spectrum_ref, f32[512,128]{1,0:T(8,128)S(1)} %copy-done, s32[4,128]{1,0:T(4,128)S(1)} %copy-done.2, ...), custom_call_target="tpu_custom_call" | custom-call | tf_op jit(solution)/shard_map/last_step_edges/pallas_call | solution.py:698
Async XLA Ops:
  0.0 23.5 %copy-start = (f32[512,128]{1,0:T(8,128)S(1)}, f32[512,128]{1,0:T(8,128)}, u32[]{:S(2)}) copy-start(f32[512,128]{1,0:T(8,128)} %constant.6.clone.table_hbm.table_ref) | copy-start | bytes 786436
  4.7 24.8 %collective-permute-start = (f32[552,128]{1,0:T(8,128)}, f32[552,128]{1,0:T(8,128)S(1)}, u32[]{:S(2)}, u32[]{:S(2)}) collective-permute-start(f32[552,128]{1,0:T(8,128)} %get-tuple-element.31), channel_id=1, source_target_pairs={{0,1},{1,0},{2,3},{3,2},{4,5},{5,4},{6,7},{7,6},{8,9},{9,8},{10,11... | collective-permute-start | bytes 847880 | tf_op jit(solution)/shard_map/ppermute | solution.py:624
  6.2 23.3 %collective-permute-start.1 = (f32[552,128]{1,0:T(8,128)}, f32[552,128]{1,0:T(8,128)S(1)}, u32[]{:S(2)}, u32[]{:S(2)}) collective-permute-start(f32[552,128]{1,0:T(8,128)} %get-tuple-element.32), channel_id=1, source_target_pairs={{1,2},{2,1},{3,4},{4,3},{5,6},{6,5},{7,8},{8,7},{9,10},{10,9},{11,... | collective-permute-start | bytes 847880 | tf_op jit(solution)/shard_map/ppermute | solution.py:623
  11.1 18.5 %all-to-all-start = ((f32[128,1,128]{2,1,0:T(1,128)}), f32[128,1,128]{2,1,0:T(1,128)S(1)}, u32[]{:S(2)}, u32[]{:S(2)}) async-start(f32[128,1,128]{2,1,0:T(1,128)} %bitcast.15), calls=%async_computation | async-start | bytes 131072 | tf_op jit(solution)/shard_map/all_to_all | solution.py:658
  19.9 7.3 %collective-permute-start.2 = (f32[40,128]{1,0:T(8,128)}, f32[40,128]{1,0:T(8,128)S(1)}, u32[]{:S(2)}, u32[]{:S(2)}) collective-permute-start(f32[40,128]{1,0:T(8,128)} %get-tuple-element.33), channel_id=1, source_target_pairs={{0,112},{16,0},{32,16},{48,32},{64,48},{80,64},{96,80},{112,96},{1... | collective-permute-start | bytes 61448 | tf_op jit(solution)/shard_map/ppermute | solution.py:625
  23.5 5.2 %collective-permute-start.3 = (f32[40,128]{1,0:T(8,128)}, f32[40,128]{1,0:T(8,128)S(1)}, u32[]{:S(2)}, u32[]{:S(2)}) collective-permute-start(f32[40,128]{1,0:T(8,128)} %get-tuple-element.34), channel_id=1, source_target_pairs={{0,16},{16,32},{32,48},{48,64},{64,80},{80,96},{96,112},{112,0},{1... | collective-permute-start | bytes 61448 | tf_op jit(solution)/shard_map/ppermute | solution.py:626
  23.5 6.0 %copy-start.1 = (f32[36,30]{0,1:T(8,128)S(1)}, f32[36,30]{0,1:T(8,128)}, u32[]{:S(2)}) copy-start(f32[36,30]{0,1:T(8,128)} %param.11) | copy-start | bytes 12964
  23.5 6.0 %copy-start.2 = (s32[4,128]{1,0:T(4,128)S(1)}, s32[4,128]{1,0:T(4,128)}, u32[]{:S(2)}) copy-start(s32[4,128]{1,0:T(4,128)} %ice_ref.3) | copy-start | bytes 6148
  34.2 10.9 %collective-permute-start.4 = (f32[552,128]{1,0:T(8,128)S(1)}, f32[552,128]{1,0:T(8,128)S(1)}, u32[]{:S(2)}, u32[]{:S(2)}) collective-permute-start(f32[552,128]{1,0:T(8,128)S(1)} %get-tuple-element.39), channel_id=1, source_target_pairs={{0,1},{1,0},{2,3},{3,2},{4,5},{5,4},{6,7},{7,6},{8,9},{9,8},{10,11... | collective-permute-start | bytes 847880 | tf_op jit(solution)/shard_map/ppermute | solution.py:624
  35.3 12.6 %collective-permute-start.5 = (f32[552,128]{1,0:T(8,128)S(1)}, f32[552,128]{1,0:T(8,128)S(1)}, u32[]{:S(2)}, u32[]{:S(2)}) collective-permute-start(f32[552,128]{1,0:T(8,128)S(1)} %get-tuple-element.40), channel_id=1, source_target_pairs={{1,2},{2,1},{3,4},{4,3},{5,6},{6,5},{7,8},{8,7},{9,10},{10,9},{11,... | collective-permute-start | bytes 847880 | tf_op jit(solution)/shard_map/ppermute | solution.py:623
  39.4 3.5 %collective-permute-start.6 = (f32[40,128]{1,0:T(8,128)S(1)}, f32[40,128]{1,0:T(8,128)S(1)}, u32[]{:S(2)}, u32[]{:S(2)}) collective-permute-start(f32[40,128]{1,0:T(8,128)S(1)} %get-tuple-element.41), channel_id=1, source_target_pairs={{0,112},{16,0},{32,16},{48,32},{64,48},{80,64},{96,80},{112,96},{1... | collective-permute-start | bytes 61448 | tf_op jit(solution)/shard_map/ppermute | solution.py:625
  40.4 4.7 %collective-permute-start.7 = (f32[40,128]{1,0:T(8,128)S(1)}, f32[40,128]{1,0:T(8,128)S(1)}, u32[]{:S(2)}, u32[]{:S(2)}) collective-permute-start(f32[40,128]{1,0:T(8,128)S(1)} %get-tuple-element.42), channel_id=1, source_target_pairs={{0,16},{16,32},{32,48},{48,64},{64,80},{80,96},{96,112},{112,0},{1... | collective-permute-start | bytes 61448 | tf_op jit(solution)/shard_map/ppermute | solution.py:626

commit v4 on v3

--- a/solution.py
+++ b/solution.py
@@ -457,7 +457,7 @@
 def middle_kernel(
     where_ref, beta_hbm, nu_hbm, spectrum_ref, table_ref, sea8_ref, ice_ref, field_ref,
     coupling_ref, energy_ref, obs_ref, on_in, off_in, lon_east_ref, lon_west_ref,
-    mu_ref, on_ref, off_ref, west_ref, east_ref,
+    mu_ref, on_ref, off_ref,
     beta_ref, nu_ref, north_ref, south_ref, fields_ref, add_ref, sems,
 ):
     copies = fetch(sems, (beta_hbm, beta_ref), (nu_hbm, nu_ref))
@@ -504,24 +504,32 @@
     rate = sea8 * (1.0 - jnp.concatenate([ice, ice], axis=0))
     base = sea8 - 0.2 * rate * energy
     set_weighted(table_ref, 0.2 * rate * coupling, add_ref)
+    for copy in copies:
+        copy.wait()
+
+    def source(i, carry):
+        for jp in range(PAIRS):
+            for q in range(4):
+                beta = rate_of(beta_ref, i + QUAD * q, jp, upper)
+                place = direction_rows(i, q, jp)
+                x = (nu_ref[place, :] + mu_ref[place, :]) * (base + rate * beta)
+                mu_ref[place, :] = x - add_ref[tab(jp), :]
+        return carry
+
+    lax.fori_loop(0, QUAD, source, 0)
+    send_rows(par, mu_ref, on_ref, off_ref)
+
+
+def pack_kernel(mu_ref, west_ref, east_ref):
+    _, lane = iotas()
     west_ref[...] = jnp.zeros_like(west_ref)
     east_ref[...] = jnp.zeros_like(east_ref)
-    for copy in copies:
-        copy.wait()
-
-    def source(i, carry):
-        def value_of(q, jp):
-            beta = rate_of(beta_ref, i + QUAD * q, jp, upper)
-            place = direction_rows(i, q, jp)
-            x = (nu_ref[place, :] + mu_ref[place, :]) * (base + rate * beta) - add_ref[tab(jp), :]
-            mu_ref[place, :] = x
-            return x
-
-        pack_edges(west_ref, east_ref, i, value_of, lane)
+
+    def pack(i, carry):
+        pack_edges(west_ref, east_ref, i, lambda q, jp: mu_ref[direction_rows(i, q, jp), :], lane)
         return carry
 
-    lax.fori_loop(0, QUAD, source, 0)
-    send_rows(par, mu_ref, on_ref, off_ref)
+    lax.fori_loop(0, QUAD, pack, 0)
 
 
 def first_inner_kernel(
@@ -671,11 +679,11 @@
         cost_estimate=hint,
         name="first_step_inside",
     )(where, pltpu.with_memory_space_constraint(adj, pltpu.HBM), early, table, sea8)
-    mu, on, off, west, east = pl.pallas_call(
+    mu, on, off = pl.pallas_call(
         middle_kernel,
-        out_shape=(f32(ROWS, LON),) + payload,
+        out_shape=(f32(ROWS, LON),) + payload[:2],
         in_specs=[SMEM, HBM, HBM] + [VMEM] * 12,
-        out_specs=(VMEM,) * 5,
+        out_specs=(VMEM,) * 3,
         scratch_shapes=[rates, tiles(ROWS), tiles(SPREAD), tiles(SPREAD), tiles(16), tiles(BLOCK), dma(2)],
         compiler_params=params(),
         name="first_step_edges",
@@ -684,6 +692,15 @@
         from_east, from_west,
     )
 
+    west, east = pl.pallas_call(
+        pack_kernel,
+        out_shape=payload[2:],
+        in_specs=[VMEM],
+        out_specs=(VMEM,) * 2,
+        compiler_params=params(),
+        cost_estimate=pl.CostEstimate(flops=3_000_000, bytes_accessed=2_200_000, transcendentals=0),
+        name="edges_of_first_step",
+    )(mu)
     on, off, from_east, from_west = exchange(on, off, west, east)
 
     nu, coupling, energy = pl.pallas_call(

time: 51.7 us -> 50.5 us (0.977)
  waiting for transfers between devices: 7.89 us -> 6.47 us
    ppermute x2, waiting for transfers between devices: 2.76 us -> 1.31 us  [exchange(): off = lax.ppermute(off, 'lat', far)]
    ppermute x2, waiting for transfers between devices: 3.7 us -> 4.24 us  [exchange(): lax.ppermute(east, 'lon', [(i, (i + 1) % n_lon) for i in range(n_lon)])]
    pallas_call x1 -> x2, Pallas kernels: 4.67 us -> 5.03 us  [the longest x1 3.5 us: on_device(): pl.pallas_call(middle_kernel, out_shape=(f32(ROWS, LON),) + payload[:2],...]
  transfers between devices with their start and end apart: 9 -> 9, of which waited for: 5 -> 5; matrix products, arithmetic and copies ran while one was open for 0% -> 0% of each run, Pallas kernels for 10% -> 13%
where the time goes in v4:
time: 50.5 us; the launch traced here: 50.3 us
  starting transfers between devices  25.4 us (50%)
  Pallas kernels  18.4 us (36%)
  waiting for transfers between devices  6.47 us (13%)
    all_to_all x1, starting transfers between devices, on_device(): lax.all_to_all(obs.reshape(128, 1, 128), ('lon', 'lat'), split_axis=0, co...  8.87 us
    ppermute x2, starting transfers between devices, exchange(): off = lax.ppermute(off, 'lat', far)  8.87 us
    pallas_call x1, Pallas kernels, on_device(): pl.pallas_call(start_kernel, out_shape=payload + (f32(128, 128), tiles(8)...  4.74 us
    ppermute x2, starting transfers between devices, exchange(): lax.ppermute(west, 'lon', [(i, (i - 1) % n_lon) for i in range(n_lon)])  4.54 us
    ppermute x2, waiting for transfers between devices, exchange(): lax.ppermute(east, 'lon', [(i, (i + 1) % n_lon) for i in range(n_lon)])  4.24 us
    pallas_call x1, Pallas kernels, on_device(): pl.pallas_call(first_inner_kernel, out_shape=(pltpu.HBM((ROWS, LON), F32)...  3.75 us
    pallas_call x1, Pallas kernels, on_device(): pl.pallas_call(last_kernel, out_shape=f32(ROWS, LON), in_specs=[SMEM, HBM...  3.57 us
    pallas_call x1, Pallas kernels, on_device(): pl.pallas_call(middle_kernel, out_shape=(f32(ROWS, LON),) + payload[:2],...  3.5 us
  transfers between devices with their start and end apart: 9, of which 5 were waited for; matrix products, arithmetic and copies ran while one was open for 0% of the time, Pallas kernels for 13%

profile of v4, /device:TPU:1, one launch (start us, length us, event | category | flops | bytes accessed | tf_op | source)
XLA Modules:
  0.0 50.3 jit_solution(13018324862373132171)
XLA Ops:
  0.0 0.0 copy-start
  0.0 4.7 %edges_and_observations.1 = (f32[552,128]{1,0:T(8,128)}, f32[552,128]{1,0:T(8,128)}, f32[40,128]{1,0:T(8,128)}, f32[40,128]{1,0:T(8,128)}, f32[128,128]{1,0:T(8,...) custom-call(s32[1]{0:T(128)} %bitcast.where_ref, f32[4320,128]{1,0:T(8,128)} %bitcast.12, ...), custom_call_target="tpu_custom_call" | custom-call | tf_op jit(solution)/shard_map/edges_and_observations/pallas_call | solution.py:650
  4.8 1.5 %collective-permute-start = (f32[552,128]{1,0:T(8,128)}, f32[552,128]{1,0:T(8,128)S(1)}, u32[]{:S(2)}, u32[]{:S(2)}) collective-permute-start(f32[552,128]{1,0:T(8,128)} %get-tuple-element.31), channel_id=1, source_target_pairs={{0,1},{1,0},{2,3},{3,2},{4,5},{5,4},{6,7},{7,6},{8,9},{9,8},{10,11... | collective-permute-start | bytes 847880 | tf_op jit(solution)/shard_map/ppermute | solution.py:632
  6.3 4.8 %collective-permute-start.1 = (f32[552,128]{1,0:T(8,128)}, f32[552,128]{1,0:T(8,128)S(1)}, u32[]{:S(2)}, u32[]{:S(2)}) collective-permute-start(f32[552,128]{1,0:T(8,128)} %get-tuple-element.32), channel_id=1, source_target_pairs={{1,2},{2,1},{3,4},{4,3},{5,6},{6,5},{7,8},{8,7},{9,10},{10,9},{11,... | collective-permute-start | bytes 847880 | tf_op jit(solution)/shard_map/ppermute | solution.py:631
  11.1 8.9 %all-to-all-start = ((f32[128,1,128]{2,1,0:T(1,128)}), f32[128,1,128]{2,1,0:T(1,128)S(1)}, u32[]{:S(2)}, u32[]{:S(2)}) async-start(f32[128,1,128]{2,1,0:T(1,128)} %bitcast.15), calls=%async_computation | async-start | bytes 131072 | tf_op jit(solution)/shard_map/all_to_all | solution.py:666
  19.9 3.6 %collective-permute-start.2 = (f32[40,128]{1,0:T(8,128)}, f32[40,128]{1,0:T(8,128)S(1)}, u32[]{:S(2)}, u32[]{:S(2)}) collective-permute-start(f32[40,128]{1,0:T(8,128)} %get-tuple-element.33), channel_id=1, source_target_pairs={{0,112},{16,0},{32,16},{48,32},{64,48},{80,64},{96,80},{112,96},{1... | collective-permute-start | bytes 61448 | tf_op jit(solution)/shard_map/ppermute | solution.py:633
  23.5 0.0 collective-permute-start.3
  23.5 0.0 copy-done
  23.5 0.0 copy-start.1
  23.5 0.0 copy-start.2
  23.5 3.8 %first_step_inside.1 = (f32[4320,128]{1,0:T(8,128)}, f32[8,128]{1,0:T(8,128)S(1)}, f32[8,128]{1,0:T(8,128)S(1)}) custom-call(s32[1]{0:T(128)} %bitcast.where_ref, f32[4320,128]{1,0:T(8,128)} %bitcast.13, bf16[8640,128]{1,0:T(8,128)(2,1)S(1)} %get-tuple-element.24.spectrum_ref, f32[512,128]{1,0:T(8,128)S(1)} %copy-done, f32[8,128]{1,0:T(8,128)S(1)} %get-tuple-element.25.sea8_ref), custom_call_target="tpu_custom_call" | custom-call | flops 20000000 | bytes 6000000 | tf_op jit(solution)/shard_map/first_step_inside/pallas_call | solution.py:672
  27.3 0.0 collective-permute-done.2.lon_east_ref
  27.3 1.5 %collective-permute-done.3.lon_west_ref = f32[40,128]{1,0:T(8,128)S(1)} collective-permute-done((f32[40,128]{1,0:T(8,128)}, f32[40,128]{1,0:T(8,128)S(1)}, u32[]{:S(2)}, u32[]{:S(2)}) %collective-permute-start.3) | collective-permute-done | bytes 20512 | tf_op jit(solution)/shard_map/ppermute | solution.py:634
  28.8 0.8 %all-to-all-done = f32[128,1,128]{2,1,0:T(1,128)S(1)} async-done(((f32[128,1,128]{2,1,0:T(1,128)}), f32[128,1,128]{2,1,0:T(1,128)S(1)}, u32[]{:S(2)}, u32[]{:S(2)}) %all-to-all-start) | async-done | bytes 65568 | tf_op jit(solution)/shard_map/all_to_all | solution.py:666
  29.5 0.0 collective-permute-done.on_in
  29.5 0.0 collective-permute-done.1.off_in
  29.5 0.0 copy-done.1
  29.5 0.0 copy-done.2
  29.6 3.5 %first_step_edges.1 = (f32[4320,128]{1,0:T(8,128)S(1)}, f32[552,128]{1,0:T(8,128)S(1)}, f32[552,128]{1,0:T(8,128)S(1)}) custom-call(s32[1]{0:T(128)} %bitcast.where_ref, f32[30,36]{1,0:T(8,128)S(1)} %bitcast.10, f32[4320,128]{1,0:T(8,128)} %get-tuple-element.26.nu_hbm, bf16[8640,128]{1,0:T(8,128)(2,1)S(1)} %get-tuple-element.24.spectrum_ref, ...), custom_call_target="tpu_custom_call" | custom-call | tf_op jit(solution)/shard_map/first_step_edges/pallas_call | solution.py:682
  33.1 1.1 %collective-permute-start.4 = (f32[552,128]{1,0:T(8,128)S(1)}, f32[552,128]{1,0:T(8,128)S(1)}, u32[]{:S(2)}, u32[]{:S(2)}) collective-permute-start(f32[552,128]{1,0:T(8,128)S(1)} %get-tuple-element.39), channel_id=1, source_target_pairs={{0,1},{1,0},{2,3},{3,2},{4,5},{5,4},{6,7},{7,6},{8,9},{9,8},{10,11... | collective-permute-start | bytes 847880 | tf_op jit(solution)/shard_map/ppermute | solution.py:632
  34.1 4.1 %collective-permute-start.5 = (f32[552,128]{1,0:T(8,128)S(1)}, f32[552,128]{1,0:T(8,128)S(1)}, u32[]{:S(2)}, u32[]{:S(2)}) collective-permute-start(f32[552,128]{1,0:T(8,128)S(1)} %get-tuple-element.40), channel_id=1, source_target_pairs={{1,2},{2,1},{3,4},{4,3},{5,6},{6,5},{7,8},{8,7},{9,10},{10,9},{11,... | collective-permute-start | bytes 847880 | tf_op jit(solution)/shard_map/ppermute | solution.py:631
  38.2 1.5 %edges_of_first_step.1 = (f32[40,128]{1,0:T(8,128)S(1)}, f32[40,128]{1,0:T(8,128)S(1)}) custom-call(f32[4320,128]{1,0:T(8,128)S(1)} %get-tuple-element.35.mu_ref), custom_call_target="tpu_custom_call" | custom-call | flops 3000000 | bytes 2200000 | tf_op jit(solution)/shard_map/edges_of_first_step/pallas_call | solution.py:695
  39.7 1.0 %collective-permute-start.6 = (f32[40,128]{1,0:T(8,128)S(1)}, f32[40,128]{1,0:T(8,128)S(1)}, u32[]{:S(2)}, u32[]{:S(2)}) collective-permute-start(f32[40,128]{1,0:T(8,128)S(1)} %get-tuple-element.41), channel_id=1, source_target_pairs={{0,112},{16,0},{32,16},{48,32},{64,48},{80,64},{96,80},{112,96},{1... | collective-permute-start | bytes 61448 | tf_op jit(solution)/shard_map/ppermute | solution.py:633
  40.7 0.5 %collective-permute-start.7 = (f32[40,128]{1,0:T(8,128)S(1)}, f32[40,128]{1,0:T(8,128)S(1)}, u32[]{:S(2)}, u32[]{:S(2)}) collective-permute-start(f32[40,128]{1,0:T(8,128)S(1)} %get-tuple-element.42), channel_id=1, source_target_pairs={{0,16},{16,32},{32,48},{48,64},{64,80},{80,96},{96,112},{112,0},{1... | collective-permute-start | bytes 61448 | tf_op jit(solution)/shard_map/ppermute | solution.py:634
  41.2 1.3 %last_step_inside.1 = (f32[4320,128]{1,0:T(8,128)S(1)}, f32[8,128]{1,0:T(8,128)S(1)}, f32[8,128]{1,0:T(8,128)S(1)}) custom-call(s32[1]{0:T(128)} %bitcast.where_ref, f32[4320,128]{1,0:T(8,128)S(1)} %get-tuple-element.35.mu_ref, bf16[8640,128]{1,0:T(8,128)(2,1)S(1)} %get-tuple-element.24.spectrum_ref, f32[512,128]{1,0:T(8,128)S(1)} %copy-done), custom_call_target="tpu_custom_call" | custom-call | flops 20000000 | bytes 6000000 | tf_op jit(solution)/shard_map/last_step_inside/pallas_call | solution.py:706
  42.5 0.2 collective-permute-done.6.lon_east_ref
  42.7 2.8 %collective-permute-done.7.lon_west_ref = f32[40,128]{1,0:T(8,128)S(1)} collective-permute-done((f32[40,128]{1,0:T(8,128)S(1)}, f32[40,128]{1,0:T(8,128)S(1)}, u32[]{:S(2)}, u32[]{:S(2)}) %collective-permute-start.7) | collective-permute-done | bytes 20512 | tf_op jit(solution)/shard_map/ppermute | solution.py:634
  45.4 0.0 collective-permute-done.4.on_in
  45.4 1.3 %collective-permute-done.5.off_in = f32[552,128]{1,0:T(8,128)S(1)} collective-permute-done((f32[552,128]{1,0:T(8,128)S(1)}, f32[552,128]{1,0:T(8,128)S(1)}, u32[]{:S(2)}, u32[]{:S(2)}) %collective-permute-start.5) | collective-permute-done | bytes 282656 | tf_op jit(solution)/shard_map/ppermute | solution.py:631
  46.8 3.6 %last_step_edges.1 = f32[4320,128]{1,0:T(8,128)} custom-call(s32[1]{0:T(128)} %bitcast.where_ref, f32[30,36]{1,0:T(8,128)S(1)} %bitcast.11, f32[4320,128]{1,0:T(8,128)S(1)} %get-tuple-element.36.nu_ref, bf16[8640,128]{1,0:T(8,128)(2,1)S(1)} %get-tuple-element.24.spectrum_ref, f32[512,128]{1,0:T(8,128)S(1)} %copy-done, s32[4,128]{1,0:T(4,128)S(1)} %copy-done.2, ...), custom_call_target="tpu_custom_call" | custom-call | tf_op jit(solution)/shard_map/last_step_edges/pallas_call | solution.py:715
Async XLA Ops:
  0.0 23.5 %copy-start = (f32[512,128]{1,0:T(8,128)S(1)}, f32[512,128]{1,0:T(8,128)}, u32[]{:S(2)}) copy-start(f32[512,128]{1,0:T(8,128)} %constant.6.clone.table_hbm.table_ref) | copy-start | bytes 786436
  4.8 24.8 %collective-permute-start = (f32[552,128]{1,0:T(8,128)}, f32[552,128]{1,0:T(8,128)S(1)}, u32[]{:S(2)}, u32[]{:S(2)}) collective-permute-start(f32[552,128]{1,0:T(8,128)} %get-tuple-element.31), channel_id=1, source_target_pairs={{0,1},{1,0},{2,3},{3,2},{4,5},{5,4},{6,7},{7,6},{8,9},{9,8},{10,11... | collective-permute-start | bytes 847880 | tf_op jit(solution)/shard_map/ppermute | solution.py:632
  6.3 23.3 %collective-permute-start.1 = (f32[552,128]{1,0:T(8,128)}, f32[552,128]{1,0:T(8,128)S(1)}, u32[]{:S(2)}, u32[]{:S(2)}) collective-permute-start(f32[552,128]{1,0:T(8,128)} %get-tuple-element.32), channel_id=1, source_target_pairs={{1,2},{2,1},{3,4},{4,3},{5,6},{6,5},{7,8},{8,7},{9,10},{10,9},{11,... | collective-permute-start | bytes 847880 | tf_op jit(solution)/shard_map/ppermute | solution.py:631
  11.1 18.5 %all-to-all-start = ((f32[128,1,128]{2,1,0:T(1,128)}), f32[128,1,128]{2,1,0:T(1,128)S(1)}, u32[]{:S(2)}, u32[]{:S(2)}) async-start(f32[128,1,128]{2,1,0:T(1,128)} %bitcast.15), calls=%async_computation | async-start | bytes 131072 | tf_op jit(solution)/shard_map/all_to_all | solution.py:666
  19.9 7.3 %collective-permute-start.2 = (f32[40,128]{1,0:T(8,128)}, f32[40,128]{1,0:T(8,128)S(1)}, u32[]{:S(2)}, u32[]{:S(2)}) collective-permute-start(f32[40,128]{1,0:T(8,128)} %get-tuple-element.33), channel_id=1, source_target_pairs={{0,112},{16,0},{32,16},{48,32},{64,48},{80,64},{96,80},{112,96},{1... | collective-permute-start | bytes 61448 | tf_op jit(solution)/shard_map/ppermute | solution.py:633
  23.5 5.2 %collective-permute-start.3 = (f32[40,128]{1,0:T(8,128)}, f32[40,128]{1,0:T(8,128)S(1)}, u32[]{:S(2)}, u32[]{:S(2)}) collective-permute-start(f32[40,128]{1,0:T(8,128)} %get-tuple-element.34), channel_id=1, source_target_pairs={{0,16},{16,32},{32,48},{48,64},{64,80},{80,96},{96,112},{112,0},{1... | collective-permute-start | bytes 61448 | tf_op jit(solution)/shard_map/ppermute | solution.py:634
  23.5 6.0 %copy-start.1 = (f32[36,30]{0,1:T(8,128)S(1)}, f32[36,30]{0,1:T(8,128)}, u32[]{:S(2)}) copy-start(f32[36,30]{0,1:T(8,128)} %param.11) | copy-start | bytes 12964
  23.5 6.0 %copy-start.2 = (s32[4,128]{1,0:T(4,128)S(1)}, s32[4,128]{1,0:T(4,128)}, u32[]{:S(2)}) copy-start(s32[4,128]{1,0:T(4,128)} %ice_ref.3) | copy-start | bytes 6148
  33.1 12.4 %collective-permute-start.4 = (f32[552,128]{1,0:T(8,128)S(1)}, f32[552,128]{1,0:T(8,128)S(1)}, u32[]{:S(2)}, u32[]{:S(2)}) collective-permute-start(f32[552,128]{1,0:T(8,128)S(1)} %get-tuple-element.39), channel_id=1, source_target_pairs={{0,1},{1,0},{2,3},{3,2},{4,5},{5,4},{6,7},{7,6},{8,9},{9,8},{10,11... | collective-permute-start | bytes 847880 | tf_op jit(solution)/shard_map/ppermute | solution.py:632
  34.1 12.6 %collective-permute-start.5 = (f32[552,128]{1,0:T(8,128)S(1)}, f32[552,128]{1,0:T(8,128)S(1)}, u32[]{:S(2)}, u32[]{:S(2)}) collective-permute-start(f32[552,128]{1,0:T(8,128)S(1)} %get-tuple-element.40), channel_id=1, source_target_pairs={{1,2},{2,1},{3,4},{4,3},{5,6},{6,5},{7,8},{8,7},{9,10},{10,9},{11,... | collective-permute-start | bytes 847880 | tf_op jit(solution)/shard_map/ppermute | solution.py:631
  39.7 2.9 %collective-permute-start.6 = (f32[40,128]{1,0:T(8,128)S(1)}, f32[40,128]{1,0:T(8,128)S(1)}, u32[]{:S(2)}, u32[]{:S(2)}) collective-permute-start(f32[40,128]{1,0:T(8,128)S(1)} %get-tuple-element.41), channel_id=1, source_target_pairs={{0,112},{16,0},{32,16},{48,32},{64,48},{80,64},{96,80},{112,96},{1... | collective-permute-start | bytes 61448 | tf_op jit(solution)/shard_map/ppermute | solution.py:633
  40.7 4.7 %collective-permute-start.7 = (f32[40,128]{1,0:T(8,128)S(1)}, f32[40,128]{1,0:T(8,128)S(1)}, u32[]{:S(2)}, u32[]{:S(2)}) collective-permute-start(f32[40,128]{1,0:T(8,128)S(1)} %get-tuple-element.42), channel_id=1, source_target_pairs={{0,16},{16,32},{32,48},{48,64},{64,80},{80,96},{96,112},{112,0},{1... | collective-permute-start | bytes 61448 | tf_op jit(solution)/shard_map/ppermute | solution.py:634

commit v5 on v4

--- a/solution.py
+++ b/solution.py
@@ -655,7 +655,7 @@
         in_specs=[SMEM] + [HBM] * 7,
         out_specs=(VMEM,) * 8,
         scratch_shapes=[
-            tiles(ROWS), level, tiles(BLOCK), whole(sea_mask), whole(obs_count), whole(obs_cell), whole(obs_value), dma(9),
+            tiles(ROWS + 8), level, tiles(BLOCK), whole(sea_mask), whole(obs_count), whole(obs_cell), whole(obs_value), dma(9),
             dma(QUAD, 4),
         ],
         compiler_params=params(FIRST),
@@ -681,7 +681,7 @@
     )(where, pltpu.with_memory_space_constraint(adj, pltpu.HBM), early, table, sea8)
     mu, on, off = pl.pallas_call(
         middle_kernel,
-        out_shape=(f32(ROWS, LON),) + payload[:2],
+        out_shape=(f32(ROWS + 8, LON),) + payload[:2],
         in_specs=[SMEM, HBM, HBM] + [VMEM] * 12,
         out_specs=(VMEM,) * 3,
         scratch_shapes=[rates, tiles(ROWS), tiles(SPREAD), tiles(SPREAD), tiles(16), tiles(BLOCK), dma(2)],

time: 50.5 us -> 50.5 us (level)
  no operation moved by 1% of the time
where the time goes in v5:
time: 50.5 us; the launch traced here: 50.3 us
  starting transfers between devices  25.4 us (50%)
  Pallas kernels  18.4 us (36%)
  waiting for transfers between devices  6.47 us (13%)
    all_to_all x1, starting transfers between devices, on_device(): lax.all_to_all(obs.reshape(128, 1, 128), ('lon', 'lat'), split_axis=0, co...  8.87 us
    ppermute x2, starting transfers between devices, exchange(): off = lax.ppermute(off, 'lat', far)  8.87 us
    pallas_call x1, Pallas kernels, on_device(): pl.pallas_call(start_kernel, out_shape=payload + (f32(128, 128), tiles(8)...  4.74 us
    ppermute x2, starting transfers between devices, exchange(): lax.ppermute(west, 'lon', [(i, (i - 1) % n_lon) for i in range(n_lon)])  4.54 us
    ppermute x2, waiting for transfers between devices, exchange(): lax.ppermute(east, 'lon', [(i, (i + 1) % n_lon) for i in range(n_lon)])  4.24 us
    pallas_call x1, Pallas kernels, on_device(): pl.pallas_call(first_inner_kernel, out_shape=(pltpu.HBM((ROWS, LON), F32)...  3.75 us
    pallas_call x1, Pallas kernels, on_device(): pl.pallas_call(last_kernel, out_shape=f32(ROWS, LON), in_specs=[SMEM, HBM...  3.57 us
    pallas_call x1, Pallas kernels, on_device(): pl.pallas_call(middle_kernel, out_shape=(f32(ROWS + 8, LON),) + payload[:...  3.5 us
  transfers between devices with their start and end apart: 9, of which 5 were waited for; matrix products, arithmetic and copies ran while one was open for 0% of the time, Pallas kernels for 13%

profile of v5, /device:TPU:1, one launch (start us, length us, event | category | flops | bytes accessed | tf_op | source)
XLA Modules:
  0.0 50.3 jit_solution(16777670963998858547)
XLA Ops:
  0.0 0.0 copy-start
  0.0 4.7 %edges_and_observations.1 = (f32[552,128]{1,0:T(8,128)}, f32[552,128]{1,0:T(8,128)}, f32[40,128]{1,0:T(8,128)}, f32[40,128]{1,0:T(8,128)}, f32[128,128]{1,0:T(8,...) custom-call(s32[1]{0:T(128)} %bitcast.where_ref, f32[4320,128]{1,0:T(8,128)} %bitcast.12, ...), custom_call_target="tpu_custom_call" | custom-call | tf_op jit(solution)/shard_map/edges_and_observations/pallas_call | solution.py:650
  4.8 1.5 %collective-permute-start = (f32[552,128]{1,0:T(8,128)}, f32[552,128]{1,0:T(8,128)S(1)}, u32[]{:S(2)}, u32[]{:S(2)}) collective-permute-start(f32[552,128]{1,0:T(8,128)} %get-tuple-element.31), channel_id=1, source_target_pairs={{0,1},{1,0},{2,3},{3,2},{4,5},{5,4},{6,7},{7,6},{8,9},{9,8},{10,11... | collective-permute-start | bytes 847880 | tf_op jit(solution)/shard_map/ppermute | solution.py:632
  6.3 4.8 %collective-permute-start.1 = (f32[552,128]{1,0:T(8,128)}, f32[552,128]{1,0:T(8,128)S(1)}, u32[]{:S(2)}, u32[]{:S(2)}) collective-permute-start(f32[552,128]{1,0:T(8,128)} %get-tuple-element.32), channel_id=1, source_target_pairs={{1,2},{2,1},{3,4},{4,3},{5,6},{6,5},{7,8},{8,7},{9,10},{10,9},{11,... | collective-permute-start | bytes 847880 | tf_op jit(solution)/shard_map/ppermute | solution.py:631
  11.1 8.9 %all-to-all-start = ((f32[128,1,128]{2,1,0:T(1,128)}), f32[128,1,128]{2,1,0:T(1,128)S(1)}, u32[]{:S(2)}, u32[]{:S(2)}) async-start(f32[128,1,128]{2,1,0:T(1,128)} %bitcast.15), calls=%async_computation | async-start | bytes 131072 | tf_op jit(solution)/shard_map/all_to_all | solution.py:666
  19.9 3.6 %collective-permute-start.2 = (f32[40,128]{1,0:T(8,128)}, f32[40,128]{1,0:T(8,128)S(1)}, u32[]{:S(2)}, u32[]{:S(2)}) collective-permute-start(f32[40,128]{1,0:T(8,128)} %get-tuple-element.33), channel_id=1, source_target_pairs={{0,112},{16,0},{32,16},{48,32},{64,48},{80,64},{96,80},{112,96},{1... | collective-permute-start | bytes 61448 | tf_op jit(solution)/shard_map/ppermute | solution.py:633
  23.5 0.0 collective-permute-start.3
  23.5 0.0 copy-done
  23.5 0.0 copy-start.1
  23.5 0.0 copy-start.2
  23.5 3.8 %first_step_inside.1 = (f32[4320,128]{1,0:T(8,128)}, f32[8,128]{1,0:T(8,128)S(1)}, f32[8,128]{1,0:T(8,128)S(1)}) custom-call(s32[1]{0:T(128)} %bitcast.where_ref, f32[4320,128]{1,0:T(8,128)} %bitcast.13, bf16[8640,128]{1,0:T(8,128)(2,1)S(1)} %get-tuple-element.24.spectrum_ref, f32[512,128]{1,0:T(8,128)S(1)} %copy-done, f32[8,128]{1,0:T(8,128)S(1)} %get-tuple-element.25.sea8_ref), custom_call_target="tpu_custom_call" | custom-call | flops 20000000 | bytes 6000000 | tf_op jit(solution)/shard_map/first_step_inside/pallas_call | solution.py:672
  27.3 0.0 collective-permute-done.2.lon_east_ref
  27.3 1.5 %collective-permute-done.3.lon_west_ref = f32[40,128]{1,0:T(8,128)S(1)} collective-permute-done((f32[40,128]{1,0:T(8,128)}, f32[40,128]{1,0:T(8,128)S(1)}, u32[]{:S(2)}, u32[]{:S(2)}) %collective-permute-start.3) | collective-permute-done | bytes 20512 | tf_op jit(solution)/shard_map/ppermute | solution.py:634
  28.8 0.8 %all-to-all-done = f32[128,1,128]{2,1,0:T(1,128)S(1)} async-done(((f32[128,1,128]{2,1,0:T(1,128)}), f32[128,1,128]{2,1,0:T(1,128)S(1)}, u32[]{:S(2)}, u32[]{:S(2)}) %all-to-all-start) | async-done | bytes 65568 | tf_op jit(solution)/shard_map/all_to_all | solution.py:666
  29.5 0.0 collective-permute-done.on_in
  29.5 0.0 collective-permute-done.1.off_in
  29.5 0.0 copy-done.1
  29.5 0.0 copy-done.2
  29.6 3.5 %first_step_edges.1 = (f32[4328,128]{1,0:T(8,128)S(1)}, f32[552,128]{1,0:T(8,128)S(1)}, f32[552,128]{1,0:T(8,128)S(1)}) custom-call(s32[1]{0:T(128)} %bitcast.where_ref, f32[30,36]{1,0:T(8,128)S(1)} %bitcast.10, f32[4320,128]{1,0:T(8,128)} %get-tuple-element.26.nu_hbm, bf16[8640,128]{1,0:T(8,128)(2,1)S(1)} %get-tuple-element.24.spectrum_ref, ...), custom_call_target="tpu_custom_call" | custom-call | tf_op jit(solution)/shard_map/first_step_edges/pallas_call | solution.py:682
  33.1 1.1 %collective-permute-start.4 = (f32[552,128]{1,0:T(8,128)S(1)}, f32[552,128]{1,0:T(8,128)S(1)}, u32[]{:S(2)}, u32[]{:S(2)}) collective-permute-start(f32[552,128]{1,0:T(8,128)S(1)} %get-tuple-element.39), channel_id=1, source_target_pairs={{0,1},{1,0},{2,3},{3,2},{4,5},{5,4},{6,7},{7,6},{8,9},{9,8},{10,11... | collective-permute-start | bytes 847880 | tf_op jit(solution)/shard_map/ppermute | solution.py:632
  34.1 4.1 %collective-permute-start.5 = (f32[552,128]{1,0:T(8,128)S(1)}, f32[552,128]{1,0:T(8,128)S(1)}, u32[]{:S(2)}, u32[]{:S(2)}) collective-permute-start(f32[552,128]{1,0:T(8,128)S(1)} %get-tuple-element.40), channel_id=1, source_target_pairs={{1,2},{2,1},{3,4},{4,3},{5,6},{6,5},{7,8},{8,7},{9,10},{10,9},{11,... | collective-permute-start | bytes 847880 | tf_op jit(solution)/shard_map/ppermute | solution.py:631
  38.2 1.5 %edges_of_first_step.1 = (f32[40,128]{1,0:T(8,128)S(1)}, f32[40,128]{1,0:T(8,128)S(1)}) custom-call(f32[4328,128]{1,0:T(8,128)S(1)} %get-tuple-element.35.mu_ref), custom_call_target="tpu_custom_call" | custom-call | flops 3000000 | bytes 2200000 | tf_op jit(solution)/shard_map/edges_of_first_step/pallas_call | solution.py:695
  39.7 1.0 %collective-permute-start.6 = (f32[40,128]{1,0:T(8,128)S(1)}, f32[40,128]{1,0:T(8,128)S(1)}, u32[]{:S(2)}, u32[]{:S(2)}) collective-permute-start(f32[40,128]{1,0:T(8,128)S(1)} %get-tuple-element.41), channel_id=1, source_target_pairs={{0,112},{16,0},{32,16},{48,32},{64,48},{80,64},{96,80},{112,96},{1... | collective-permute-start | bytes 61448 | tf_op jit(solution)/shard_map/ppermute | solution.py:633
  40.7 0.5 %collective-permute-start.7 = (f32[40,128]{1,0:T(8,128)S(1)}, f32[40,128]{1,0:T(8,128)S(1)}, u32[]{:S(2)}, u32[]{:S(2)}) collective-permute-start(f32[40,128]{1,0:T(8,128)S(1)} %get-tuple-element.42), channel_id=1, source_target_pairs={{0,16},{16,32},{32,48},{48,64},{64,80},{80,96},{96,112},{112,0},{1... | collective-permute-start | bytes 61448 | tf_op jit(solution)/shard_map/ppermute | solution.py:634
  41.2 1.3 %last_step_inside.1 = (f32[4320,128]{1,0:T(8,128)S(1)}, f32[8,128]{1,0:T(8,128)S(1)}, f32[8,128]{1,0:T(8,128)S(1)}) custom-call(s32[1]{0:T(128)} %bitcast.where_ref, f32[4328,128]{1,0:T(8,128)S(1)} %get-tuple-element.35.mu_ref, bf16[8640,128]{1,0:T(8,128)(2,1)S(1)} %get-tuple-element.24.spectrum_ref, f32[512,128]{1,0:T(8,128)S(1)} %copy-done), custom_call_target="tpu_custom_call" | custom-call | flops 20000000 | bytes 6000000 | tf_op jit(solution)/shard_map/last_step_inside/pallas_call | solution.py:706
  42.5 0.2 collective-permute-done.6.lon_east_ref
  42.7 2.8 %collective-permute-done.7.lon_west_ref = f32[40,128]{1,0:T(8,128)S(1)} collective-permute-done((f32[40,128]{1,0:T(8,128)S(1)}, f32[40,128]{1,0:T(8,128)S(1)}, u32[]{:S(2)}, u32[]{:S(2)}) %collective-permute-start.7) | collective-permute-done | bytes 20512 | tf_op jit(solution)/shard_map/ppermute | solution.py:634
  45.4 0.0 collective-permute-done.4.on_in
  45.4 1.3 %collective-permute-done.5.off_in = f32[552,128]{1,0:T(8,128)S(1)} collective-permute-done((f32[552,128]{1,0:T(8,128)S(1)}, f32[552,128]{1,0:T(8,128)S(1)}, u32[]{:S(2)}, u32[]{:S(2)}) %collective-permute-start.5) | collective-permute-done | bytes 282656 | tf_op jit(solution)/shard_map/ppermute | solution.py:631
  46.8 3.6 %last_step_edges.1 = f32[4320,128]{1,0:T(8,128)} custom-call(s32[1]{0:T(128)} %bitcast.where_ref, f32[30,36]{1,0:T(8,128)S(1)} %bitcast.11, f32[4320,128]{1,0:T(8,128)S(1)} %get-tuple-element.36.nu_ref, bf16[8640,128]{1,0:T(8,128)(2,1)S(1)} %get-tuple-element.24.spectrum_ref, f32[512,128]{1,0:T(8,128)S(1)} %copy-done, s32[4,128]{1,0:T(4,128)S(1)} %copy-done.2, ...), custom_call_target="tpu_custom_call" | custom-call | tf_op jit(solution)/shard_map/last_step_edges/pallas_call | solution.py:715
Async XLA Ops:
  0.0 23.5 %copy-start = (f32[512,128]{1,0:T(8,128)S(1)}, f32[512,128]{1,0:T(8,128)}, u32[]{:S(2)}) copy-start(f32[512,128]{1,0:T(8,128)} %constant.6.clone.table_hbm.table_ref) | copy-start | bytes 786436
  4.8 24.8 %collective-permute-start = (f32[552,128]{1,0:T(8,128)}, f32[552,128]{1,0:T(8,128)S(1)}, u32[]{:S(2)}, u32[]{:S(2)}) collective-permute-start(f32[552,128]{1,0:T(8,128)} %get-tuple-element.31), channel_id=1, source_target_pairs={{0,1},{1,0},{2,3},{3,2},{4,5},{5,4},{6,7},{7,6},{8,9},{9,8},{10,11... | collective-permute-start | bytes 847880 | tf_op jit(solution)/shard_map/ppermute | solution.py:632
  6.3 23.3 %collective-permute-start.1 = (f32[552,128]{1,0:T(8,128)}, f32[552,128]{1,0:T(8,128)S(1)}, u32[]{:S(2)}, u32[]{:S(2)}) collective-permute-start(f32[552,128]{1,0:T(8,128)} %get-tuple-element.32), channel_id=1, source_target_pairs={{1,2},{2,1},{3,4},{4,3},{5,6},{6,5},{7,8},{8,7},{9,10},{10,9},{11,... | collective-permute-start | bytes 847880 | tf_op jit(solution)/shard_map/ppermute | solution.py:631
  11.1 18.5 %all-to-all-start = ((f32[128,1,128]{2,1,0:T(1,128)}), f32[128,1,128]{2,1,0:T(1,128)S(1)}, u32[]{:S(2)}, u32[]{:S(2)}) async-start(f32[128,1,128]{2,1,0:T(1,128)} %bitcast.15), calls=%async_computation | async-start | bytes 131072 | tf_op jit(solution)/shard_map/all_to_all | solution.py:666
  19.9 7.3 %collective-permute-start.2 = (f32[40,128]{1,0:T(8,128)}, f32[40,128]{1,0:T(8,128)S(1)}, u32[]{:S(2)}, u32[]{:S(2)}) collective-permute-start(f32[40,128]{1,0:T(8,128)} %get-tuple-element.33), channel_id=1, source_target_pairs={{0,112},{16,0},{32,16},{48,32},{64,48},{80,64},{96,80},{112,96},{1... | collective-permute-start | bytes 61448 | tf_op jit(solution)/shard_map/ppermute | solution.py:633
  23.5 5.2 %collective-permute-start.3 = (f32[40,128]{1,0:T(8,128)}, f32[40,128]{1,0:T(8,128)S(1)}, u32[]{:S(2)}, u32[]{:S(2)}) collective-permute-start(f32[40,128]{1,0:T(8,128)} %get-tuple-element.34), channel_id=1, source_target_pairs={{0,16},{16,32},{32,48},{48,64},{64,80},{80,96},{96,112},{112,0},{1... | collective-permute-start | bytes 61448 | tf_op jit(solution)/shard_map/ppermute | solution.py:634
  23.5 6.0 %copy-start.1 = (f32[36,30]{0,1:T(8,128)S(1)}, f32[36,30]{0,1:T(8,128)}, u32[]{:S(2)}) copy-start(f32[36,30]{0,1:T(8,128)} %param.11) | copy-start | bytes 12964
  23.5 6.0 %copy-start.2 = (s32[4,128]{1,0:T(4,128)S(1)}, s32[4,128]{1,0:T(4,128)}, u32[]{:S(2)}) copy-start(s32[4,128]{1,0:T(4,128)} %ice_ref.3) | copy-start | bytes 6148
  33.1 12.4 %collective-permute-start.4 = (f32[552,128]{1,0:T(8,128)S(1)}, f32[552,128]{1,0:T(8,128)S(1)}, u32[]{:S(2)}, u32[]{:S(2)}) collective-permute-start(f32[552,128]{1,0:T(8,128)S(1)} %get-tuple-element.39), channel_id=1, source_target_pairs={{0,1},{1,0},{2,3},{3,2},{4,5},{5,4},{6,7},{7,6},{8,9},{9,8},{10,11... | collective-permute-start | bytes 847880 | tf_op jit(solution)/shard_map/ppermute | solution.py:632
  34.1 12.6 %collective-permute-start.5 = (f32[552,128]{1,0:T(8,128)S(1)}, f32[552,128]{1,0:T(8,128)S(1)}, u32[]{:S(2)}, u32[]{:S(2)}) collective-permute-start(f32[552,128]{1,0:T(8,128)S(1)} %get-tuple-element.40), channel_id=1, source_target_pairs={{1,2},{2,1},{3,4},{4,3},{5,6},{6,5},{7,8},{8,7},{9,10},{10,9},{11,... | collective-permute-start | bytes 847880 | tf_op jit(solution)/shard_map/ppermute | solution.py:631
  39.7 2.9 %collective-permute-start.6 = (f32[40,128]{1,0:T(8,128)S(1)}, f32[40,128]{1,0:T(8,128)S(1)}, u32[]{:S(2)}, u32[]{:S(2)}) collective-permute-start(f32[40,128]{1,0:T(8,128)S(1)} %get-tuple-element.41), channel_id=1, source_target_pairs={{0,112},{16,0},{32,16},{48,32},{64,48},{80,64},{96,80},{112,96},{1... | collective-permute-start | bytes 61448 | tf_op jit(solution)/shard_map/ppermute | solution.py:633
  40.7 4.7 %collective-permute-start.7 = (f32[40,128]{1,0:T(8,128)S(1)}, f32[40,128]{1,0:T(8,128)S(1)}, u32[]{:S(2)}, u32[]{:S(2)}) collective-permute-start(f32[40,128]{1,0:T(8,128)S(1)} %get-tuple-element.42), channel_id=1, source_target_pairs={{0,16},{16,32},{32,48},{48,64},{64,80},{80,96},{96,112},{112,0},{1... | collective-permute-start | bytes 61448 | tf_op jit(solution)/shard_map/ppermute | solution.py:634

commit v6 on v5

--- a/solution.py
+++ b/solution.py
@@ -649,8 +649,8 @@
 
     on, off, west, east, obs, field, sea8, early = pl.pallas_call(
         start_kernel,
-        out_shape=payload
-        + (f32(128, 128), tiles(8), tiles(8))
+        out_shape=(tiles(HALO), tiles(HALO), tiles(EDGE), tiles(EDGE))
+        + (tiles(128), tiles(8), tiles(8))
         + (pltpu.VMEM((2 * ROWS, LON), jnp.bfloat16),),
         in_specs=[SMEM] + [HBM] * 7,
         out_specs=(VMEM,) * 8,

time: 50.5 us -> 50.6 us (level)
  no operation moved by 1% of the time
where the time goes in v6:
time: 50.6 us; the launch traced here: 50.4 us
  starting transfers between devices  25.1 us (50%)
  Pallas kernels  18.3 us (36%)
  waiting for transfers between devices  6.91 us (14%)
    all_to_all x1, starting transfers between devices, on_device(): lax.all_to_all(obs.reshape(128, 1, 128), ('lon', 'lat'), split_axis=0, co...  8.87 us
    ppermute x2, starting transfers between devices, exchange(): off = lax.ppermute(off, 'lat', far)  8.67 us
    ppermute x2, starting transfers between devices, exchange(): lax.ppermute(west, 'lon', [(i, (i - 1) % n_lon) for i in range(n_lon)])  4.75 us
    pallas_call x1, Pallas kernels, on_device(): pl.pallas_call(start_kernel, out_shape=(tiles(HALO), tiles(HALO), tiles(E...  4.63 us
    ppermute x2, waiting for transfers between devices, exchange(): lax.ppermute(east, 'lon', [(i, (i + 1) % n_lon) for i in range(n_lon)])  4.24 us
    pallas_call x1, Pallas kernels, on_device(): pl.pallas_call(first_inner_kernel, out_shape=(pltpu.HBM((ROWS, LON), F32)...  3.75 us
    pallas_call x1, Pallas kernels, on_device(): pl.pallas_call(last_kernel, out_shape=f32(ROWS, LON), in_specs=[SMEM, HBM...  3.57 us
    pallas_call x1, Pallas kernels, on_device(): pl.pallas_call(middle_kernel, out_shape=(f32(ROWS + 8, LON),) + payload[:...  3.5 us
  transfers between devices with their start and end apart: 9, of which 5 were waited for; matrix products, arithmetic and copies ran while one was open for 0% of the time, Pallas kernels for 13%

profile of v6, /device:TPU:1, one launch (start us, length us, event | category | flops | bytes accessed | tf_op | source)
XLA Modules:
  0.0 50.4 jit_solution(17502677981648105881)
XLA Ops:
  0.0 0.0 copy-start
  0.0 4.6 %edges_and_observations.1 = (f32[552,128]{1,0:T(8,128)}, f32[552,128]{1,0:T(8,128)S(1)}, f32[40,128]{1,0:T(8,128)S(1)}, f32[40,128]{1,0:T(8,128)S(1)}, f32[128,1...) custom-call(s32[1]{0:T(128)} %bitcast.where_ref, ...), custom_call_target="tpu_custom_call" | custom-call | tf_op jit(solution)/shard_map/edges_and_observations/pallas_call | solution.py:650
  4.6 1.5 %collective-permute-start = (f32[552,128]{1,0:T(8,128)}, f32[552,128]{1,0:T(8,128)S(1)}, u32[]{:S(2)}, u32[]{:S(2)}) collective-permute-start(f32[552,128]{1,0:T(8,128)} %get-tuple-element.31), channel_id=1, source_target_pairs={{0,1},{1,0},{2,3},{3,2},{4,5},{5,4},{6,7},{7,6},{8,9},{9,8},{10,11... | collective-permute-start | bytes 847880 | tf_op jit(solution)/shard_map/ppermute | solution.py:632
  6.1 4.8 %collective-permute-start.1 = (f32[552,128]{1,0:T(8,128)S(1)}, f32[552,128]{1,0:T(8,128)S(1)}, u32[]{:S(2)}, u32[]{:S(2)}) collective-permute-start(f32[552,128]{1,0:T(8,128)S(1)} %get-tuple-element.32), channel_id=1, source_target_pairs={{1,2},{2,1},{3,4},{4,3},{5,6},{6,5},{7,8},{8,7},{9,10},{10,9},{11,... | collective-permute-start | bytes 847880 | tf_op jit(solution)/shard_map/ppermute | solution.py:631
  11.0 8.9 %all-to-all-start = ((f32[128,1,128]{2,1,0:T(1,128)}), f32[128,1,128]{2,1,0:T(1,128)S(1)}, u32[]{:S(2)}, u32[]{:S(2)}) async-start(f32[128,1,128]{2,1,0:T(1,128)} %bitcast.5), calls=%async_computation | async-start | bytes 131072 | tf_op jit(solution)/shard_map/all_to_all | solution.py:666
  19.8 3.6 %collective-permute-start.2 = (f32[40,128]{1,0:T(8,128)S(1)}, f32[40,128]{1,0:T(8,128)S(1)}, u32[]{:S(2)}, u32[]{:S(2)}) collective-permute-start(f32[40,128]{1,0:T(8,128)S(1)} %get-tuple-element.33), channel_id=1, source_target_pairs={{0,112},{16,0},{32,16},{48,32},{64,48},{80,64},{96,80},{112,96},{1... | collective-permute-start | bytes 61448 | tf_op jit(solution)/shard_map/ppermute | solution.py:633
  23.4 0.0 collective-permute-start.3
  23.4 0.0 copy-done
  23.4 0.0 copy-start.1
  23.4 0.0 copy-start.2
  23.4 3.8 %first_step_inside.1 = (f32[4320,128]{1,0:T(8,128)}, f32[8,128]{1,0:T(8,128)S(1)}, f32[8,128]{1,0:T(8,128)S(1)}) custom-call(s32[1]{0:T(128)} %bitcast.where_ref, f32[4320,128]{1,0:T(8,128)} %bitcast.13, bf16[8640,128]{1,0:T(8,128)(2,1)S(1)} %get-tuple-element.24.spectrum_ref, f32[512,128]{1,0:T(8,128)S(1)} %copy-done, f32[8,128]{1,0:T(8,128)S(1)} %get-tuple-element.25.sea8_ref), custom_call_target="tpu_custom_call" | custom-call | flops 20000000 | bytes 6000000 | tf_op jit(solution)/shard_map/first_step_inside/pallas_call | solution.py:672
  27.2 0.0 collective-permute-done.2.lon_east_ref
  27.2 1.3 %collective-permute-done.3.lon_west_ref = f32[40,128]{1,0:T(8,128)S(1)} collective-permute-done((f32[40,128]{1,0:T(8,128)S(1)}, f32[40,128]{1,0:T(8,128)S(1)}, u32[]{:S(2)}, u32[]{:S(2)}) %collective-permute-start.3) | collective-permute-done | bytes 20512 | tf_op jit(solution)/shard_map/ppermute | solution.py:634
  28.4 1.0 %all-to-all-done = f32[128,1,128]{2,1,0:T(1,128)S(1)} async-done(((f32[128,1,128]{2,1,0:T(1,128)}), f32[128,1,128]{2,1,0:T(1,128)S(1)}, u32[]{:S(2)}, u32[]{:S(2)}) %all-to-all-start) | async-done | bytes 65568 | tf_op jit(solution)/shard_map/all_to_all | solution.py:666
  29.5 0.0 collective-permute-done.on_in
  29.5 0.0 collective-permute-done.1.off_in
  29.5 0.0 copy-done.1
  29.5 0.0 copy-done.2
  29.5 3.5 %first_step_edges.1 = (f32[4328,128]{1,0:T(8,128)S(1)}, f32[552,128]{1,0:T(8,128)S(1)}, f32[552,128]{1,0:T(8,128)S(1)}) custom-call(s32[1]{0:T(128)} %bitcast.where_ref, f32[30,36]{1,0:T(8,128)S(1)} %bitcast.10, f32[4320,128]{1,0:T(8,128)} %get-tuple-element.26.nu_hbm, bf16[8640,128]{1,0:T(8,128)(2,1)S(1)} %get-tuple-element.24.spectrum_ref, ...), custom_call_target="tpu_custom_call" | custom-call | tf_op jit(solution)/shard_map/first_step_edges/pallas_call | solution.py:682
  33.0 1.0 %collective-permute-start.4 = (f32[552,128]{1,0:T(8,128)S(1)}, f32[552,128]{1,0:T(8,128)S(1)}, u32[]{:S(2)}, u32[]{:S(2)}) collective-permute-start(f32[552,128]{1,0:T(8,128)S(1)} %get-tuple-element.39), channel_id=1, source_target_pairs={{0,1},{1,0},{2,3},{3,2},{4,5},{5,4},{6,7},{7,6},{8,9},{9,8},{10,11... | collective-permute-start | bytes 847880 | tf_op jit(solution)/shard_map/ppermute | solution.py:632
  34.0 3.9 %collective-permute-start.5 = (f32[552,128]{1,0:T(8,128)S(1)}, f32[552,128]{1,0:T(8,128)S(1)}, u32[]{:S(2)}, u32[]{:S(2)}) collective-permute-start(f32[552,128]{1,0:T(8,128)S(1)} %get-tuple-element.40), channel_id=1, source_target_pairs={{1,2},{2,1},{3,4},{4,3},{5,6},{6,5},{7,8},{8,7},{9,10},{10,9},{11,... | collective-permute-start | bytes 847880 | tf_op jit(solution)/shard_map/ppermute | solution.py:631
  37.9 1.5 %edges_of_first_step.1 = (f32[40,128]{1,0:T(8,128)S(1)}, f32[40,128]{1,0:T(8,128)S(1)}) custom-call(f32[4328,128]{1,0:T(8,128)S(1)} %get-tuple-element.35.mu_ref), custom_call_target="tpu_custom_call" | custom-call | flops 3000000 | bytes 2200000 | tf_op jit(solution)/shard_map/edges_of_first_step/pallas_call | solution.py:695
  39.4 1.2 %collective-permute-start.6 = (f32[40,128]{1,0:T(8,128)S(1)}, f32[40,128]{1,0:T(8,128)S(1)}, u32[]{:S(2)}, u32[]{:S(2)}) collective-permute-start(f32[40,128]{1,0:T(8,128)S(1)} %get-tuple-element.41), channel_id=1, source_target_pairs={{0,112},{16,0},{32,16},{48,32},{64,48},{80,64},{96,80},{112,96},{1... | collective-permute-start | bytes 61448 | tf_op jit(solution)/shard_map/ppermute | solution.py:633
  40.6 0.3 collective-permute-start.7
  40.9 1.3 %last_step_inside.1 = (f32[4320,128]{1,0:T(8,128)S(1)}, f32[8,128]{1,0:T(8,128)S(1)}, f32[8,128]{1,0:T(8,128)S(1)}) custom-call(s32[1]{0:T(128)} %bitcast.where_ref, f32[4328,128]{1,0:T(8,128)S(1)} %get-tuple-element.35.mu_ref, bf16[8640,128]{1,0:T(8,128)(2,1)S(1)} %get-tuple-element.24.spectrum_ref, f32[512,128]{1,0:T(8,128)S(1)} %copy-done), custom_call_target="tpu_custom_call" | custom-call | flops 20000000 | bytes 6000000 | tf_op jit(solution)/shard_map/last_step_inside/pallas_call | solution.py:706
  42.2 0.2 collective-permute-done.6.lon_east_ref
  42.4 3.0 %collective-permute-done.7.lon_west_ref = f32[40,128]{1,0:T(8,128)S(1)} collective-permute-done((f32[40,128]{1,0:T(8,128)S(1)}, f32[40,128]{1,0:T(8,128)S(1)}, u32[]{:S(2)}, u32[]{:S(2)}) %collective-permute-start.7) | collective-permute-done | bytes 20512 | tf_op jit(solution)/shard_map/ppermute | solution.py:634
  45.3 0.0 collective-permute-done.4.on_in
  45.3 1.5 %collective-permute-done.5.off_in = f32[552,128]{1,0:T(8,128)S(1)} collective-permute-done((f32[552,128]{1,0:T(8,128)S(1)}, f32[552,128]{1,0:T(8,128)S(1)}, u32[]{:S(2)}, u32[]{:S(2)}) %collective-permute-start.5) | collective-permute-done | bytes 282656 | tf_op jit(solution)/shard_map/ppermute | solution.py:631
  46.8 3.6 %last_step_edges.1 = f32[4320,128]{1,0:T(8,128)} custom-call(s32[1]{0:T(128)} %bitcast.where_ref, f32[30,36]{1,0:T(8,128)S(1)} %bitcast.11, f32[4320,128]{1,0:T(8,128)S(1)} %get-tuple-element.36.nu_ref, bf16[8640,128]{1,0:T(8,128)(2,1)S(1)} %get-tuple-element.24.spectrum_ref, f32[512,128]{1,0:T(8,128)S(1)} %copy-done, s32[4,128]{1,0:T(4,128)S(1)} %copy-done.2, ...), custom_call_target="tpu_custom_call" | custom-call | tf_op jit(solution)/shard_map/last_step_edges/pallas_call | solution.py:715
Async XLA Ops:
  0.0 23.4 %copy-start = (f32[512,128]{1,0:T(8,128)S(1)}, f32[512,128]{1,0:T(8,128)}, u32[]{:S(2)}) copy-start(f32[512,128]{1,0:T(8,128)} %constant.6.clone.table_hbm.table_ref) | copy-start | bytes 786436
  4.6 24.8 %collective-permute-start = (f32[552,128]{1,0:T(8,128)}, f32[552,128]{1,0:T(8,128)S(1)}, u32[]{:S(2)}, u32[]{:S(2)}) collective-permute-start(f32[552,128]{1,0:T(8,128)} %get-tuple-element.31), channel_id=1, source_target_pairs={{0,1},{1,0},{2,3},{3,2},{4,5},{5,4},{6,7},{7,6},{8,9},{9,8},{10,11... | collective-permute-start | bytes 847880 | tf_op jit(solution)/shard_map/ppermute | solution.py:632
  6.1 23.3 %collective-permute-start.1 = (f32[552,128]{1,0:T(8,128)S(1)}, f32[552,128]{1,0:T(8,128)S(1)}, u32[]{:S(2)}, u32[]{:S(2)}) collective-permute-start(f32[552,128]{1,0:T(8,128)S(1)} %get-tuple-element.32), channel_id=1, source_target_pairs={{1,2},{2,1},{3,4},{4,3},{5,6},{6,5},{7,8},{8,7},{9,10},{10,9},{11,... | collective-permute-start | bytes 847880 | tf_op jit(solution)/shard_map/ppermute | solution.py:631
  11.0 18.5 %all-to-all-start = ((f32[128,1,128]{2,1,0:T(1,128)}), f32[128,1,128]{2,1,0:T(1,128)S(1)}, u32[]{:S(2)}, u32[]{:S(2)}) async-start(f32[128,1,128]{2,1,0:T(1,128)} %bitcast.5), calls=%async_computation | async-start | bytes 131072 | tf_op jit(solution)/shard_map/all_to_all | solution.py:666
  19.8 7.3 %collective-permute-start.2 = (f32[40,128]{1,0:T(8,128)S(1)}, f32[40,128]{1,0:T(8,128)S(1)}, u32[]{:S(2)}, u32[]{:S(2)}) collective-permute-start(f32[40,128]{1,0:T(8,128)S(1)} %get-tuple-element.33), channel_id=1, source_target_pairs={{0,112},{16,0},{32,16},{48,32},{64,48},{80,64},{96,80},{112,96},{1... | collective-permute-start | bytes 61448 | tf_op jit(solution)/shard_map/ppermute | solution.py:633
  23.4 5.0 %collective-permute-start.3 = (f32[40,128]{1,0:T(8,128)S(1)}, f32[40,128]{1,0:T(8,128)S(1)}, u32[]{:S(2)}, u32[]{:S(2)}) collective-permute-start(f32[40,128]{1,0:T(8,128)S(1)} %get-tuple-element.34), channel_id=1, source_target_pairs={{0,16},{16,32},{32,48},{48,64},{64,80},{80,96},{96,112},{112,0},{1... | collective-permute-start | bytes 61448 | tf_op jit(solution)/shard_map/ppermute | solution.py:634
  23.4 6.0 %copy-start.1 = (f32[36,30]{0,1:T(8,128)S(1)}, f32[36,30]{0,1:T(8,128)}, u32[]{:S(2)}) copy-start(f32[36,30]{0,1:T(8,128)} %param.11) | copy-start | bytes 12964
  23.4 6.0 %copy-start.2 = (s32[4,128]{1,0:T(4,128)S(1)}, s32[4,128]{1,0:T(4,128)}, u32[]{:S(2)}) copy-start(s32[4,128]{1,0:T(4,128)} %ice_ref.3) | copy-start | bytes 6148
  33.0 12.4 %collective-permute-start.4 = (f32[552,128]{1,0:T(8,128)S(1)}, f32[552,128]{1,0:T(8,128)S(1)}, u32[]{:S(2)}, u32[]{:S(2)}) collective-permute-start(f32[552,128]{1,0:T(8,128)S(1)} %get-tuple-element.39), channel_id=1, source_target_pairs={{0,1},{1,0},{2,3},{3,2},{4,5},{5,4},{6,7},{7,6},{8,9},{9,8},{10,11... | collective-permute-start | bytes 847880 | tf_op jit(solution)/shard_map/ppermute | solution.py:632
  34.0 12.8 %collective-permute-start.5 = (f32[552,128]{1,0:T(8,128)S(1)}, f32[552,128]{1,0:T(8,128)S(1)}, u32[]{:S(2)}, u32[]{:S(2)}) collective-permute-start(f32[552,128]{1,0:T(8,128)S(1)} %get-tuple-element.40), channel_id=1, source_target_pairs={{1,2},{2,1},{3,4},{4,3},{5,6},{6,5},{7,8},{8,7},{9,10},{10,9},{11,... | collective-permute-start | bytes 847880 | tf_op jit(solution)/shard_map/ppermute | solution.py:631
  39.4 2.9 %collective-permute-start.6 = (f32[40,128]{1,0:T(8,128)S(1)}, f32[40,128]{1,0:T(8,128)S(1)}, u32[]{:S(2)}, u32[]{:S(2)}) collective-permute-start(f32[40,128]{1,0:T(8,128)S(1)} %get-tuple-element.41), channel_id=1, source_target_pairs={{0,112},{16,0},{32,16},{48,32},{64,48},{80,64},{96,80},{112,96},{1... | collective-permute-start | bytes 61448 | tf_op jit(solution)/shard_map/ppermute | solution.py:633
  40.6 4.7 %collective-permute-start.7 = (f32[40,128]{1,0:T(8,128)S(1)}, f32[40,128]{1,0:T(8,128)S(1)}, u32[]{:S(2)}, u32[]{:S(2)}) collective-permute-start(f32[40,128]{1,0:T(8,128)S(1)} %get-tuple-element.42), channel_id=1, source_target_pairs={{0,16},{16,32},{32,48},{48,64},{64,80},{80,96},{96,112},{112,0},{1... | collective-permute-start | bytes 61448 | tf_op jit(solution)/shard_map/ppermute | solution.py:634
